TPU v7x, 512 devices: a whole 4x4x16 slice. The times are simulated.
512 devices in a mesh: seq: 64 (over x, z), head: 8 (over y, core).
Axes of the slice: x: 4, y: 4, z: 16, core: 2. Of those that a mesh axis runs over, the one named last changes fastest.
Arguments:
- query_rows: bfloat16 [32768, 2048], P('seq', 'head'), may hold values from -10 to 10
- key_rows: bfloat16 [32768, 2048], P('seq', 'head'), may hold values from -10 to 10
- value_rows: bfloat16 [32768, 2048], P('seq', 'head'), may hold values from -6 to 6
- saved_output: bfloat16 [32768, 2048], P('seq', 'head'), may hold values from -6 to 6
- output_grad: bfloat16 [32768, 2048], P('seq', 'head'), may hold values from -16 to 16
- out_weight: bfloat16 [2048, 2048], P('seq', 'head'), may hold values from -0.125 to 0.125
- cluster_id: int32 [16, 32768], P('head', 'seq'), may hold values from 0 to 63, as said below
- cluster_slot: int32 [16, 32768], P('head', 'seq'), may hold values from 0 to 511, as said below
Outputs:
- query_grad: bfloat16 [32768, 2048], P('seq', 'head')
- key_grad: bfloat16 [32768, 2048], P('seq', 'head')
- value_grad: bfloat16 [32768, 2048], P('seq', 'head')
- weight_grad: float32 [2048, 2048], P('seq', 'head')
Inputs may be any that keep to these rules, and one draw needn't show every extreme that they name: `cluster_id`: for every head each of the 64 clusters holds exactly 512 tokens. Index o of seq owns cluster o of every head. In one head, at most 16 of the 512 tokens of one index of seq fall into the clusters owned by one index of seq, and in every head some pairs reach 16. `cluster_slot`: within a head no two tokens share both cluster and slot.
All inputs are finite; a program needn't handle non-finite values.
Results may differ from a plain program's by a relative error of at most 0.008.
Values may be sent and summed in bfloat16 or wider, within the bound.
No kernel may reach another device: no remote copies, remote signals or barrier semaphores. Data moves between devices by JAX's collectives and lax.ppermute only.
A program may use at most 64 MiB of HBM per device.

v0:
```python
import math

import jax
import jax.numpy as jnp
from jax import lax
from jax.sharding import PartitionSpec as P

DH = 128
CLUSTER = 512
CPD = 1


def attend_cluster(queries, key_block, value_block, cotangent, row_term, positions):
    score_scale = 1.0 / math.sqrt(DH)
    scores = (
        jnp.einsum("id,jd->ij", queries, key_block, preferred_element_type=jnp.float32)
        * score_scale
    )
    allowed = positions[None, :] <= positions[:, None]
    scores = jnp.where(allowed, scores, -jnp.inf)
    row_max = jnp.max(scores, axis=1, keepdims=True)
    exponent = jnp.exp(scores - row_max)
    softmax_p = exponent / jnp.sum(exponent, axis=1, keepdims=True)
    rounded_p = softmax_p.astype(jnp.bfloat16)
    grad_prob = jnp.einsum("id,jd->ij", cotangent, value_block, preferred_element_type=jnp.float32)
    grad_score = (softmax_p * (grad_prob - row_term[:, None]) * score_scale).astype(jnp.bfloat16)
    grad_query = jnp.einsum("ij,jd->id", grad_score, key_block, preferred_element_type=jnp.float32)
    grad_key = jnp.einsum("ij,id->jd", grad_score, queries, preferred_element_type=jnp.float32)
    grad_value = jnp.einsum("ij,id->jd", rounded_p, cotangent, preferred_element_type=jnp.float32)
    return jnp.concatenate([grad_query, grad_key, grad_value], axis=1).astype(jnp.bfloat16)


def owner_work(received):

    def one_head(members):
        payload = members[0]
        labels = members[1]
        senders = payload.shape[0]
        capacity = payload.shape[1]
        slots = senders * capacity
        payload = payload.reshape(slots, payload.shape[2])
        labels = labels.reshape(slots, 3)
        occupied = labels[:, 1] >= 0
        held = CPD * CLUSTER
        target = jnp.where(occupied, labels[:, 1] * CLUSTER + labels[:, 2], held)
        arrange_index = (
            jnp.zeros((held + 1,), jnp.int32)
            .at[target]
            .set(jnp.arange(slots, dtype=jnp.int32))[:held]
        )
        arranged = payload[arrange_index].reshape(CPD, CLUSTER, payload.shape[1])
        positions = labels[arrange_index, 0].reshape(CPD, CLUSTER)
        queries = arranged[:, :, 0:DH]
        key_block = arranged[:, :, DH : 2 * DH]
        value_block = arranged[:, :, 2 * DH : 3 * DH]
        cotangent = arranged[:, :, 3 * DH : 4 * DH]
        saved = arranged[:, :, 4 * DH : 5 * DH]
        summed = jnp.sum(cotangent.astype(jnp.float32) * saved.astype(jnp.float32), axis=2)
        row_term = lax.optimization_barrier(summed.astype(jnp.bfloat16)).astype(jnp.float32)
        gradients = jax.vmap(attend_cluster)(
            queries, key_block, value_block, cotangent, row_term, positions
        )
        gradients = gradients.reshape(held, 3 * DH)
        returned = jnp.where(
            occupied[:, None], gradients[jnp.minimum(target, held - 1)], jnp.zeros((), jnp.bfloat16)
        )
        return returned.reshape(senders, capacity, 3 * DH)

    homeward = lax.map(one_head, received)
    return lax.all_to_all(homeward, "seq", split_axis=1, concat_axis=1, tiled=True)


def local(
    query_rows,
    key_rows,
    value_rows,
    saved_output,
    output_grad,
    out_weight,
    cluster_id,
    cluster_slot,
):
    local_tokens = query_rows.shape[0]
    width_heads = query_rows.shape[1]
    local_heads = cluster_id.shape[0]
    senders = lax.axis_size("seq")
    capacity = 2 * local_tokens // senders
    slots = senders * capacity
    full_grad = lax.all_gather(output_grad, "head", axis=1, tiled=True)
    columns = full_grad
    projected = jnp.dot(
        columns,
        lax.all_gather(out_weight, "seq", axis=0, tiled=True),
        preferred_element_type=jnp.float32,
    )
    cotangent = projected.astype(jnp.bfloat16)
    columns = full_grad
    weight_grad = lax.psum_scatter(
        jnp.einsum("tc,td->cd", columns, saved_output, preferred_element_type=jnp.float32),
        "seq",
        scatter_dimension=0,
        tiled=True,
    )
    owner_dev = cluster_id // CPD
    local_cluster = cluster_id % CPD
    onehot = (owner_dev[:, :, None] == jnp.arange(senders, dtype=jnp.int32)[None, None, :]).astype(
        jnp.int32
    )
    pair_rank = jnp.sum((jnp.cumsum(onehot, axis=1) - 1) * onehot, axis=2)
    send_index = owner_dev * capacity + pair_rank
    token_ids = jnp.arange(local_tokens, dtype=jnp.int32)
    source_of = jax.vmap(
        lambda where_to: jnp.full((slots,), local_tokens, jnp.int32).at[where_to].set(token_ids)
    )(send_index)
    start_token = lax.axis_index("seq") * local_tokens
    position_ids = jnp.broadcast_to(start_token + token_ids, (local_heads, local_tokens))
    labels_tok = jnp.stack([position_ids, local_cluster, cluster_slot], axis=2)
    labels_pad = jnp.concatenate([labels_tok, jnp.full((local_heads, 1, 3), -1, jnp.int32)], axis=1)
    label_send = jnp.take_along_axis(labels_pad, source_of[:, :, None], axis=1).reshape(
        local_heads, senders, capacity, 3
    )

    def by_head(matrix):
        return matrix.reshape(local_tokens, local_heads, DH).transpose(1, 0, 2)

    query_h = by_head(query_rows)
    key_h = by_head(key_rows)
    value_h = by_head(value_rows)
    cot_h = by_head(cotangent)
    saved_h = by_head(saved_output)
    pieces = [query_h, key_h, value_h, cot_h, saved_h]
    stacked = jnp.stack(pieces, axis=2).reshape(local_heads, local_tokens, len(pieces) * DH)
    padded = jnp.concatenate(
        [stacked, jnp.zeros((local_heads, 1, stacked.shape[2]), jnp.bfloat16)], axis=1
    )
    gathered = jnp.take_along_axis(padded, source_of[:, :, None], axis=1)
    packed = gathered.reshape(local_heads, senders, capacity, stacked.shape[2])
    homeward = owner_work(
        (
            lax.all_to_all(packed, "seq", split_axis=1, concat_axis=1, tiled=True),
            lax.all_to_all(label_send, "seq", split_axis=1, concat_axis=1, tiled=True),
        )
    )
    flat_home = homeward.reshape(local_heads, slots, 3 * DH)
    per_token = jnp.take_along_axis(flat_home, send_index[:, :, None], axis=1)
    per_token = per_token.reshape(local_heads, local_tokens, 3, DH).transpose(2, 1, 0, 3)
    per_token = per_token.reshape(3, local_tokens, width_heads)
    return (per_token[0], per_token[1], per_token[2], weight_grad)


def solution(mesh):
    in_specs = (
        P("seq", "head"),
        P("seq", "head"),
        P("seq", "head"),
        P("seq", "head"),
        P("seq", "head"),
        P("seq", "head"),
        P("head", "seq"),
        P("head", "seq"),
    )
    out_specs = (P("seq", "head"), P("seq", "head"), P("seq", "head"), P("seq", "head"))
    return jax.shard_map(local, mesh=mesh, in_specs=in_specs, out_specs=out_specs, check_vma=False)
```

profile of v0, /device:TPU:6, one launch (start us, length us, event | category | flops | bytes accessed | tf_op | source)
XLA Modules:
  0.0 1122.6 jit_solution(541727252146302675)
XLA Ops:
  9.5 2.4 reduce-window.6
  13.8 4.3 scatter_custom_fusion.1
  18.9 8.7 gather_fusion.3
  29.3 18.8 %all-to-all-start = ((s32[2,64,16,3]{2,0,3,1:T(2,128)}), s32[2,64,16,3]{2,0,3,1:T(2,128)S(1)}, u32[]{:S(2)}, u32[]{:S(2)}) async-start(s32[2,64,16,3]{2,0,3,1:T(2,128)} %broadcast_select_fusion.1), calls=%async_computation | async-start | bytes 393216 | tf_op jit(solution)/shard_map/all_to_all | solution.py:141
  48.8 104.9 %all-gather.5.cloned.1.call-done = bf16[2048,256]{1,0:T(8,128)(2,1)} async-done(((bf16[32,256]{1,0:T(8,128)(2,1)}), bf16[2048,256]{1,0:T(8,128)(2,1)}) %all-gather.5.cloned.1.call-update) | async-done | bytes 1048592 | tf_op jit(solution)/shard_map/all_gather | solution.py:93
  153.8 34.2 %all-gather.3.cloned.1.call-done = bf16[512,2048]{1,0:T(8,128)(2,1)} async-done(((bf16[512,256]{1,0:T(8,128)(2,1)}), bf16[512,2048]{1,0:T(8,128)(2,1)}) %all-gather.3.cloned.1.call-update) | async-done | bytes 2097168 | tf_op jit(solution)/shard_map/all_gather | solution.py:89
  188.0 2.6 convolution_convert_fusion.3
  193.5 22.7 %gather_fusion.4 = bf16[2048,640]{1,0:T(8,128)(2,1)} fusion(bf16[2,513,640]{2,0,1:T(2,128)(2,1)S(1)} %concatenate.17, s32[2048]{0:T(1024)S(1)} %bitcast.149), kind=kCustom, calls=%fused_computation.4 | custom fusion | bytes 5259264 | tf_op jit(solution)/shard_map/jit(take_along_axis)/gather | solution.py:136
  216.2 3.1 copy_select_fusion
  219.3 16.1 %all-to-all-start.1 = ((bf16[2,64,16,640]{3,2,0,1:T(8,128)(2,1)}), bf16[2,64,16,640]{3,2,0,1:T(8,128)(2,1)}, u32[]{:S(2)}, u32[]{:S(2)}) async-start(bf16[2,64,16,640]{3,2,0,1:T(8,128)(2,1)} %copy_select_fusion), calls=%async_computation.1 | async-start | bytes 5242880 | tf_op jit(solution)/shard_map/all_to_all | solution.py:140
  235.4 119.3 %all-to-all-done.1 = bf16[2,64,16,640]{3,2,0,1:T(8,128)(2,1)} async-done(((bf16[2,64,16,640]{3,2,0,1:T(8,128)(2,1)}), bf16[2,64,16,640]{3,2,0,1:T(8,128)(2,1)}, u32[]{:S(2)}, u32[]{:S(2)}) %all-to-all-start.1) | async-done | bytes 2621472 | tf_op jit(solution)/shard_map/all_to_all | solution.py:140
  354.7 41.7 %while.10 = (s32[]{:T(128)}, bf16[2,64,16,384]{3,2,0,1:T(8,128)(2,1)}, s32[2,64,16,3]{2,0,3,1:T(2,128)S(1)}, bf16[2,64,16,640]{3,2,0,1:T(8,128)(2,1)}, s32[]{:T(128)}, /*index=5*/s32[]{:T(128)}) while((s32[]{:T(128)}, bf16[2,64,16,384]{3,2,0,1:T(8,128)(2,1)}, s32[2,64,16,3]{2,0,3,1:T(2,128)S(1)}, bf16[2,64,16,640]{3,2,0,1:T(8,128)(2,1)}, ...), condition=%wide.region_9.10_spmd, body=%wide.region_4.9_spmd.sunk | while | flops 341523968 | bytes 28755096 | solution.py:69
  355.1 4.3 scatter_custom_fusion.7
  359.5 4.8 gather_fusion.1
  365.8 2.0 gather_fusion
  370.1 3.9 gather_fusion.2
  375.9 4.3 scatter_custom_fusion.7
  380.3 4.8 gather_fusion.1
  390.9 3.9 gather_fusion.2
  396.4 9.1 all-to-all-start.2
  405.5 3.7 fusion.23
  409.3 74.2 %all-to-all-done.2 = bf16[2,64,16,384]{3,2,0,1:T(8,128)(2,1)S(1)} async-done(((bf16[2,64,16,384]{3,2,0,1:T(8,128)(2,1)}), bf16[2,64,16,384]{3,2,0,1:T(8,128)(2,1)S(1)}, u32[]{:S(2)}, u32[]{:S(2)}) %all-to-all-start.2) | async-done | bytes 1572896 | tf_op jit(solution)/shard_map/all_to_all | solution.py:70
  483.7 6.8 gather_fusion.5
  495.2 620.9 %reduce-scatter.2.cloned.1.call-done = f32[32,256]{1,0:T(8,128)} async-done(((f32[2048,256]{1,0:T(8,128)}), f32[32,256]{1,0:T(8,128)}) %reduce-scatter.2.cloned.1.call-update) | async-done | bytes 32784 | tf_op jit(solution)/shard_map/reduce_scatter | solution.py:98
  (138 shorter events, 28.0 us)
Async XLA Ops:
  7.2 6.0 copy-start.9
  7.2 6.3 copy-start.8
  7.2 5.9 copy-start.6
  7.2 11.2 copy-start.7
  7.2 146.6 %all-gather.5.cloned.1.call-start = ((), (), s32[]{:S(2)}) async-start(), calls=%async_computation.5 | async-start | bytes 1064960 | tf_op jit(solution)/shard_map/all_gather | solution.py:93
  7.9 180.0 %all-gather.3.cloned.1.call-start = ((), (), s32[]{:S(2)}) async-start(), calls=%async_computation.4 | async-start | bytes 2359296 | tf_op jit(solution)/shard_map/all_gather | solution.py:89
  27.6 20.5 %copy-start.3 = (bf16[512,256]{1,0:T(8,128)(2,1)S(1)}, bf16[512,256]{1,0:T(8,128)(2,1)}, u32[]{:S(2)}) copy-start(bf16[512,256]{1,0:T(8,128)(2,1)} %param.10) | copy-start | bytes 786436
  27.6 20.7 %copy-start.4 = (bf16[512,256]{1,0:T(8,128)(2,1)S(1)}, bf16[512,256]{1,0:T(8,128)(2,1)}, u32[]{:S(2)}) copy-start(bf16[512,256]{1,0:T(8,128)(2,1)} %param.11) | copy-start | bytes 786436
  27.6 20.8 %copy-start.5 = (bf16[512,256]{1,0:T(8,128)(2,1)S(1)}, bf16[512,256]{1,0:T(8,128)(2,1)}, u32[]{:S(2)}) copy-start(bf16[512,256]{1,0:T(8,128)(2,1)} %param.12) | copy-start | bytes 786436
  27.6 20.9 %copy-start.2 = (bf16[512,256]{1,0:T(8,128)(2,1)S(1)}, bf16[512,256]{1,0:T(8,128)(2,1)}, u32[]{:S(2)}) copy-start(bf16[512,256]{1,0:T(8,128)(2,1)} %param.13) | copy-start | bytes 786436
  29.3 190.0 %all-to-all-start = ((s32[2,64,16,3]{2,0,3,1:T(2,128)}), s32[2,64,16,3]{2,0,3,1:T(2,128)S(1)}, u32[]{:S(2)}, u32[]{:S(2)}) async-start(s32[2,64,16,3]{2,0,3,1:T(2,128)} %broadcast_select_fusion.1), calls=%async_computation | async-start | bytes 393216 | tf_op jit(solution)/shard_map/all_to_all | solution.py:141
  219.3 135.4 %all-to-all-start.1 = ((bf16[2,64,16,640]{3,2,0,1:T(8,128)(2,1)}), bf16[2,64,16,640]{3,2,0,1:T(8,128)(2,1)}, u32[]{:S(2)}, u32[]{:S(2)}) async-start(bf16[2,64,16,640]{3,2,0,1:T(8,128)(2,1)} %copy_select_fusion), calls=%async_computation.1 | async-start | bytes 5242880 | tf_op jit(solution)/shard_map/all_to_all | solution.py:140
  370.1 3.9 copy-start
  374.3 1.2 copy-start.1
  390.9 3.9 copy-start
  395.2 1.2 copy-start.1
  396.4 87.1 %all-to-all-start.2 = ((bf16[2,64,16,384]{3,2,0,1:T(8,128)(2,1)}), bf16[2,64,16,384]{3,2,0,1:T(8,128)(2,1)S(1)}, u32[]{:S(2)}, u32[]{:S(2)}) async-start(bf16[2,64,16,384]{3,2,0,1:T(8,128)(2,1)} %get-tuple-element.26), calls=%async_computation.2 | async-start | bytes 3145728 | tf_op jit(solution)/shard_map/all_to_all | solution.py:70
  405.5 710.6 %reduce-scatter.2.cloned.1.call-start = ((), (), s32[]{:S(2)}) async-start(), calls=%async_computation.6 | async-start | bytes 2129920 | tf_op jit(solution)/shard_map/reduce_scatter | solution.py:98
Sparse Core Ops, SparseCore 0:
  11.0 142.7 all-gather.4
  155.9 32.0 all-gather.2
  411.3 704.7 reduce-scatter.1
where the time goes:
time: 1120 us
  waiting for transfers between devices  955 us (85%)
  local copies, waits for them, and re-layouts  89.8 us (8%)
  starting transfers between devices  44.1 us (4%)
  between operations  14.2 us (1%)
    reduce_scatter x1, waiting for transfers between devices, local(): lax.psum_scatter(jnp.einsum('tc,td->cd', columns, saved_output, preferred...  621 us
    all_to_all x1, waiting for transfers between devices, local(): lax.all_to_all(packed, 'seq', split_axis=1, concat_axis=1, tiled=True)  119 us
    all_gather x1, waiting for transfers between devices, local(): lax.all_gather(out_weight, 'seq', axis=0, tiled=True)  105 us
    all_to_all x1, waiting for transfers between devices, owner_work(): lax.all_to_all(homeward, 'seq', split_axis=1, concat_axis=1, tiled=True)  74.2 us
    all_gather x1, waiting for transfers between devices, local(): full_grad = lax.all_gather(output_grad, 'head', axis=1, tiled=True)  34.2 us
    gather x1, local copies, waits for them, and re-layouts, local(): gathered = jnp.take_along_axis(padded, source_of[:, :, None], axis=1)  22.7 us
  transfers between devices with their start and end apart: 6, of which 5 were waited for; matrix products, arithmetic and copies ran while one was open for 6% of the time, Pallas kernels for 0%

commit v1 on v0

v1 whole, which is shorter than its diff:
```python
import math

import jax
import jax.numpy as jnp
from jax import lax
from jax.experimental import pallas as pl
from jax.experimental.pallas import tpu as pltpu
from jax.sharding import Mesh
from jax.sharding import PartitionSpec as P

DH = 128
CAP = 16
BLOCK = 256
MASKED = -1e30
SCALE = 1.0 / math.sqrt(DH)
SEQ = ("x", "z")
HEAD = ("y", "core")
PARAMS = pltpu.CompilerParams(vmem_limit_bytes=48 * 1024 * 1024)


def pair_places(ids, owners):
    heads, tokens = ids.shape
    earlier = (
        lax.broadcasted_iota(jnp.int32, (tokens, tokens), 0)
        < lax.broadcasted_iota(jnp.int32, (tokens, tokens), 1)
    ).astype(jnp.float32).astype(jnp.bfloat16)
    owner_iota = lax.broadcasted_iota(jnp.int32, (owners, tokens), 0)
    places = []
    for h in range(heads):
        onehot = jnp.where(owner_iota == ids[h : h + 1, :], 1.0, 0.0)
        before = jnp.dot(onehot.astype(jnp.bfloat16), earlier, preferred_element_type=jnp.float32)
        rank = jnp.sum(onehot * before, axis=0, keepdims=True)
        places.append((onehot, rank))
    return places


def pack_kernel(ids_ref, q_ref, k_ref, v_ref, out_ref):
    owners = out_ref.shape[0]
    ids = ids_ref[...]
    heads, tokens = ids.shape
    slots = owners * CAP
    slot_iota = lax.broadcasted_iota(jnp.int32, (slots, tokens), 0)
    for h, (_, rank) in enumerate(pair_places(ids, owners)):
        place = ids[h : h + 1, :] * CAP + rank.astype(jnp.int32)
        select = jnp.where(slot_iota == place, 1.0, 0.0).astype(jnp.bfloat16)
        for n, ref in enumerate((q_ref, k_ref, v_ref)):
            rows = jnp.dot(
                select, ref[:, h * DH : (h + 1) * DH], preferred_element_type=jnp.float32
            ).astype(jnp.bfloat16)
            out_ref[:, h * CAP : (h + 1) * CAP, n * DH : (n + 1) * DH] = rows.reshape(
                owners, CAP, DH
            )


def cotangent_kernel(ids_ref, grad_ref, weight_ref, saved_ref, out_ref, place_ref):
    owners = out_ref.shape[0]
    ids = ids_ref[...]
    heads, tokens = ids.shape
    slots = owners * CAP
    cot = jnp.dot(grad_ref[...], weight_ref[...], preferred_element_type=jnp.float32).astype(
        jnp.bfloat16
    )
    slot_iota = lax.broadcasted_iota(jnp.int32, (slots, tokens), 0)
    lane = lax.broadcasted_iota(jnp.int32, (tokens, DH), 1)
    row8 = lax.broadcasted_iota(jnp.int32, (8, tokens), 0)
    meta = jnp.zeros((owners, DH), jnp.float32)
    places = pair_places(ids, owners)
    rank_rows = jnp.zeros((8, tokens), jnp.float32)
    place_rows = jnp.zeros((8, tokens), jnp.float32)
    for h, (_, rank) in enumerate(places):
        place = ids[h : h + 1, :].astype(jnp.float32) * CAP + rank
        rank_rows = jnp.where(row8 == h, rank, rank_rows)
        place_rows = jnp.where(row8 == h, place, place_rows)
    rank_columns = rank_rows.T
    place_ref[...] = place_rows.T.astype(jnp.int32)
    for h, (onehot, rank) in enumerate(places):
        g = cot[:, h * DH : (h + 1) * DH]
        o = saved_ref[:, h * DH : (h + 1) * DH]
        row_term = jnp.sum(g.astype(jnp.float32) * o.astype(jnp.float32), axis=1, keepdims=True)
        row_term = row_term.astype(jnp.bfloat16).astype(jnp.float32)
        where_to = rank_columns[:, h : h + 1].astype(jnp.int32) + 2 * CAP * h
        spread = jnp.where(lane == where_to, row_term, 0.0) + jnp.where(
            lane == where_to + CAP, 1.0, 0.0
        )
        meta = meta + jnp.dot(
            onehot.astype(jnp.bfloat16),
            spread.astype(jnp.bfloat16),
            preferred_element_type=jnp.float32,
        )
        place = ids[h : h + 1, :] * CAP + rank.astype(jnp.int32)
        select = jnp.where(slot_iota == place, 1.0, 0.0).astype(jnp.bfloat16)
        rows = jnp.dot(select, g, preferred_element_type=jnp.float32).astype(jnp.bfloat16)
        out_ref[:, h * CAP : (h + 1) * CAP, :] = rows.reshape(owners, CAP, DH)
    meta_lane = lax.broadcasted_iota(jnp.int32, (owners, DH), 1)
    meta = jnp.where((meta_lane & CAP) != 0, (1.0 - meta) * MASKED, meta)
    first = lax.broadcasted_iota(jnp.int32, (owners, 8, DH), 1) == 0
    out_ref[:, heads * CAP :, :] = jnp.where(first, meta[:, None, :], 0.0).astype(jnp.bfloat16)


def attend_kernel(qkv_ref, g_ref, out_ref, prob_ref, score_ref):
    owners = qkv_ref.shape[0]
    heads = qkv_ref.shape[1] // CAP
    slots = owners * CAP
    meta = jnp.sum(g_ref[:, heads * CAP :, :].astype(jnp.float32), axis=1, keepdims=True)
    meta = jnp.broadcast_to(meta, (owners, CAP, DH)).reshape(slots, DH)
    lane = lax.broadcasted_iota(jnp.int32, (slots, DH), 1)
    rank = lax.broadcasted_iota(jnp.int32, (slots, DH), 0) & (CAP - 1)
    later = lax.broadcasted_iota(jnp.int32, (BLOCK, BLOCK), 0) > lax.broadcasted_iota(
        jnp.int32, (BLOCK, BLOCK), 1
    )
    contract_last = (((1,), (1,)), ((), ()))
    contract_first = (((0,), (0,)), ((), ()))

    def rows_of(ref, h, n):
        return ref[:, h * CAP : (h + 1) * CAP, n * DH : (n + 1) * DH].reshape(slots, DH)

    for h in range(heads):
        q, k, v = (rows_of(qkv_ref, h, n) for n in range(3))
        g = rows_of(g_ref, h, 0)
        term_lanes = (lane >= 2 * CAP * h) & (lane < 2 * CAP * h + CAP)
        bias_lanes = (lane >= 2 * CAP * h + CAP) & (lane < 2 * CAP * (h + 1))
        own = jnp.where((lane & (CAP - 1)) == rank, meta, 0.0)
        extra = jnp.where(term_lanes | bias_lanes, own, 0.0).astype(jnp.bfloat16)
        minus_one = jnp.where(term_lanes, -1.0, 0.0).astype(jnp.bfloat16)
        one = jnp.where(bias_lanes, 1.0, 0.0).astype(jnp.bfloat16)
        q_wide = jnp.concatenate([q, one], axis=1)
        k_wide = jnp.concatenate([k, extra], axis=1)
        g_wide = jnp.concatenate([g, extra], axis=1)
        v_wide = jnp.concatenate([v, minus_one], axis=1)
        for start in range(0, slots, BLOCK):
            stop = start + BLOCK
            scores = (
                lax.dot_general(
                    k_wide[:stop], q_wide[start:stop], contract_last,
                    preferred_element_type=jnp.float32,
                )
                * SCALE
            )
            last = jnp.where(later, MASKED, scores[start:stop])
            if start:
                scores = jnp.concatenate([scores[:start], last], axis=0)
            else:
                scores = last
            exponent = jnp.exp(scores - jnp.max(scores, axis=0, keepdims=True))
            prob = exponent * (1.0 / jnp.sum(exponent, axis=0, keepdims=True))
            grad_prob = lax.dot_general(
                v_wide[:stop], g_wide[start:stop], contract_last,
                preferred_element_type=jnp.float32,
            )
            grad_score = (prob * grad_prob * SCALE).astype(jnp.bfloat16)
            prob_ref[:stop, start:stop] = prob.astype(jnp.bfloat16)
            score_ref[:stop, start:stop] = grad_score
            grad_query = lax.dot_general(
                grad_score, k[:stop], contract_first, preferred_element_type=jnp.float32
            )
            out_ref[start // CAP : stop // CAP, h * CAP : (h + 1) * CAP, 0:DH] = (
                grad_query.astype(jnp.bfloat16).reshape(BLOCK // CAP, CAP, DH)
            )
        for start in range(0, slots, BLOCK):
            stop = start + BLOCK
            for n, ref, other in ((1, score_ref, q), (2, prob_ref, g)):
                grad = jnp.dot(
                    ref[start:stop, start:], other[start:], preferred_element_type=jnp.float32
                )
                out_ref[
                    start // CAP : stop // CAP, h * CAP : (h + 1) * CAP, n * DH : (n + 1) * DH
                ] = grad.astype(jnp.bfloat16).reshape(BLOCK // CAP, CAP, DH)


def unpack_kernel(home_ref, place_ref, dq_ref, dk_ref, dv_ref):
    owners = home_ref.shape[0]
    heads = home_ref.shape[1] // CAP
    slots = owners * CAP
    tokens = place_ref.shape[0]
    slot_iota = lax.broadcasted_iota(jnp.int32, (tokens, slots), 1)
    for h in range(heads):
        select = jnp.where(slot_iota == place_ref[:, h : h + 1], 1.0, 0.0).astype(jnp.bfloat16)
        for n, ref in enumerate((dq_ref, dk_ref, dv_ref)):
            rows = home_ref[:, h * CAP : (h + 1) * CAP, n * DH : (n + 1) * DH].reshape(slots, DH)
            ref[:, h * DH : (h + 1) * DH] = jnp.dot(
                select, rows, preferred_element_type=jnp.float32
            ).astype(jnp.bfloat16)


def copies_to_all(block, axis):
    size = lax.axis_size(axis)
    return lax.all_to_all(
        jnp.broadcast_to(block[None], (size, *block.shape)), axis, 0, 0, tiled=True
    )


def local(
    query_rows, key_rows, value_rows, saved_output, output_grad, out_weight, cluster_id, _slot
):
    tokens, width = query_rows.shape
    heads = cluster_id.shape[0]
    owners = lax.axis_size(SEQ)
    bf16 = jnp.bfloat16
    shape = jax.ShapeDtypeStruct

    full_grad = lax.all_gather(output_grad, HEAD, axis=1, tiled=True)
    weight_z = copies_to_all(out_weight, "z").reshape(-1, width)
    weight = copies_to_all(weight_z, "x").reshape(-1, width)

    qkv = pl.pallas_call(
        pack_kernel,
        out_shape=shape((owners, heads * CAP, 3 * DH), bf16),
        compiler_params=PARAMS,
        name="pack_rows",
    )(cluster_id, query_rows, key_rows, value_rows)
    qkv = lax.all_to_all(qkv, SEQ, 0, 0, tiled=True)

    cot, places = pl.pallas_call(
        cotangent_kernel,
        out_shape=(
            shape((owners, heads * CAP + 8, DH), bf16),
            shape((tokens, 8), jnp.int32),
        ),
        compiler_params=PARAMS,
        name="cotangent_rows",
    )(cluster_id, full_grad, weight, saved_output)
    cot = lax.all_to_all(cot, SEQ, 0, 0, tiled=True)

    share = jnp.einsum("tc,td->cd", full_grad, saved_output, preferred_element_type=jnp.float32)
    model = share.shape[0]
    n_x, n_z = lax.axis_size("x"), lax.axis_size("z")
    share = share.astype(bf16).reshape(n_x, model // n_x, width)
    share = lax.all_to_all(share, "x", 0, 0, tiled=True)
    share = jnp.sum(share.astype(jnp.float32), axis=0).astype(bf16)
    share = share.reshape(n_z, model // owners, width)
    share = lax.all_to_all(share, "z", 0, 0, tiled=True)
    weight_grad = jnp.sum(share.astype(jnp.float32), axis=0)

    grads = pl.pallas_call(
        attend_kernel,
        out_shape=shape((owners, heads * CAP, 3 * DH), bf16),
        scratch_shapes=[
            pltpu.VMEM((owners * CAP, owners * CAP), bf16),
            pltpu.VMEM((owners * CAP, owners * CAP), bf16),
        ],
        compiler_params=PARAMS,
        name="attend_cluster",
    )(qkv, cot)
    home = lax.all_to_all(grads, SEQ, 0, 0, tiled=True)
    dq, dk, dv = pl.pallas_call(
        unpack_kernel,
        out_shape=tuple(shape((tokens, width), bf16) for _ in range(3)),
        compiler_params=PARAMS,
        name="unpack_rows",
    )(home, places)
    return dq, dk, dv, weight_grad


def solution(mesh):
    n_seq, n_head = mesh.devices.shape
    n_x, n_y = 4, n_head // 2
    grid = Mesh(mesh.devices.reshape(n_x, n_seq // n_x, n_y, 2), ("x", "z", "y", "core"))
    rows, ids = P(SEQ, HEAD), P(HEAD, SEQ)
    return jax.shard_map(
        local,
        mesh=grid,
        in_specs=(rows,) * 6 + (ids,) * 2,
        out_specs=(rows,) * 4,
        check_vma=False,
    )
```

time: 1120 us -> 319 us (0.28)
  waiting for transfers between devices: 955 us -> 197 us
  local copies, waits for them, and re-layouts: 89.8 us -> 3.41 us
  blocking collectives: 0 us -> 33.4 us
  Pallas kernels: 0 us -> 16.5 us
    reduce_scatter x1 -> x0, waiting for transfers between devices: 621 us -> none  [local(): lax.psum_scatter(jnp.einsum('tc,td->cd', columns, saved_output, preferred...]
    all_gather x2 -> x1, waiting for transfers between devices: 139 us -> 1.66 us  [local(): full_grad = lax.all_gather(output_grad, HEAD, axis=1, tiled=True)]
    gather x12 -> x0, local copies, waits for them, and re-layouts: 61.5 us -> none  [the longest x1 22.7 us: local(): gathered = jnp.take_along_axis(padded, source_of[:, :, None], axis=1)]
    all_to_all x0 -> x1, blocking collectives: none -> 33.4 us  [copies_to_all(): lax.all_to_all(jnp.broadcast_to(block[None], (size, *block.shape)), axis,...]
    pallas_call x0 -> x4, Pallas kernels: none -> 16.5 us  [the longest x1 7.32 us: local(): pl.pallas_call(attend_kernel, out_shape=shape((owners, heads * CAP, 3 * D...]
    all_to_all x3 -> x6, starting transfers between devices: 44 us -> 47.9 us  [the longest x1 16.7 us: local(): qkv = lax.all_to_all(qkv, SEQ, 0, 0, tiled=True)]
    all_to_all x3 -> x6, waiting for transfers between devices: 194 us -> 195 us  [the longest x1 74.1 us: local(): home = lax.all_to_all(grads, SEQ, 0, 0, tiled=True)]
  transfers between devices with their start and end apart: 6 -> 7, of which waited for: 5 -> 7; matrix products, arithmetic and copies ran while one was open for 6% -> 2% of each run, Pallas kernels for 0% -> 4%
where the time goes in v1:
time: 319 us
  waiting for transfers between devices  197 us (62%)
  starting transfers between devices  47.9 us (15%)
  blocking collectives  33.4 us (10%)
  Pallas kernels  16.5 us (5%)
  between operations  14.1 us (4%)
  local copies, waits for them, and re-layouts  3.41 us (1%)
  matrix products  3.35 us (1%)
    all_to_all x1, waiting for transfers between devices, local(): home = lax.all_to_all(grads, SEQ, 0, 0, tiled=True)  74.1 us
    all_to_all x1, waiting for transfers between devices, local(): qkv = lax.all_to_all(qkv, SEQ, 0, 0, tiled=True)  68.7 us
    all_to_all x1, blocking collectives, copies_to_all(): lax.all_to_all(jnp.broadcast_to(block[None], (size, *block.shape)), axis,...  33.4 us
    all_to_all x1, waiting for transfers between devices, local(): cot = lax.all_to_all(cot, SEQ, 0, 0, tiled=True)  32.6 us
    all_to_all x1, starting transfers between devices, local(): qkv = lax.all_to_all(qkv, SEQ, 0, 0, tiled=True)  16.7 us
    all_to_all x1, waiting for transfers between devices, local(): share = lax.all_to_all(share, 'z', 0, 0, tiled=True)  9.88 us
    all_to_all x1, starting transfers between devices, local(): home = lax.all_to_all(grads, SEQ, 0, 0, tiled=True)  8.71 us
    all_to_all x1, starting transfers between devices, local(): cot = lax.all_to_all(cot, SEQ, 0, 0, tiled=True)  7.43 us
  transfers between devices with their start and end apart: 7, of which 7 were waited for; matrix products, arithmetic and copies ran while one was open for 2% of the time, Pallas kernels for 4%

profile of v1, /device:TPU:6, one launch (start us, length us, event | category | flops | bytes accessed | tf_op | source)
XLA Modules:
  0.0 318.6 jit_solution(2096515679838896454)
XLA Ops:
  7.2 0.7 all-gather.2.cloned.1.call-update
  7.9 0.8 broadcast_in_dim.6
  8.7 33.4 %all_to_all.35 = bf16[16,32,256]{2,1,0:T(8,128)(2,1)S(1)} all-to-all(bf16[16,32,256]{2,1,0:T(8,128)(2,1)S(1)} %broadcast_in_dim.6), channel_id=1, replica_groups=mesh['x'=4,'z'=16,'y'=4,'core'=2] {'z'}, dimensions={0} | all-to-all | bytes 524288 | tf_op jit(solution)/shard_map/all_to_all | solution.py:187
  42.1 1.0 broadcast_in_dim.15
  43.1 4.8 %all-to-all-start.2 = ((bf16[4,512,256]{2,1,0:T(8,128)(2,1)}), bf16[4,512,256]{2,1,0:T(8,128)(2,1)S(1)}, u32[]{:S(2)}, u32[]{:S(2)}) async-start(bf16[4,512,256]{2,1,0:T(8,128)(2,1)} %broadcast_in_dim.15), calls=%async_computation.2 | async-start | bytes 2097152 | tf_op jit(solution)/shard_map/all_to_all | solution.py:187
  47.8 1.7 all-gather.2.cloned.1.call-done.grad_ref
  49.5 3.3 %convolution_convert_fusion = bf16[2048,256]{1,0:T(8,128)(2,1)} fusion(bf16[512,2048]{1,0:T(8,128)(2,1)} %all-gather.2.cloned.1.call-done.grad_ref, bf16[512,256]{1,0:T(8,128)(2,1)S(1)} %copy-done.4), kind=kOutput, calls=%fused_computation | convolution fusion | flops 537395200 | bytes 3407872 | tf_op jit(solution)/shard_map/tc,td->cd/dot_general | solution.py:224
  52.9 3.8 %all-to-all-done.2 = bf16[4,512,256]{2,1,0:T(8,128)(2,1)S(1)} async-done(((bf16[4,512,256]{2,1,0:T(8,128)(2,1)}), bf16[4,512,256]{2,1,0:T(8,128)(2,1)S(1)}, u32[]{:S(2)}, u32[]{:S(2)}) %all-to-all-start.2) | async-done | bytes 1048608 | tf_op jit(solution)/shard_map/all_to_all | solution.py:187
  56.7 6.3 %all-to-all-start.5 = ((bf16[4,512,256]{2,1,0:T(8,128)(2,1)}), bf16[4,512,256]{2,1,0:T(8,128)(2,1)}, u32[]{:S(2)}, u32[]{:S(2)}) async-start(bf16[4,512,256]{2,1,0:T(8,128)(2,1)} %bitcast.2), calls=%async_computation.5 | async-start | bytes 2097152 | tf_op jit(solution)/shard_map/all_to_all | solution.py:228
  63.0 3.2 pack_rows.1
  66.1 5.7 %all-to-all-done.5 = bf16[4,512,256]{2,1,0:T(8,128)(2,1)} async-done(((bf16[4,512,256]{2,1,0:T(8,128)(2,1)}), bf16[4,512,256]{2,1,0:T(8,128)(2,1)}, u32[]{:S(2)}, u32[]{:S(2)}) %all-to-all-start.5) | async-done | bytes 1048608 | tf_op jit(solution)/shard_map/all_to_all | solution.py:228
  71.9 16.7 %all-to-all-start = ((bf16[64,32,384]{2,1,0:T(8,128)(2,1)}), bf16[64,32,384]{2,1,0:T(8,128)(2,1)S(1)}, u32[]{:S(2)}, u32[]{:S(2)}) async-start(bf16[64,32,384]{2,1,0:T(8,128)(2,1)} %pack_rows.1), calls=%async_computation | async-start | bytes 3145728 | tf_op jit(solution)/shard_map/all_to_all | solution.py:211
  88.6 1.6 copy-done
  90.2 3.3 %cotangent_rows.1 = (bf16[64,40,128]{2,1,0:T(8,128)(2,1)}, s32[512,8]{1,0:T(8,128)S(1)}) custom-call(s32[2,512]{1,0:T(2,128)S(1)} %copy-done.5, bf16[512,2048]{1,0:T(8,128)(2,1)S(1)} %copy-done, bf16[2048,256]{1,0:T(8,128)(2,1)S(1)} %bitcast.6, bf16[512,256]{1,0:T(8,128)(2,1)S(1)} %copy-done.4), custom_call_target="tpu_custom_call" | custom-call | tf_op jit(solution)/shard_map/cotangent_rows/pallas_call | solution.py:213
  93.5 68.7 %all-to-all-done.qkv_ref = bf16[64,32,384]{2,1,0:T(8,128)(2,1)S(1)} async-done(((bf16[64,32,384]{2,1,0:T(8,128)(2,1)}), bf16[64,32,384]{2,1,0:T(8,128)(2,1)S(1)}, u32[]{:S(2)}, u32[]{:S(2)}) %all-to-all-start) | async-done | bytes 1572896 | tf_op jit(solution)/shard_map/all_to_all | solution.py:211
  162.2 7.4 %all-to-all-start.3 = ((bf16[64,40,128]{2,1,0:T(8,128)(2,1)}), bf16[64,40,128]{2,1,0:T(8,128)(2,1)S(1)}, u32[]{:S(2)}, u32[]{:S(2)}) async-start(bf16[64,40,128]{2,1,0:T(8,128)(2,1)} %get-tuple-element.9), calls=%async_computation.3 | async-start | bytes 1310720 | tf_op jit(solution)/shard_map/all_to_all | solution.py:222
  169.6 2.2 reduce_sum.21
  171.8 32.6 %all-to-all-done.3.g_ref = bf16[64,40,128]{2,1,0:T(8,128)(2,1)S(1)} async-done(((bf16[64,40,128]{2,1,0:T(8,128)(2,1)}), bf16[64,40,128]{2,1,0:T(8,128)(2,1)S(1)}, u32[]{:S(2)}, u32[]{:S(2)}) %all-to-all-start.3) | async-done | bytes 655392 | tf_op jit(solution)/shard_map/all_to_all | solution.py:222
  204.4 4.0 %all-to-all-start.6 = ((bf16[16,32,256]{2,1,0:T(8,128)(2,1)}), bf16[16,32,256]{2,1,0:T(8,128)(2,1)S(1)}, u32[]{:S(2)}, u32[]{:S(2)}) async-start(bf16[16,32,256]{2,1,0:T(8,128)(2,1)} %bitcast.3), calls=%async_computation.6 | async-start | bytes 524288 | tf_op jit(solution)/shard_map/all_to_all | solution.py:231
  208.4 7.3 %attend_cluster.1 = bf16[64,32,384]{2,1,0:T(8,128)(2,1)} custom-call(bf16[64,32,384]{2,1,0:T(8,128)(2,1)S(1)} %all-to-all-done.qkv_ref, bf16[64,40,128]{2,1,0:T(8,128)(2,1)S(1)} %all-to-all-done.3.g_ref), custom_call_target="tpu_custom_call" | custom-call | tf_op jit(solution)/shard_map/attend_cluster/pallas_call | solution.py:234
  215.7 9.9 %all-to-all-done.6 = bf16[16,32,256]{2,1,0:T(8,128)(2,1)S(1)} async-done(((bf16[16,32,256]{2,1,0:T(8,128)(2,1)}), bf16[16,32,256]{2,1,0:T(8,128)(2,1)S(1)}, u32[]{:S(2)}, u32[]{:S(2)}) %all-to-all-start.6) | async-done | bytes 262176 | tf_op jit(solution)/shard_map/all_to_all | solution.py:231
  225.6 8.7 %all-to-all-start.4 = ((bf16[64,32,384]{2,1,0:T(8,128)(2,1)}), bf16[64,32,384]{2,1,0:T(8,128)(2,1)S(1)}, u32[]{:S(2)}, u32[]{:S(2)}) async-start(bf16[64,32,384]{2,1,0:T(8,128)(2,1)} %attend_cluster.1), calls=%async_computation.4 | async-start | bytes 3145728 | tf_op jit(solution)/shard_map/all_to_all | solution.py:244
  235.0 74.1 %all-to-all-done.4.home_ref = bf16[64,32,384]{2,1,0:T(8,128)(2,1)S(1)} async-done(((bf16[64,32,384]{2,1,0:T(8,128)(2,1)}), bf16[64,32,384]{2,1,0:T(8,128)(2,1)S(1)}, u32[]{:S(2)}, u32[]{:S(2)}) %all-to-all-start.4) | async-done | bytes 1572896 | tf_op jit(solution)/shard_map/all_to_all | solution.py:244
  309.1 2.6 unpack_rows.1
  (13 shorter events, 0.7 us)
Async XLA Ops:
  7.2 42.3 %all-gather.2.cloned.1.call-start = ((), (), s32[]{:S(2)}) async-start(), calls=%async_computation.7 | async-start | bytes 2359296 | tf_op jit(solution)/shard_map/all_gather | solution.py:201
  7.9 41.6 %copy-start.4 = (bf16[512,256]{1,0:T(8,128)(2,1)S(1)}, bf16[512,256]{1,0:T(8,128)(2,1)}, u32[]{:S(2)}) copy-start(bf16[512,256]{1,0:T(8,128)(2,1)} %saved_ref.1) | copy-start | bytes 786436
  43.1 13.6 %all-to-all-start.2 = ((bf16[4,512,256]{2,1,0:T(8,128)(2,1)}), bf16[4,512,256]{2,1,0:T(8,128)(2,1)S(1)}, u32[]{:S(2)}, u32[]{:S(2)}) async-start(bf16[4,512,256]{2,1,0:T(8,128)(2,1)} %broadcast_in_dim.15), calls=%async_computation.2 | async-start | bytes 2097152 | tf_op jit(solution)/shard_map/all_to_all | solution.py:187
  52.9 10.1 %copy-start.1 = (bf16[512,256]{1,0:T(8,128)(2,1)S(1)}, bf16[512,256]{1,0:T(8,128)(2,1)}, u32[]{:S(2)}) copy-start(bf16[512,256]{1,0:T(8,128)(2,1)} %q_ref.1) | copy-start | bytes 786436
  52.9 10.1 %copy-start.2 = (bf16[512,256]{1,0:T(8,128)(2,1)S(1)}, bf16[512,256]{1,0:T(8,128)(2,1)}, u32[]{:S(2)}) copy-start(bf16[512,256]{1,0:T(8,128)(2,1)} %k_ref.1) | copy-start | bytes 786436
  52.9 10.1 %copy-start.3 = (bf16[512,256]{1,0:T(8,128)(2,1)S(1)}, bf16[512,256]{1,0:T(8,128)(2,1)}, u32[]{:S(2)}) copy-start(bf16[512,256]{1,0:T(8,128)(2,1)} %v_ref.1) | copy-start | bytes 786436
  52.9 10.1 %copy-start.5 = (s32[2,512]{1,0:T(2,128)S(1)}, s32[2,512]{1,0:T(2,128)}, u32[]{:S(2)}) copy-start(s32[2,512]{1,0:T(2,128)} %ids_ref.3) | copy-start | bytes 12292
  56.7 15.2 %all-to-all-start.5 = ((bf16[4,512,256]{2,1,0:T(8,128)(2,1)}), bf16[4,512,256]{2,1,0:T(8,128)(2,1)}, u32[]{:S(2)}, u32[]{:S(2)}) async-start(bf16[4,512,256]{2,1,0:T(8,128)(2,1)} %bitcast.2), calls=%async_computation.5 | async-start | bytes 2097152 | tf_op jit(solution)/shard_map/all_to_all | solution.py:228
  71.9 90.3 %all-to-all-start = ((bf16[64,32,384]{2,1,0:T(8,128)(2,1)}), bf16[64,32,384]{2,1,0:T(8,128)(2,1)S(1)}, u32[]{:S(2)}, u32[]{:S(2)}) async-start(bf16[64,32,384]{2,1,0:T(8,128)(2,1)} %pack_rows.1), calls=%async_computation | async-start | bytes 3145728 | tf_op jit(solution)/shard_map/all_to_all | solution.py:211
  88.6 1.6 copy-start
  162.2 42.2 %all-to-all-start.3 = ((bf16[64,40,128]{2,1,0:T(8,128)(2,1)}), bf16[64,40,128]{2,1,0:T(8,128)(2,1)S(1)}, u32[]{:S(2)}, u32[]{:S(2)}) async-start(bf16[64,40,128]{2,1,0:T(8,128)(2,1)} %get-tuple-element.9), calls=%async_computation.3 | async-start | bytes 1310720 | tf_op jit(solution)/shard_map/all_to_all | solution.py:222
  204.4 21.2 %all-to-all-start.6 = ((bf16[16,32,256]{2,1,0:T(8,128)(2,1)}), bf16[16,32,256]{2,1,0:T(8,128)(2,1)S(1)}, u32[]{:S(2)}, u32[]{:S(2)}) async-start(bf16[16,32,256]{2,1,0:T(8,128)(2,1)} %bitcast.3), calls=%async_computation.6 | async-start | bytes 524288 | tf_op jit(solution)/shard_map/all_to_all | solution.py:231
  225.6 83.5 %all-to-all-start.4 = ((bf16[64,32,384]{2,1,0:T(8,128)(2,1)}), bf16[64,32,384]{2,1,0:T(8,128)(2,1)S(1)}, u32[]{:S(2)}, u32[]{:S(2)}) async-start(bf16[64,32,384]{2,1,0:T(8,128)(2,1)} %attend_cluster.1), calls=%async_computation.4 | async-start | bytes 3145728 | tf_op jit(solution)/shard_map/all_to_all | solution.py:244
Sparse Core Ops, SparseCore 0:
  10.1 39.3 all-gather.1

commit v2 on v1

--- a/solution.py
+++ b/solution.py
@@ -13,7 +13,9 @@
 BLOCK = 256
 MASKED = -1e30
 SCALE = 1.0 / math.sqrt(DH)
-SEQ = ("x", "z")
+LOG2_E = math.log2(math.e)
+Z = ("z_hi", "z_lo")
+SEQ = ("x", *Z)
 HEAD = ("y", "core")
 PARAMS = pltpu.CompilerParams(vmem_limit_bytes=48 * 1024 * 1024)
 
@@ -129,26 +131,24 @@
         v_wide = jnp.concatenate([v, minus_one], axis=1)
         for start in range(0, slots, BLOCK):
             stop = start + BLOCK
-            scores = (
-                lax.dot_general(
-                    k_wide[:stop], q_wide[start:stop], contract_last,
-                    preferred_element_type=jnp.float32,
-                )
-                * SCALE
+            scores = lax.dot_general(
+                k_wide[:stop], q_wide[start:stop], contract_last,
+                preferred_element_type=jnp.float32,
             )
             last = jnp.where(later, MASKED, scores[start:stop])
             if start:
                 scores = jnp.concatenate([scores[:start], last], axis=0)
             else:
                 scores = last
-            exponent = jnp.exp(scores - jnp.max(scores, axis=0, keepdims=True))
-            prob = exponent * (1.0 / jnp.sum(exponent, axis=0, keepdims=True))
+            row_max = jnp.max(scores, axis=0, keepdims=True)
+            exponent = jnp.exp2((scores - row_max) * (SCALE * LOG2_E))
+            inverse = 1.0 / jnp.sum(exponent, axis=0, keepdims=True)
             grad_prob = lax.dot_general(
                 v_wide[:stop], g_wide[start:stop], contract_last,
                 preferred_element_type=jnp.float32,
             )
-            grad_score = (prob * grad_prob * SCALE).astype(jnp.bfloat16)
-            prob_ref[:stop, start:stop] = prob.astype(jnp.bfloat16)
+            grad_score = (exponent * (inverse * SCALE) * grad_prob).astype(jnp.bfloat16)
+            prob_ref[:stop, start:stop] = (exponent * inverse).astype(jnp.bfloat16)
             score_ref[:stop, start:stop] = grad_score
             grad_query = lax.dot_general(
                 grad_score, k[:stop], contract_first, preferred_element_type=jnp.float32
@@ -189,6 +189,10 @@
     )
 
 
+def after(value, earlier):
+    return lax.optimization_barrier((value, earlier))[0]
+
+
 def local(
     query_rows, key_rows, value_rows, saved_output, output_grad, out_weight, cluster_id, _slot
 ):
@@ -199,8 +203,8 @@
     shape = jax.ShapeDtypeStruct
 
     full_grad = lax.all_gather(output_grad, HEAD, axis=1, tiled=True)
-    weight_z = copies_to_all(out_weight, "z").reshape(-1, width)
-    weight = copies_to_all(weight_z, "x").reshape(-1, width)
+    weight_z = copies_to_all(out_weight, Z).reshape(-1, width)
+    weight = lax.all_gather(weight_z, "x", axis=0, tiled=True)
 
     qkv = pl.pallas_call(
         pack_kernel,
@@ -208,7 +212,7 @@
         compiler_params=PARAMS,
         name="pack_rows",
     )(cluster_id, query_rows, key_rows, value_rows)
-    qkv = lax.all_to_all(qkv, SEQ, 0, 0, tiled=True)
+    qkv = lax.all_to_all(after(qkv, weight_z), SEQ, 0, 0, tiled=True)
 
     cot, places = pl.pallas_call(
         cotangent_kernel,
@@ -219,17 +223,13 @@
         compiler_params=PARAMS,
         name="cotangent_rows",
     )(cluster_id, full_grad, weight, saved_output)
-    cot = lax.all_to_all(cot, SEQ, 0, 0, tiled=True)
-
     share = jnp.einsum("tc,td->cd", full_grad, saved_output, preferred_element_type=jnp.float32)
-    model = share.shape[0]
-    n_x, n_z = lax.axis_size("x"), lax.axis_size("z")
-    share = share.astype(bf16).reshape(n_x, model // n_x, width)
-    share = lax.all_to_all(share, "x", 0, 0, tiled=True)
-    share = jnp.sum(share.astype(jnp.float32), axis=0).astype(bf16)
-    share = share.reshape(n_z, model // owners, width)
-    share = lax.all_to_all(share, "z", 0, 0, tiled=True)
-    weight_grad = jnp.sum(share.astype(jnp.float32), axis=0)
+    n_x, n_hi, n_lo = (lax.axis_size(axis) for axis in SEQ)
+    share = share.reshape(n_x, n_hi, n_lo, -1, width).transpose(0, 2, 1, 3, 4)
+    share = after(share.reshape(full_grad.shape[1], width), weight)
+    cot = lax.all_to_all(after(cot, (share, qkv)), SEQ, 0, 0, tiled=True)
+    share = lax.psum_scatter(share, "x", scatter_dimension=0, tiled=True)
+    share = lax.psum_scatter(share, "z_lo", scatter_dimension=0, tiled=True)
 
     grads = pl.pallas_call(
         attend_kernel,
@@ -241,7 +241,8 @@
         compiler_params=PARAMS,
         name="attend_cluster",
     )(qkv, cot)
-    home = lax.all_to_all(grads, SEQ, 0, 0, tiled=True)
+    home = lax.all_to_all(after(grads, share), SEQ, 0, 0, tiled=True)
+    weight_grad = lax.psum_scatter(share, "z_hi", scatter_dimension=0, tiled=True)
     dq, dk, dv = pl.pallas_call(
         unpack_kernel,
         out_shape=tuple(shape((tokens, width), bf16) for _ in range(3)),
@@ -252,9 +253,8 @@
 
 
 def solution(mesh):
-    n_seq, n_head = mesh.devices.shape
-    n_x, n_y = 4, n_head // 2
-    grid = Mesh(mesh.devices.reshape(n_x, n_seq // n_x, n_y, 2), ("x", "z", "y", "core"))
+    n_head = mesh.devices.shape[1]
+    grid = Mesh(mesh.devices.reshape(4, 4, 4, n_head // 2, 2), (*SEQ, *HEAD))
     rows, ids = P(SEQ, HEAD), P(HEAD, SEQ)
     return jax.shard_map(
         local,

time: 319 us -> 281 us (0.88)
  blocking collectives: 33.4 us -> 0 us
  starting transfers between devices: 47.9 us -> 40.1 us
  local copies, waits for them, and re-layouts: 3.41 us -> 7.65 us
    all_to_all x5 -> x3, waiting for transfers between devices: 191 us -> 153 us  [the longest x1 79.3 us: local(): home = lax.all_to_all(after(grads, share), SEQ, 0, 0, tiled=True)]
    all_to_all x1 -> x0, blocking collectives: 33.4 us -> none  [copies_to_all(): lax.all_to_all(jnp.broadcast_to(block[None], (size, *block.shape)), axis,...]
    all_gather x0 -> x1, waiting for transfers between devices: none -> 31.9 us  [local(): weight = lax.all_gather(weight_z, 'x', axis=0, tiled=True)]
    all_to_all x5 -> x3, starting transfers between devices: 43.1 us -> 24.6 us  [the longest x1 9.55 us: local(): qkv = lax.all_to_all(after(qkv, weight_z), SEQ, 0, 0, tiled=True)]
    all_to_all x1, starting transfers between devices: 4.77 us -> 15.2 us  [copies_to_all(): lax.all_to_all(jnp.broadcast_to(block[None], (size, *block.shape)), axis,...]
    all_to_all x1, waiting for transfers between devices: 3.81 us -> 11.6 us  [copies_to_all(): lax.all_to_all(jnp.broadcast_to(block[None], (size, *block.shape)), axis,...]
  transfers between devices with their start and end apart: 7 -> 9, of which waited for: 7 -> 5; matrix products, arithmetic and copies ran while one was open for 2% -> 2% of each run, Pallas kernels for 4% -> 6%
where the time goes in v2:
time: 281 us; the launch traced here: 280 us
  waiting for transfers between devices  199 us (71%)
  starting transfers between devices  40.1 us (14%)
  Pallas kernels  17.7 us (6%)
  between operations  13.9 us (5%)
  local copies, waits for them, and re-layouts  7.65 us (3%)
    all_to_all x1, waiting for transfers between devices, local(): home = lax.all_to_all(after(grads, share), SEQ, 0, 0, tiled=True)  79.3 us
    all_to_all x1, waiting for transfers between devices, local(): cot = lax.all_to_all(after(cot, (share, qkv)), SEQ, 0, 0, tiled=True)  38.6 us
    all_to_all x1, waiting for transfers between devices, local(): qkv = lax.all_to_all(after(qkv, weight_z), SEQ, 0, 0, tiled=True)  35 us
    all_gather x1, waiting for transfers between devices, local(): weight = lax.all_gather(weight_z, 'x', axis=0, tiled=True)  31.9 us
    all_to_all x1, starting transfers between devices, copies_to_all(): lax.all_to_all(jnp.broadcast_to(block[None], (size, *block.shape)), axis,...  15.2 us
    all_to_all x1, waiting for transfers between devices, copies_to_all(): lax.all_to_all(jnp.broadcast_to(block[None], (size, *block.shape)), axis,...  11.6 us
    all_to_all x1, starting transfers between devices, local(): qkv = lax.all_to_all(after(qkv, weight_z), SEQ, 0, 0, tiled=True)  9.55 us
    pallas_call x1, Pallas kernels, local(): pl.pallas_call(attend_kernel, out_shape=shape((owners, heads * CAP, 3 * D...  8.55 us
  transfers between devices with their start and end apart: 9, of which 5 were waited for; matrix products, arithmetic and copies ran while one was open for 2% of the time, Pallas kernels for 6%

profile of v2, /device:TPU:6, one launch (start us, length us, event | category | flops | bytes accessed | tf_op | source)
XLA Modules:
  0.0 280.4 jit_solution(5856358759479254236)
XLA Ops:
  7.2 0.7 all-gather.3.cloned.1.call-update
  7.9 1.4 broadcast_in_dim.2
  9.3 15.2 %all-to-all-start = ((bf16[16,32,256]{2,1,0:T(8,128)(2,1)}), bf16[16,32,256]{2,1,0:T(8,128)(2,1)S(1)}, u32[]{:S(2)}, u32[]{:S(2)}) async-start(bf16[16,32,256]{2,1,0:T(8,128)(2,1)} %broadcast_in_dim.2), calls=%async_computation | async-start | bytes 524288 | tf_op jit(solution)/shard_map/all_to_all | solution.py:187
  24.6 0.9 copy-done.3
  25.5 0.9 copy-done.4
  26.5 0.9 copy-done.5
  27.4 0.7 copy-done.6
  28.1 3.2 %pack_rows.1 = bf16[64,32,384]{2,1,0:T(8,128)(2,1)} custom-call(s32[2,512]{1,0:T(2,128)S(1)} %copy-done.6, bf16[512,256]{1,0:T(8,128)(2,1)S(1)} %copy-done.3, bf16[512,256]{1,0:T(8,128)(2,1)S(1)} %copy-done.4, bf16[512,256]{1,0:T(8,128)(2,1)S(1)} %copy-done.5), custom_call_target="tpu_custom_call" | custom-call | tf_op jit(solution)/shard_map/pack_rows/pallas_call | solution.py:209
  31.3 11.6 %all-to-all-done = bf16[16,32,256]{2,1,0:T(8,128)(2,1)S(1)} async-done(((bf16[16,32,256]{2,1,0:T(8,128)(2,1)}), bf16[16,32,256]{2,1,0:T(8,128)(2,1)S(1)}, u32[]{:S(2)}, u32[]{:S(2)}) %all-to-all-start) | async-done | bytes 262176 | tf_op jit(solution)/shard_map/all_to_all | solution.py:187
  42.9 9.6 %all-to-all-start.1 = ((bf16[64,32,384]{2,1,0:T(8,128)(2,1)}), bf16[64,32,384]{2,1,0:T(8,128)(2,1)}, u32[]{:S(2)}, u32[]{:S(2)}) async-start(bf16[64,32,384]{2,1,0:T(8,128)(2,1)} %pack_rows.1), calls=%async_computation.1 | async-start | bytes 3145728 | tf_op jit(solution)/shard_map/all_to_all | solution.py:215
  52.5 0.7 all-gather.5.cloned.1.call-update
  53.3 2.3 fusion
  55.6 1.4 copy.11
  57.1 31.9 %all-gather.5.cloned.1.call-done.weight_ref = bf16[2048,256]{1,0:T(8,128)(2,1)} async-done(((bf16[512,256]{1,0:T(8,128)(2,1)}), bf16[2048,256]{1,0:T(8,128)(2,1)}) %all-gather.5.cloned.1.call-update) | async-done | bytes 1048592 | tf_op jit(solution)/shard_map/all_gather | solution.py:207
  89.1 1.2 copy-done.2
  90.3 3.4 %cotangent_rows.1 = (bf16[64,40,128]{2,1,0:T(8,128)(2,1)}, s32[512,8]{1,0:T(8,128)S(1)}) custom-call(s32[2,512]{1,0:T(2,128)S(1)} %copy-done.7, bf16[512,2048]{1,0:T(8,128)(2,1)S(1)} %copy-done, bf16[2048,256]{1,0:T(8,128)(2,1)S(1)} %copy-done.2, bf16[512,256]{1,0:T(8,128)(2,1)S(1)} %copy-done.1), custom_call_target="tpu_custom_call" | custom-call | tf_op jit(solution)/shard_map/cotangent_rows/pallas_call | solution.py:217
  93.7 35.0 %all-to-all-done.1.qkv_ref = bf16[64,32,384]{2,1,0:T(8,128)(2,1)} async-done(((bf16[64,32,384]{2,1,0:T(8,128)(2,1)}), bf16[64,32,384]{2,1,0:T(8,128)(2,1)}, u32[]{:S(2)}, u32[]{:S(2)}) %all-to-all-start.1) | async-done | bytes 1572896 | tf_op jit(solution)/shard_map/all_to_all | solution.py:215
  128.6 6.9 %all-to-all-start.2 = ((bf16[64,40,128]{2,1,0:T(8,128)(2,1)}), bf16[64,40,128]{2,1,0:T(8,128)(2,1)S(1)}, u32[]{:S(2)}, u32[]{:S(2)}) async-start(bf16[64,40,128]{2,1,0:T(8,128)(2,1)} %get-tuple-element.16), calls=%async_computation.2 | async-start | bytes 1310720 | tf_op jit(solution)/shard_map/all_to_all | solution.py:230
  136.1 38.6 %all-to-all-done.2.g_ref = bf16[64,40,128]{2,1,0:T(8,128)(2,1)S(1)} async-done(((bf16[64,40,128]{2,1,0:T(8,128)(2,1)}), bf16[64,40,128]{2,1,0:T(8,128)(2,1)S(1)}, u32[]{:S(2)}, u32[]{:S(2)}) %all-to-all-start.2) | async-done | bytes 655392 | tf_op jit(solution)/shard_map/all_to_all | solution.py:230
  174.7 8.5 %attend_cluster.1 = bf16[64,32,384]{2,1,0:T(8,128)(2,1)} custom-call(bf16[64,32,384]{2,1,0:T(8,128)(2,1)} %all-to-all-done.1.qkv_ref, bf16[64,40,128]{2,1,0:T(8,128)(2,1)S(1)} %all-to-all-done.2.g_ref), custom_call_target="tpu_custom_call" | custom-call | tf_op jit(solution)/shard_map/attend_cluster/pallas_call | solution.py:234
  183.3 8.1 %all-to-all-start.3 = ((bf16[64,32,384]{2,1,0:T(8,128)(2,1)}), bf16[64,32,384]{2,1,0:T(8,128)(2,1)S(1)}, u32[]{:S(2)}, u32[]{:S(2)}) async-start(bf16[64,32,384]{2,1,0:T(8,128)(2,1)} %attend_cluster.1), calls=%async_computation.5 | async-start | bytes 3145728 | tf_op jit(solution)/shard_map/all_to_all | solution.py:244
  191.4 0.5 reduce-scatter.8.cloned.1.call-update
  192.0 79.3 %all-to-all-done.3.home_ref = bf16[64,32,384]{2,1,0:T(8,128)(2,1)S(1)} async-done(((bf16[64,32,384]{2,1,0:T(8,128)(2,1)}), bf16[64,32,384]{2,1,0:T(8,128)(2,1)S(1)}, u32[]{:S(2)}, u32[]{:S(2)}) %all-to-all-start.3) | async-done | bytes 1572896 | tf_op jit(solution)/shard_map/all_to_all | solution.py:244
  271.3 2.6 unpack_rows.1
  (24 shorter events, 0.8 us)
Async XLA Ops:
  7.2 46.1 %all-gather.3.cloned.1.call-start = ((), (), s32[]{:S(2)}) async-start(), calls=%async_computation.7 | async-start | bytes 2359296 | tf_op jit(solution)/shard_map/all_gather | solution.py:205
  9.3 33.6 %all-to-all-start = ((bf16[16,32,256]{2,1,0:T(8,128)(2,1)}), bf16[16,32,256]{2,1,0:T(8,128)(2,1)S(1)}, u32[]{:S(2)}, u32[]{:S(2)}) async-start(bf16[16,32,256]{2,1,0:T(8,128)(2,1)} %broadcast_in_dim.2), calls=%async_computation | async-start | bytes 524288 | tf_op jit(solution)/shard_map/all_to_all | solution.py:187
  24.5 1.0 copy-start.3
  25.5 0.9 copy-start.4
  26.5 0.9 copy-start.5
  27.4 0.7 copy-start.6
  31.3 22.0 %copy-start.1 = (bf16[512,256]{1,0:T(8,128)(2,1)S(1)}, bf16[512,256]{1,0:T(8,128)(2,1)}, u32[]{:S(2)}) copy-start(bf16[512,256]{1,0:T(8,128)(2,1)} %saved_ref.1) | copy-start | bytes 786436
  42.9 9.6 %copy-start.8 = (bf16[16,32,256]{2,1,0:T(8,128)(2,1)}, bf16[16,32,256]{2,1,0:T(8,128)(2,1)S(1)}, u32[]{:S(2)}) copy-start(bf16[16,32,256]{2,1,0:T(8,128)(2,1)S(1)} %all-to-all-done) | copy-start | bytes 786436
  42.9 85.7 %all-to-all-start.1 = ((bf16[64,32,384]{2,1,0:T(8,128)(2,1)}), bf16[64,32,384]{2,1,0:T(8,128)(2,1)}, u32[]{:S(2)}, u32[]{:S(2)}) async-start(bf16[64,32,384]{2,1,0:T(8,128)(2,1)} %pack_rows.1), calls=%async_computation.1 | async-start | bytes 3145728 | tf_op jit(solution)/shard_map/all_to_all | solution.py:215
  52.5 36.5 %all-gather.5.cloned.1.call-start = ((), (), s32[]{:S(2)}) async-start(), calls=%async_computation.8 | async-start | bytes 1310720 | tf_op jit(solution)/shard_map/all_gather | solution.py:207
  53.2 82.6 %reduce-scatter.4.cloned.1.call-start = ((), (), s32[]{:S(2)}) async-start(), calls=%async_computation.9 | async-start | bytes 2621440 | tf_op jit(solution)/shard_map/reduce_scatter | solution.py:231
  57.1 32.0 %copy-start = (bf16[512,2048]{1,0:T(8,128)(2,1)S(1)}, bf16[512,2048]{1,0:T(8,128)(2,1)}, u32[]{:S(2)}) copy-start(bf16[512,2048]{1,0:T(8,128)(2,1)} %all-gather.3.cloned.1.call-done.grad_ref) | copy-start | bytes 6291460
  57.1 32.0 %copy-start.7 = (s32[2,512]{1,0:T(2,128)S(1)}, s32[2,512]{1,0:T(2,128)}, u32[]{:S(2)}) copy-start(s32[2,512]{1,0:T(2,128)} %ids_ref.3) | copy-start | bytes 12292
  89.1 1.2 copy-start.2
  128.6 46.1 %all-to-all-start.2 = ((bf16[64,40,128]{2,1,0:T(8,128)(2,1)}), bf16[64,40,128]{2,1,0:T(8,128)(2,1)S(1)}, u32[]{:S(2)}, u32[]{:S(2)}) async-start(bf16[64,40,128]{2,1,0:T(8,128)(2,1)} %get-tuple-element.16), calls=%async_computation.2 | async-start | bytes 1310720 | tf_op jit(solution)/shard_map/all_to_all | solution.py:230
  135.6 47.7 %reduce-scatter.6.cloned.1.call-start = ((), (), s32[]{:S(2)}) async-start(), calls=%async_computation.10 | async-start | bytes 655360 | tf_op jit(solution)/shard_map/reduce_scatter | solution.py:232
  183.3 88.0 %all-to-all-start.3 = ((bf16[64,32,384]{2,1,0:T(8,128)(2,1)}), bf16[64,32,384]{2,1,0:T(8,128)(2,1)S(1)}, u32[]{:S(2)}, u32[]{:S(2)}) async-start(bf16[64,32,384]{2,1,0:T(8,128)(2,1)} %attend_cluster.1), calls=%async_computation.5 | async-start | bytes 3145728 | tf_op jit(solution)/shard_map/all_to_all | solution.py:244
  191.4 82.5 %reduce-scatter.8.cloned.1.call-start = ((), (), s32[]{:S(2)}) async-start(), calls=%async_computation.11 | async-start | bytes 163840 | tf_op jit(solution)/shard_map/reduce_scatter | solution.py:245
Sparse Core Ops, SparseCore 0:
  10.1 39.3 all-gather.2
  56.0 32.9 all-gather.4
  91.9 40.3 reduce-scatter.3
  139.1 37.1 reduce-scatter.5
  195.5 41.2 reduce-scatter.7

commit v3 on v2

--- a/solution.py
+++ b/solution.py
@@ -17,7 +17,8 @@
 Z = ("z_hi", "z_lo")
 SEQ = ("x", *Z)
 HEAD = ("y", "core")
-PARAMS = pltpu.CompilerParams(vmem_limit_bytes=48 * 1024 * 1024)
+EARLY = pl.CostEstimate(flops=70_000_000_000, bytes_accessed=0, transcendentals=0)
+PARAMS = pltpu.CompilerParams(vmem_limit_bytes=24 * 1024 * 1024)
 
 
 def pair_places(ids, owners):
@@ -125,6 +126,7 @@
         extra = jnp.where(term_lanes | bias_lanes, own, 0.0).astype(jnp.bfloat16)
         minus_one = jnp.where(term_lanes, -1.0, 0.0).astype(jnp.bfloat16)
         one = jnp.where(bias_lanes, 1.0, 0.0).astype(jnp.bfloat16)
+        k_turned = k.T
         q_wide = jnp.concatenate([q, one], axis=1)
         k_wide = jnp.concatenate([k, extra], axis=1)
         g_wide = jnp.concatenate([g, extra], axis=1)
@@ -150,14 +152,14 @@
             grad_score = (exponent * (inverse * SCALE) * grad_prob).astype(jnp.bfloat16)
             prob_ref[:stop, start:stop] = (exponent * inverse).astype(jnp.bfloat16)
             score_ref[:stop, start:stop] = grad_score
-            grad_query = lax.dot_general(
-                grad_score, k[:stop], contract_first, preferred_element_type=jnp.float32
-            )
+        for start in range(0, slots, BLOCK):
+            stop = start + BLOCK
+            grad_query = jnp.dot(
+                k_turned[:, :stop], score_ref[:stop, start:stop], preferred_element_type=jnp.float32
+            ).T
             out_ref[start // CAP : stop // CAP, h * CAP : (h + 1) * CAP, 0:DH] = (
                 grad_query.astype(jnp.bfloat16).reshape(BLOCK // CAP, CAP, DH)
             )
-        for start in range(0, slots, BLOCK):
-            stop = start + BLOCK
             for n, ref, other in ((1, score_ref, q), (2, prob_ref, g)):
                 grad = jnp.dot(
                     ref[start:stop, start:], other[start:], preferred_element_type=jnp.float32
@@ -165,6 +167,10 @@
                 out_ref[
                     start // CAP : stop // CAP, h * CAP : (h + 1) * CAP, n * DH : (n + 1) * DH
                 ] = grad.astype(jnp.bfloat16).reshape(BLOCK // CAP, CAP, DH)
+
+
+def copy_kernel(from_ref, to_ref):
+    to_ref[...] = from_ref[...]
 
 
 def unpack_kernel(home_ref, place_ref, dq_ref, dk_ref, dv_ref):
@@ -224,12 +230,16 @@
         name="cotangent_rows",
     )(cluster_id, full_grad, weight, saved_output)
     share = jnp.einsum("tc,td->cd", full_grad, saved_output, preferred_element_type=jnp.float32)
-    n_x, n_hi, n_lo = (lax.axis_size(axis) for axis in SEQ)
-    share = share.reshape(n_x, n_hi, n_lo, -1, width).transpose(0, 2, 1, 3, 4)
-    share = after(share.reshape(full_grad.shape[1], width), weight)
+    share = after(share, weight)
     cot = lax.all_to_all(after(cot, (share, qkv)), SEQ, 0, 0, tiled=True)
     share = lax.psum_scatter(share, "x", scatter_dimension=0, tiled=True)
-    share = lax.psum_scatter(share, "z_lo", scatter_dimension=0, tiled=True)
+    weight_grad = pl.pallas_call(
+        copy_kernel,
+        out_shape=shape(out_weight.shape, jnp.float32),
+        compiler_params=PARAMS,
+        cost_estimate=EARLY,
+        name="weight_grad",
+    )(lax.psum_scatter(share, Z, scatter_dimension=0, tiled=True))
 
     grads = pl.pallas_call(
         attend_kernel,
@@ -241,8 +251,7 @@
         compiler_params=PARAMS,
         name="attend_cluster",
     )(qkv, cot)
-    home = lax.all_to_all(after(grads, share), SEQ, 0, 0, tiled=True)
-    weight_grad = lax.psum_scatter(share, "z_hi", scatter_dimension=0, tiled=True)
+    home = lax.all_to_all(grads, SEQ, 0, 0, tiled=True)
     dq, dk, dv = pl.pallas_call(
         unpack_kernel,
         out_shape=tuple(shape((tokens, width), bf16) for _ in range(3)),

time: 281 us -> 274 us (0.975)
  waiting for transfers between devices: 199 us -> 194 us
    all_to_all x1, waiting for transfers between devices: 79.3 us -> 43.6 us  [local(): home = lax.all_to_all(grads, SEQ, 0, 0, tiled=True)]
    reduce_scatter x2 -> x1, waiting for transfers between devices: 0.01 us -> 32.2 us  [local(): lax.psum_scatter(share, Z, scatter_dimension=0, tiled=True)]
  transfers between devices with their start and end apart: 9 -> 8, of which waited for: 5 -> 6; matrix products, arithmetic and copies ran while one was open for 2% -> 2% of each run, Pallas kernels for 6% -> 5%
where the time goes in v3:
time: 274 us; the launch traced here: 273 us
  waiting for transfers between devices  194 us (71%)
  starting transfers between devices  38.1 us (14%)
  Pallas kernels  16.5 us (6%)
  between operations  13.9 us (5%)
  local copies, waits for them, and re-layouts  6.97 us (3%)
  matrix products  3.64 us (1%)
    all_to_all x1, waiting for transfers between devices, local(): home = lax.all_to_all(grads, SEQ, 0, 0, tiled=True)  43.6 us
    all_to_all x1, waiting for transfers between devices, local(): cot = lax.all_to_all(after(cot, (share, qkv)), SEQ, 0, 0, tiled=True)  37.9 us
    all_to_all x1, waiting for transfers between devices, local(): qkv = lax.all_to_all(after(qkv, weight_z), SEQ, 0, 0, tiled=True)  35 us
    reduce_scatter x1, waiting for transfers between devices, local(): lax.psum_scatter(share, Z, scatter_dimension=0, tiled=True)  32.2 us
    all_gather x1, waiting for transfers between devices, local(): weight = lax.all_gather(weight_z, 'x', axis=0, tiled=True)  32.1 us
    all_to_all x1, starting transfers between devices, copies_to_all(): lax.all_to_all(jnp.broadcast_to(block[None], (size, *block.shape)), axis,...  15.2 us
    all_to_all x1, waiting for transfers between devices, copies_to_all(): lax.all_to_all(jnp.broadcast_to(block[None], (size, *block.shape)), axis,...  11.7 us
    all_to_all x1, starting transfers between devices, local(): qkv = lax.all_to_all(after(qkv, weight_z), SEQ, 0, 0, tiled=True)  9.55 us
  transfers between devices with their start and end apart: 8, of which 6 were waited for; matrix products, arithmetic and copies ran while one was open for 2% of the time, Pallas kernels for 5%

profile of v3, /device:TPU:6, one launch (start us, length us, event | category | flops | bytes accessed | tf_op | source)
XLA Modules:
  0.0 273.5 jit_solution(9752391741415167578)
XLA Ops:
  7.2 0.7 all-gather.3.cloned.1.call-update
  7.9 1.4 broadcast_in_dim.2
  9.3 15.2 %all-to-all-start = ((bf16[16,32,256]{2,1,0:T(8,128)(2,1)}), bf16[16,32,256]{2,1,0:T(8,128)(2,1)S(1)}, u32[]{:S(2)}, u32[]{:S(2)}) async-start(bf16[16,32,256]{2,1,0:T(8,128)(2,1)} %broadcast_in_dim.2), calls=%async_computation | async-start | bytes 524288 | tf_op jit(solution)/shard_map/all_to_all | solution.py:193
  24.6 0.9 copy-done.3
  25.5 0.9 copy-done.4
  26.5 0.9 copy-done.5
  27.4 0.7 copy-done.6
  28.1 3.2 %pack_rows.1 = bf16[64,32,384]{2,1,0:T(8,128)(2,1)} custom-call(s32[2,512]{1,0:T(2,128)S(1)} %copy-done.6, bf16[512,256]{1,0:T(8,128)(2,1)S(1)} %copy-done.3, bf16[512,256]{1,0:T(8,128)(2,1)S(1)} %copy-done.4, bf16[512,256]{1,0:T(8,128)(2,1)S(1)} %copy-done.5), custom_call_target="tpu_custom_call" | custom-call | tf_op jit(solution)/shard_map/pack_rows/pallas_call | solution.py:215
  31.2 11.7 %all-to-all-done = bf16[16,32,256]{2,1,0:T(8,128)(2,1)S(1)} async-done(((bf16[16,32,256]{2,1,0:T(8,128)(2,1)}), bf16[16,32,256]{2,1,0:T(8,128)(2,1)S(1)}, u32[]{:S(2)}, u32[]{:S(2)}) %all-to-all-start) | async-done | bytes 262176 | tf_op jit(solution)/shard_map/all_to_all | solution.py:193
  42.9 9.6 %all-to-all-start.1 = ((bf16[64,32,384]{2,1,0:T(8,128)(2,1)}), bf16[64,32,384]{2,1,0:T(8,128)(2,1)}, u32[]{:S(2)}, u32[]{:S(2)}) async-start(bf16[64,32,384]{2,1,0:T(8,128)(2,1)} %pack_rows.1), calls=%async_computation.1 | async-start | bytes 3145728 | tf_op jit(solution)/shard_map/all_to_all | solution.py:221
  52.5 0.7 all-gather.5.cloned.1.call-update
  53.3 3.6 %fusion = f32[2048,256]{1,0:T(8,128)} fusion(bf16[512,2048]{1,0:T(8,128)(2,1)} %all-gather.3.cloned.1.call-done.grad_ref, bf16[512,256]{1,0:T(8,128)(2,1)S(1)} %copy-done.1), kind=kOutput, calls=%fused_computation | convolution fusion | flops 536870912 | bytes 4456448 | tf_op jit(solution)/shard_map/tc,td->cd/dot_general | solution.py:232
  57.0 32.1 %all-gather.5.cloned.1.call-done.weight_ref = bf16[2048,256]{1,0:T(8,128)(2,1)} async-done(((bf16[512,256]{1,0:T(8,128)(2,1)}), bf16[2048,256]{1,0:T(8,128)(2,1)}) %all-gather.5.cloned.1.call-update) | async-done | bytes 1048592 | tf_op jit(solution)/shard_map/all_gather | solution.py:213
  89.1 1.2 copy-done.2
  90.3 3.4 %cotangent_rows.1 = (bf16[64,40,128]{2,1,0:T(8,128)(2,1)}, s32[512,8]{1,0:T(8,128)S(1)}) custom-call(s32[2,512]{1,0:T(2,128)S(1)} %copy-done.7, bf16[512,2048]{1,0:T(8,128)(2,1)S(1)} %copy-done, bf16[2048,256]{1,0:T(8,128)(2,1)S(1)} %copy-done.2, bf16[512,256]{1,0:T(8,128)(2,1)S(1)} %copy-done.1), custom_call_target="tpu_custom_call" | custom-call | tf_op jit(solution)/shard_map/cotangent_rows/pallas_call | solution.py:223
  93.7 35.0 %all-to-all-done.1.qkv_ref = bf16[64,32,384]{2,1,0:T(8,128)(2,1)} async-done(((bf16[64,32,384]{2,1,0:T(8,128)(2,1)}), bf16[64,32,384]{2,1,0:T(8,128)(2,1)}, u32[]{:S(2)}, u32[]{:S(2)}) %all-to-all-start.1) | async-done | bytes 1572896 | tf_op jit(solution)/shard_map/all_to_all | solution.py:221
  128.6 6.9 %all-to-all-start.2 = ((bf16[64,40,128]{2,1,0:T(8,128)(2,1)}), bf16[64,40,128]{2,1,0:T(8,128)(2,1)S(1)}, u32[]{:S(2)}, u32[]{:S(2)}) async-start(bf16[64,40,128]{2,1,0:T(8,128)(2,1)} %get-tuple-element.15), calls=%async_computation.2 | async-start | bytes 1310720 | tf_op jit(solution)/shard_map/all_to_all | solution.py:234
  136.1 37.9 %all-to-all-done.2.g_ref = bf16[64,40,128]{2,1,0:T(8,128)(2,1)S(1)} async-done(((bf16[64,40,128]{2,1,0:T(8,128)(2,1)}), bf16[64,40,128]{2,1,0:T(8,128)(2,1)S(1)}, u32[]{:S(2)}, u32[]{:S(2)}) %all-to-all-start.2) | async-done | bytes 655392 | tf_op jit(solution)/shard_map/all_to_all | solution.py:234
  174.0 6.8 %attend_cluster.1 = bf16[64,32,384]{2,1,0:T(8,128)(2,1)} custom-call(bf16[64,32,384]{2,1,0:T(8,128)(2,1)} %all-to-all-done.1.qkv_ref, bf16[64,40,128]{2,1,0:T(8,128)(2,1)S(1)} %all-to-all-done.2.g_ref), custom_call_target="tpu_custom_call" | custom-call | tf_op jit(solution)/shard_map/attend_cluster/pallas_call | solution.py:244
  180.8 6.3 %all-to-all-start.3 = ((bf16[64,32,384]{2,1,0:T(8,128)(2,1)}), bf16[64,32,384]{2,1,0:T(8,128)(2,1)S(1)}, u32[]{:S(2)}, u32[]{:S(2)}) async-start(bf16[64,32,384]{2,1,0:T(8,128)(2,1)} %attend_cluster.1), calls=%async_computation.3 | async-start | bytes 3145728 | tf_op jit(solution)/shard_map/all_to_all | solution.py:254
  187.1 32.2 %reduce-scatter.5.cloned.1.call-done.from_ref = f32[32,256]{1,0:T(8,128)} async-done(((f32[512,256]{1,0:T(8,128)}), f32[32,256]{1,0:T(8,128)}) %reduce-scatter.5.cloned.1.call-update) | async-done | bytes 32784 | tf_op jit(solution)/shard_map/reduce_scatter | solution.py:242
  219.3 0.8 copy-done.8
  220.7 43.6 %all-to-all-done.3.home_ref = bf16[64,32,384]{2,1,0:T(8,128)(2,1)S(1)} async-done(((bf16[64,32,384]{2,1,0:T(8,128)(2,1)}), bf16[64,32,384]{2,1,0:T(8,128)(2,1)S(1)}, u32[]{:S(2)}, u32[]{:S(2)}) %all-to-all-start.3) | async-done | bytes 1572896 | tf_op jit(solution)/shard_map/all_to_all | solution.py:254
  264.3 2.6 unpack_rows.1
  (23 shorter events, 1.4 us)
Async XLA Ops:
  7.2 46.1 %all-gather.3.cloned.1.call-start = ((), (), s32[]{:S(2)}) async-start(), calls=%async_computation.6 | async-start | bytes 2359296 | tf_op jit(solution)/shard_map/all_gather | solution.py:211
  9.3 33.6 %all-to-all-start = ((bf16[16,32,256]{2,1,0:T(8,128)(2,1)}), bf16[16,32,256]{2,1,0:T(8,128)(2,1)S(1)}, u32[]{:S(2)}, u32[]{:S(2)}) async-start(bf16[16,32,256]{2,1,0:T(8,128)(2,1)} %broadcast_in_dim.2), calls=%async_computation | async-start | bytes 524288 | tf_op jit(solution)/shard_map/all_to_all | solution.py:193
  24.5 1.0 copy-start.3
  25.5 0.9 copy-start.4
  26.5 0.9 copy-start.5
  27.4 0.7 copy-start.6
  31.2 22.1 %copy-start.1 = (bf16[512,256]{1,0:T(8,128)(2,1)S(1)}, bf16[512,256]{1,0:T(8,128)(2,1)}, u32[]{:S(2)}) copy-start(bf16[512,256]{1,0:T(8,128)(2,1)} %saved_ref.1) | copy-start | bytes 786436
  42.9 9.6 %copy-start.9 = (bf16[16,32,256]{2,1,0:T(8,128)(2,1)}, bf16[16,32,256]{2,1,0:T(8,128)(2,1)S(1)}, u32[]{:S(2)}) copy-start(bf16[16,32,256]{2,1,0:T(8,128)(2,1)S(1)} %all-to-all-done) | copy-start | bytes 786436
  42.9 85.7 %all-to-all-start.1 = ((bf16[64,32,384]{2,1,0:T(8,128)(2,1)}), bf16[64,32,384]{2,1,0:T(8,128)(2,1)}, u32[]{:S(2)}, u32[]{:S(2)}) async-start(bf16[64,32,384]{2,1,0:T(8,128)(2,1)} %pack_rows.1), calls=%async_computation.1 | async-start | bytes 3145728 | tf_op jit(solution)/shard_map/all_to_all | solution.py:221
  52.5 36.5 %all-gather.5.cloned.1.call-start = ((), (), s32[]{:S(2)}) async-start(), calls=%async_computation.7 | async-start | bytes 1310720 | tf_op jit(solution)/shard_map/all_gather | solution.py:213
  53.2 82.4 %reduce-scatter.3.cloned.1.call-start = ((), (), s32[]{:S(2)}) async-start(), calls=%async_computation.8 | async-start | bytes 2621440 | tf_op jit(solution)/shard_map/reduce_scatter | solution.py:235
  53.3 35.7 %copy-start.7 = (s32[2,512]{1,0:T(2,128)S(1)}, s32[2,512]{1,0:T(2,128)}, u32[]{:S(2)}) copy-start(s32[2,512]{1,0:T(2,128)} %ids_ref.3) | copy-start | bytes 12292
  57.0 32.1 %copy-start = (bf16[512,2048]{1,0:T(8,128)(2,1)S(1)}, bf16[512,2048]{1,0:T(8,128)(2,1)}, u32[]{:S(2)}) copy-start(bf16[512,2048]{1,0:T(8,128)(2,1)} %all-gather.3.cloned.1.call-done.grad_ref) | copy-start | bytes 6291460
  89.1 1.2 copy-start.2
  128.6 45.4 %all-to-all-start.2 = ((bf16[64,40,128]{2,1,0:T(8,128)(2,1)}), bf16[64,40,128]{2,1,0:T(8,128)(2,1)S(1)}, u32[]{:S(2)}, u32[]{:S(2)}) async-start(bf16[64,40,128]{2,1,0:T(8,128)(2,1)} %get-tuple-element.15), calls=%async_computation.2 | async-start | bytes 1310720 | tf_op jit(solution)/shard_map/all_to_all | solution.py:234
  135.6 83.8 %reduce-scatter.5.cloned.1.call-start = ((), (), s32[]{:S(2)}) async-start(), calls=%async_computation.9 | async-start | bytes 557056 | tf_op jit(solution)/shard_map/reduce_scatter | solution.py:242
  180.8 83.5 %all-to-all-start.3 = ((bf16[64,32,384]{2,1,0:T(8,128)(2,1)}), bf16[64,32,384]{2,1,0:T(8,128)(2,1)S(1)}, u32[]{:S(2)}, u32[]{:S(2)}) async-start(bf16[64,32,384]{2,1,0:T(8,128)(2,1)} %attend_cluster.1), calls=%async_computation.3 | async-start | bytes 3145728 | tf_op jit(solution)/shard_map/all_to_all | solution.py:254
  219.3 0.8 copy-start.8
Sparse Core Ops, SparseCore 0:
  10.1 39.3 all-gather.2
  56.0 32.9 all-gather.4
  91.9 40.3 reduce-scatter.2
  139.1 80.1 reduce-scatter.4

commit v4 on v3

--- a/solution.py
+++ b/solution.py
@@ -10,6 +10,7 @@
 
 DH = 128
 CAP = 16
+PAIR = 2 * CAP + 2
 BLOCK = 256
 MASKED = -1e30
 SCALE = 1.0 / math.sqrt(DH)
@@ -56,17 +57,18 @@
 
 
 def cotangent_kernel(ids_ref, grad_ref, weight_ref, saved_ref, out_ref, place_ref):
-    owners = out_ref.shape[0]
+    sent = out_ref.shape[0]
+    owners = sent // PAIR
     ids = ids_ref[...]
     heads, tokens = ids.shape
-    slots = owners * CAP
     cot = jnp.dot(grad_ref[...], weight_ref[...], preferred_element_type=jnp.float32).astype(
         jnp.bfloat16
     )
-    slot_iota = lax.broadcasted_iota(jnp.int32, (slots, tokens), 0)
+    row_iota = lax.broadcasted_iota(jnp.int32, (sent, tokens), 0)
     lane = lax.broadcasted_iota(jnp.int32, (tokens, DH), 1)
     row8 = lax.broadcasted_iota(jnp.int32, (8, tokens), 0)
     meta = jnp.zeros((owners, DH), jnp.float32)
+    message = jnp.zeros((sent, DH), jnp.float32)
     places = pair_places(ids, owners)
     rank_rows = jnp.zeros((8, tokens), jnp.float32)
     place_rows = jnp.zeros((8, tokens), jnp.float32)
@@ -90,22 +92,34 @@
             spread.astype(jnp.bfloat16),
             preferred_element_type=jnp.float32,
         )
-        place = ids[h : h + 1, :] * CAP + rank.astype(jnp.int32)
-        select = jnp.where(slot_iota == place, 1.0, 0.0).astype(jnp.bfloat16)
-        rows = jnp.dot(select, g, preferred_element_type=jnp.float32).astype(jnp.bfloat16)
-        out_ref[:, h * CAP : (h + 1) * CAP, :] = rows.reshape(owners, CAP, DH)
+        place = ids[h : h + 1, :] * PAIR + h * CAP + rank.astype(jnp.int32)
+        select = jnp.where(row_iota == place, 1.0, 0.0).astype(jnp.bfloat16)
+        message = message + jnp.dot(select, g, preferred_element_type=jnp.float32)
     meta_lane = lax.broadcasted_iota(jnp.int32, (owners, DH), 1)
     meta = jnp.where((meta_lane & CAP) != 0, (1.0 - meta) * MASKED, meta)
-    first = lax.broadcasted_iota(jnp.int32, (owners, 8, DH), 1) == 0
-    out_ref[:, heads * CAP :, :] = jnp.where(first, meta[:, None, :], 0.0).astype(jnp.bfloat16)
+    meta_row = lax.broadcasted_iota(jnp.int32, (sent, owners), 1) * PAIR + heads * CAP
+    select = lax.broadcasted_iota(jnp.int32, (sent, owners), 0) == meta_row
+    message = message + jnp.dot(
+        jnp.where(select, 1.0, 0.0).astype(jnp.bfloat16),
+        meta.astype(jnp.bfloat16),
+        preferred_element_type=jnp.float32,
+    )
+    out_ref[...] = message.astype(jnp.bfloat16)
 
 
 def attend_kernel(qkv_ref, g_ref, out_ref, prob_ref, score_ref):
     owners = qkv_ref.shape[0]
     heads = qkv_ref.shape[1] // CAP
     slots = owners * CAP
-    meta = jnp.sum(g_ref[:, heads * CAP :, :].astype(jnp.float32), axis=1, keepdims=True)
-    meta = jnp.broadcast_to(meta, (owners, CAP, DH)).reshape(slots, DH)
+    meta = jnp.concatenate(
+        [
+            jnp.broadcast_to(
+                g_ref[first : first + 2, :].astype(jnp.float32)[:1], (CAP, DH)
+            )
+            for first in range(heads * CAP, owners * PAIR, PAIR)
+        ],
+        axis=0,
+    )
     lane = lax.broadcasted_iota(jnp.int32, (slots, DH), 1)
     rank = lax.broadcasted_iota(jnp.int32, (slots, DH), 0) & (CAP - 1)
     later = lax.broadcasted_iota(jnp.int32, (BLOCK, BLOCK), 0) > lax.broadcasted_iota(
@@ -114,12 +128,14 @@
     contract_last = (((1,), (1,)), ((), ()))
     contract_first = (((0,), (0,)), ((), ()))
 
-    def rows_of(ref, h, n):
-        return ref[:, h * CAP : (h + 1) * CAP, n * DH : (n + 1) * DH].reshape(slots, DH)
+    def rows_of(h, n):
+        return qkv_ref[:, h * CAP : (h + 1) * CAP, n * DH : (n + 1) * DH].reshape(slots, DH)
 
     for h in range(heads):
-        q, k, v = (rows_of(qkv_ref, h, n) for n in range(3))
-        g = rows_of(g_ref, h, 0)
+        q, k, v = (rows_of(h, n) for n in range(3))
+        g = jnp.concatenate(
+            [g_ref[n : n + CAP, :] for n in range(h * CAP, owners * PAIR, PAIR)], axis=0
+        )
         term_lanes = (lane >= 2 * CAP * h) & (lane < 2 * CAP * h + CAP)
         bias_lanes = (lane >= 2 * CAP * h + CAP) & (lane < 2 * CAP * (h + 1))
         own = jnp.where((lane & (CAP - 1)) == rank, meta, 0.0)
@@ -223,7 +239,7 @@
     cot, places = pl.pallas_call(
         cotangent_kernel,
         out_shape=(
-            shape((owners, heads * CAP + 8, DH), bf16),
+            shape((owners * PAIR, DH), bf16),
             shape((tokens, 8), jnp.int32),
         ),
         compiler_params=PARAMS,
@@ -231,7 +247,8 @@
     )(cluster_id, full_grad, weight, saved_output)
     share = jnp.einsum("tc,td->cd", full_grad, saved_output, preferred_element_type=jnp.float32)
     share = after(share, weight)
-    cot = lax.all_to_all(after(cot, (share, qkv)), SEQ, 0, 0, tiled=True)
+    cot = after(cot, (share, qkv)).reshape(owners * PAIR // 2, 2, DH)
+    cot = lax.all_to_all(cot, SEQ, 0, 0, tiled=True).reshape(owners * PAIR, DH)
     share = lax.psum_scatter(share, "x", scatter_dimension=0, tiled=True)
     weight_grad = pl.pallas_call(
         copy_kernel,

time: 274 us -> 269 us (0.982)
  waiting for transfers between devices: 194 us -> 187 us
    all_to_all x1, waiting for transfers between devices: 43.6 us -> 38.1 us  [local(): home = lax.all_to_all(grads, SEQ, 0, 0, tiled=True)]
    all_to_all x1, waiting for transfers between devices: 37.9 us -> 32.9 us  [local(): cot = lax.all_to_all(cot, SEQ, 0, 0, tiled=True).reshape(owners * PAIR, DH)]
    reduce_scatter x1, waiting for transfers between devices: 32.2 us -> 36.8 us  [local(): lax.psum_scatter(share, Z, scatter_dimension=0, tiled=True)]
  transfers between devices with their start and end apart: 8 -> 8, of which waited for: 6 -> 6; matrix products, arithmetic and copies ran while one was open for 2% -> 2% of each run, Pallas kernels for 5% -> 6%
where the time goes in v4:
time: 269 us; the launch traced here: 268 us
  waiting for transfers between devices  187 us (70%)
  starting transfers between devices  38.6 us (14%)
  Pallas kernels  17.7 us (7%)
  between operations  13.9 us (5%)
  local copies, waits for them, and re-layouts  6.97 us (3%)
  matrix products  3.64 us (1%)
    all_to_all x1, waiting for transfers between devices, local(): home = lax.all_to_all(grads, SEQ, 0, 0, tiled=True)  38.1 us
    reduce_scatter x1, waiting for transfers between devices, local(): lax.psum_scatter(share, Z, scatter_dimension=0, tiled=True)  36.8 us
    all_to_all x1, waiting for transfers between devices, local(): qkv = lax.all_to_all(after(qkv, weight_z), SEQ, 0, 0, tiled=True)  33.8 us
    all_to_all x1, waiting for transfers between devices, local(): cot = lax.all_to_all(cot, SEQ, 0, 0, tiled=True).reshape(owners * PAIR, DH)  32.9 us
    all_gather x1, waiting for transfers between devices, local(): weight = lax.all_gather(weight_z, 'x', axis=0, tiled=True)  32.1 us
    all_to_all x1, starting transfers between devices, copies_to_all(): lax.all_to_all(jnp.broadcast_to(block[None], (size, *block.shape)), axis,...  15.2 us
    all_to_all x1, waiting for transfers between devices, copies_to_all(): lax.all_to_all(jnp.broadcast_to(block[None], (size, *block.shape)), axis,...  11.7 us
    all_to_all x1, starting transfers between devices, local(): qkv = lax.all_to_all(after(qkv, weight_z), SEQ, 0, 0, tiled=True)  9.55 us
  transfers between devices with their start and end apart: 8, of which 6 were waited for; matrix products, arithmetic and copies ran while one was open for 2% of the time, Pallas kernels for 6%

profile of v4, /device:TPU:6, one launch (start us, length us, event | category | flops | bytes accessed | tf_op | source)
XLA Modules:
  0.0 267.9 jit_solution(1157151902835369249)
XLA Ops:
  7.2 0.7 all-gather.3.cloned.1.call-update
  7.9 1.4 broadcast_in_dim.2
  9.3 15.2 %all-to-all-start = ((bf16[16,32,256]{2,1,0:T(8,128)(2,1)}), bf16[16,32,256]{2,1,0:T(8,128)(2,1)S(1)}, u32[]{:S(2)}, u32[]{:S(2)}) async-start(bf16[16,32,256]{2,1,0:T(8,128)(2,1)} %broadcast_in_dim.2), calls=%async_computation | async-start | bytes 524288 | tf_op jit(solution)/shard_map/all_to_all | solution.py:209
  24.6 0.9 copy-done.3
  25.5 0.9 copy-done.4
  26.5 0.9 copy-done.5
  27.4 0.7 copy-done.6
  28.1 3.2 %pack_rows.1 = bf16[64,32,384]{2,1,0:T(8,128)(2,1)} custom-call(s32[2,512]{1,0:T(2,128)S(1)} %copy-done.6, bf16[512,256]{1,0:T(8,128)(2,1)S(1)} %copy-done.3, bf16[512,256]{1,0:T(8,128)(2,1)S(1)} %copy-done.4, bf16[512,256]{1,0:T(8,128)(2,1)S(1)} %copy-done.5), custom_call_target="tpu_custom_call" | custom-call | tf_op jit(solution)/shard_map/pack_rows/pallas_call | solution.py:231
  31.2 11.7 %all-to-all-done = bf16[16,32,256]{2,1,0:T(8,128)(2,1)S(1)} async-done(((bf16[16,32,256]{2,1,0:T(8,128)(2,1)}), bf16[16,32,256]{2,1,0:T(8,128)(2,1)S(1)}, u32[]{:S(2)}, u32[]{:S(2)}) %all-to-all-start) | async-done | bytes 262176 | tf_op jit(solution)/shard_map/all_to_all | solution.py:209
  42.9 9.6 %all-to-all-start.1 = ((bf16[64,32,384]{2,1,0:T(8,128)(2,1)}), bf16[64,32,384]{2,1,0:T(8,128)(2,1)}, u32[]{:S(2)}, u32[]{:S(2)}) async-start(bf16[64,32,384]{2,1,0:T(8,128)(2,1)} %pack_rows.1), calls=%async_computation.1 | async-start | bytes 3145728 | tf_op jit(solution)/shard_map/all_to_all | solution.py:237
  52.5 0.7 all-gather.5.cloned.1.call-update
  53.3 3.6 %fusion = f32[2048,256]{1,0:T(8,128)} fusion(bf16[512,2048]{1,0:T(8,128)(2,1)} %all-gather.3.cloned.1.call-done.grad_ref, bf16[512,256]{1,0:T(8,128)(2,1)S(1)} %copy-done.1), kind=kOutput, calls=%fused_computation | convolution fusion | flops 536870912 | bytes 4456448 | tf_op jit(solution)/shard_map/tc,td->cd/dot_general | solution.py:248
  57.0 32.1 %all-gather.5.cloned.1.call-done.weight_ref = bf16[2048,256]{1,0:T(8,128)(2,1)} async-done(((bf16[512,256]{1,0:T(8,128)(2,1)}), bf16[2048,256]{1,0:T(8,128)(2,1)}) %all-gather.5.cloned.1.call-update) | async-done | bytes 1048592 | tf_op jit(solution)/shard_map/all_gather | solution.py:229
  89.1 1.2 copy-done.2
  90.3 4.6 %cotangent_rows.1 = (bf16[2176,128]{1,0:T(8,128)(2,1)}, s32[512,8]{1,0:T(8,128)S(1)}) custom-call(s32[2,512]{1,0:T(2,128)S(1)} %copy-done.7, bf16[512,2048]{1,0:T(8,128)(2,1)S(1)} %copy-done, bf16[2048,256]{1,0:T(8,128)(2,1)S(1)} %copy-done.2, bf16[512,256]{1,0:T(8,128)(2,1)S(1)} %copy-done.1), custom_call_target="tpu_custom_call" | custom-call | tf_op jit(solution)/shard_map/cotangent_rows/pallas_call | solution.py:239
  94.8 33.8 %all-to-all-done.1.qkv_ref = bf16[64,32,384]{2,1,0:T(8,128)(2,1)} async-done(((bf16[64,32,384]{2,1,0:T(8,128)(2,1)}), bf16[64,32,384]{2,1,0:T(8,128)(2,1)}, u32[]{:S(2)}, u32[]{:S(2)}) %all-to-all-start.1) | async-done | bytes 1572896 | tf_op jit(solution)/shard_map/all_to_all | solution.py:237
  128.6 6.9 %all-to-all-start.2 = ((bf16[1088,2,128]{2,1,0:T(2,128)(2,1)}), bf16[1088,2,128]{2,1,0:T(2,128)(2,1)S(1)}, u32[]{:S(2)}, u32[]{:S(2)}) async-start(bf16[1088,2,128]{2,1,0:T(2,128)(2,1)} %bitcast.1), calls=%async_computation.2 | async-start | bytes 1114112 | tf_op jit(solution)/shard_map/all_to_all | solution.py:251
  136.1 32.9 %all-to-all-done.2 = bf16[1088,2,128]{2,1,0:T(2,128)(2,1)S(1)} async-done(((bf16[1088,2,128]{2,1,0:T(2,128)(2,1)}), bf16[1088,2,128]{2,1,0:T(2,128)(2,1)S(1)}, u32[]{:S(2)}, u32[]{:S(2)}) %all-to-all-start.2) | async-done | bytes 557088 | tf_op jit(solution)/shard_map/all_to_all | solution.py:251
  169.1 6.8 %attend_cluster.1 = bf16[64,32,384]{2,1,0:T(8,128)(2,1)} custom-call(bf16[64,32,384]{2,1,0:T(8,128)(2,1)} %all-to-all-done.1.qkv_ref, bf16[2176,128]{1,0:T(8,128)(2,1)S(1)} %bitcast.5), custom_call_target="tpu_custom_call" | custom-call | tf_op jit(solution)/shard_map/attend_cluster/pallas_call | solution.py:261
  175.9 6.6 %all-to-all-start.3 = ((bf16[64,32,384]{2,1,0:T(8,128)(2,1)}), bf16[64,32,384]{2,1,0:T(8,128)(2,1)S(1)}, u32[]{:S(2)}, u32[]{:S(2)}) async-start(bf16[64,32,384]{2,1,0:T(8,128)(2,1)} %attend_cluster.1), calls=%async_computation.3 | async-start | bytes 3145728 | tf_op jit(solution)/shard_map/all_to_all | solution.py:271
  182.5 36.8 %reduce-scatter.5.cloned.1.call-done.from_ref = f32[32,256]{1,0:T(8,128)} async-done(((f32[512,256]{1,0:T(8,128)}), f32[32,256]{1,0:T(8,128)}) %reduce-scatter.5.cloned.1.call-update) | async-done | bytes 32784 | tf_op jit(solution)/shard_map/reduce_scatter | solution.py:259
  219.3 0.8 copy-done.8
  220.6 38.1 %all-to-all-done.3.home_ref = bf16[64,32,384]{2,1,0:T(8,128)(2,1)S(1)} async-done(((bf16[64,32,384]{2,1,0:T(8,128)(2,1)}), bf16[64,32,384]{2,1,0:T(8,128)(2,1)S(1)}, u32[]{:S(2)}, u32[]{:S(2)}) %all-to-all-start.3) | async-done | bytes 1572896 | tf_op jit(solution)/shard_map/all_to_all | solution.py:271
  258.7 2.6 unpack_rows.1
  (23 shorter events, 1.4 us)
Async XLA Ops:
  7.2 46.1 %all-gather.3.cloned.1.call-start = ((), (), s32[]{:S(2)}) async-start(), calls=%async_computation.6 | async-start | bytes 2359296 | tf_op jit(solution)/shard_map/all_gather | solution.py:227
  9.3 33.6 %all-to-all-start = ((bf16[16,32,256]{2,1,0:T(8,128)(2,1)}), bf16[16,32,256]{2,1,0:T(8,128)(2,1)S(1)}, u32[]{:S(2)}, u32[]{:S(2)}) async-start(bf16[16,32,256]{2,1,0:T(8,128)(2,1)} %broadcast_in_dim.2), calls=%async_computation | async-start | bytes 524288 | tf_op jit(solution)/shard_map/all_to_all | solution.py:209
  24.5 1.0 copy-start.3
  25.5 0.9 copy-start.4
  26.5 0.9 copy-start.5
  27.4 0.7 copy-start.6
  31.2 22.1 %copy-start.1 = (bf16[512,256]{1,0:T(8,128)(2,1)S(1)}, bf16[512,256]{1,0:T(8,128)(2,1)}, u32[]{:S(2)}) copy-start(bf16[512,256]{1,0:T(8,128)(2,1)} %saved_ref.1) | copy-start | bytes 786436
  42.9 9.6 %copy-start.9 = (bf16[16,32,256]{2,1,0:T(8,128)(2,1)}, bf16[16,32,256]{2,1,0:T(8,128)(2,1)S(1)}, u32[]{:S(2)}) copy-start(bf16[16,32,256]{2,1,0:T(8,128)(2,1)S(1)} %all-to-all-done) | copy-start | bytes 786436
  42.9 85.7 %all-to-all-start.1 = ((bf16[64,32,384]{2,1,0:T(8,128)(2,1)}), bf16[64,32,384]{2,1,0:T(8,128)(2,1)}, u32[]{:S(2)}, u32[]{:S(2)}) async-start(bf16[64,32,384]{2,1,0:T(8,128)(2,1)} %pack_rows.1), calls=%async_computation.1 | async-start | bytes 3145728 | tf_op jit(solution)/shard_map/all_to_all | solution.py:237
  52.5 36.5 %all-gather.5.cloned.1.call-start = ((), (), s32[]{:S(2)}) async-start(), calls=%async_computation.7 | async-start | bytes 1310720 | tf_op jit(solution)/shard_map/all_gather | solution.py:229
  53.2 82.6 %reduce-scatter.3.cloned.1.call-start = ((), (), s32[]{:S(2)}) async-start(), calls=%async_computation.8 | async-start | bytes 2621440 | tf_op jit(solution)/shard_map/reduce_scatter | solution.py:252
  53.3 35.7 %copy-start.7 = (s32[2,512]{1,0:T(2,128)S(1)}, s32[2,512]{1,0:T(2,128)}, u32[]{:S(2)}) copy-start(s32[2,512]{1,0:T(2,128)} %ids_ref.3) | copy-start | bytes 12292
  57.0 32.1 %copy-start = (bf16[512,2048]{1,0:T(8,128)(2,1)S(1)}, bf16[512,2048]{1,0:T(8,128)(2,1)}, u32[]{:S(2)}) copy-start(bf16[512,2048]{1,0:T(8,128)(2,1)} %all-gather.3.cloned.1.call-done.grad_ref) | copy-start | bytes 6291460
  89.1 1.2 copy-start.2
  128.6 40.4 %all-to-all-start.2 = ((bf16[1088,2,128]{2,1,0:T(2,128)(2,1)}), bf16[1088,2,128]{2,1,0:T(2,128)(2,1)S(1)}, u32[]{:S(2)}, u32[]{:S(2)}) async-start(bf16[1088,2,128]{2,1,0:T(2,128)(2,1)} %bitcast.1), calls=%async_computation.2 | async-start | bytes 1114112 | tf_op jit(solution)/shard_map/all_to_all | solution.py:251
  135.6 83.7 %reduce-scatter.5.cloned.1.call-start = ((), (), s32[]{:S(2)}) async-start(), calls=%async_computation.9 | async-start | bytes 557056 | tf_op jit(solution)/shard_map/reduce_scatter | solution.py:259
  175.9 82.9 %all-to-all-start.3 = ((bf16[64,32,384]{2,1,0:T(8,128)(2,1)}), bf16[64,32,384]{2,1,0:T(8,128)(2,1)S(1)}, u32[]{:S(2)}, u32[]{:S(2)}) async-start(bf16[64,32,384]{2,1,0:T(8,128)(2,1)} %attend_cluster.1), calls=%async_computation.3 | async-start | bytes 3145728 | tf_op jit(solution)/shard_map/all_to_all | solution.py:271
  219.3 0.8 copy-start.8
Sparse Core Ops, SparseCore 0:
  10.1 39.3 all-gather.2
  56.0 32.9 all-gather.4
  91.9 40.3 reduce-scatter.2
  139.1 80.1 reduce-scatter.4

commit v5 on v4

--- a/solution.py
+++ b/solution.py
@@ -13,12 +13,14 @@
 PAIR = 2 * CAP + 2
 BLOCK = 256
 MASKED = -1e30
+CONTRACT_LAST = (((1,), (1,)), ((), ()))
+CONTRACT_FIRST = (((0,), (0,)), ((), ()))
 SCALE = 1.0 / math.sqrt(DH)
 LOG2_E = math.log2(math.e)
 Z = ("z_hi", "z_lo")
 SEQ = ("x", *Z)
 HEAD = ("y", "core")
-EARLY = pl.CostEstimate(flops=70_000_000_000, bytes_accessed=0, transcendentals=0)
+EARLY = pl.CostEstimate(flops=40_000_000_000, bytes_accessed=0, transcendentals=0)
 PARAMS = pltpu.CompilerParams(vmem_limit_bytes=24 * 1024 * 1024)
 
 
@@ -56,14 +58,48 @@
             )
 
 
-def cotangent_kernel(ids_ref, grad_ref, weight_ref, saved_ref, out_ref, place_ref):
+def block_of(here_ref, back, other):
+    y = lax.rem(here_ref[3] + 4 - back, 4)
+    return y, here_ref[4] + other - 2 * other * here_ref[4]
+
+
+def share_kernel(here_ref, saved_ref, *refs):
+    *pairs, out_ref = refs
+    half = saved_ref.shape[1]
+    depth = out_ref.shape[3]
+    for back, pair in enumerate(pairs):
+        for other in range(2):
+            x, core = block_of(here_ref, back, other)
+            share = lax.dot_general(
+                pair[other], saved_ref[...], CONTRACT_FIRST, preferred_element_type=jnp.float32
+            )
+            for n in range(half // depth):
+                ahead = [
+                    lax.rem(there + 4 - here_ref[axis], 4)
+                    for axis, there in ((0, x), (2, n % 4), (1, core * 2 + n // 4))
+                ]
+                out_ref[ahead[0], ahead[1], ahead[2]] = share[n * depth : (n + 1) * depth, :]
+
+
+def cotangent_kernel(here_ref, ids_ref, saved_ref, *refs):
+    *blocks, out_ref, place_ref, weight_ref = refs
+    parts, pairs = blocks[:4], blocks[4:]
     sent = out_ref.shape[0]
     owners = sent // PAIR
     ids = ids_ref[...]
     heads, tokens = ids.shape
-    cot = jnp.dot(grad_ref[...], weight_ref[...], preferred_element_type=jnp.float32).astype(
-        jnp.bfloat16
-    )
+    width = saved_ref.shape[1]
+    for back, part in enumerate(parts):
+        weight_ref[lax.rem(here_ref[0] + 4 - back, 4)] = part[...]
+    cot = jnp.zeros((tokens, width), jnp.float32)
+    for back, pair in enumerate(pairs):
+        for other in range(2):
+            x, core = block_of(here_ref, back, other)
+            rows = pl.ds(pl.multiple_of(core * width, width), width)
+            cot = cot + jnp.dot(
+                pair[other], weight_ref[x, rows, :], preferred_element_type=jnp.float32
+            )
+    cot = cot.astype(jnp.bfloat16)
     row_iota = lax.broadcasted_iota(jnp.int32, (sent, tokens), 0)
     lane = lax.broadcasted_iota(jnp.int32, (tokens, DH), 1)
     row8 = lax.broadcasted_iota(jnp.int32, (8, tokens), 0)
@@ -125,8 +161,6 @@
     later = lax.broadcasted_iota(jnp.int32, (BLOCK, BLOCK), 0) > lax.broadcasted_iota(
         jnp.int32, (BLOCK, BLOCK), 1
     )
-    contract_last = (((1,), (1,)), ((), ()))
-    contract_first = (((0,), (0,)), ((), ()))
 
     def rows_of(h, n):
         return qkv_ref[:, h * CAP : (h + 1) * CAP, n * DH : (n + 1) * DH].reshape(slots, DH)
@@ -150,7 +184,7 @@
         for start in range(0, slots, BLOCK):
             stop = start + BLOCK
             scores = lax.dot_general(
-                k_wide[:stop], q_wide[start:stop], contract_last,
+                k_wide[:stop], q_wide[start:stop], CONTRACT_LAST,
                 preferred_element_type=jnp.float32,
             )
             last = jnp.where(later, MASKED, scores[start:stop])
@@ -162,7 +196,7 @@
             exponent = jnp.exp2((scores - row_max) * (SCALE * LOG2_E))
             inverse = 1.0 / jnp.sum(exponent, axis=0, keepdims=True)
             grad_prob = lax.dot_general(
-                v_wide[:stop], g_wide[start:stop], contract_last,
+                v_wide[:stop], g_wide[start:stop], CONTRACT_LAST,
                 preferred_element_type=jnp.float32,
             )
             grad_score = (exponent * (inverse * SCALE) * grad_prob).astype(jnp.bfloat16)
@@ -185,8 +219,18 @@
                 ] = grad.astype(jnp.bfloat16).reshape(BLOCK // CAP, CAP, DH)
 
 
-def copy_kernel(from_ref, to_ref):
-    to_ref[...] = from_ref[...]
+def add_kernel(own_ref, *refs):
+    *others, sum_ref, sent_ref = refs
+    total = own_ref[...]
+    for ref in others:
+        total = total + ref[...].astype(jnp.float32)
+    sum_ref[...] = total[0]
+    sent_ref[...] = total.astype(jnp.bfloat16)
+
+
+def add_last_kernel(own_ref, *refs):
+    *others, sum_ref = refs
+    sum_ref[...] = own_ref[...] + sum(ref[...].astype(jnp.float32) for ref in others)
 
 
 def unpack_kernel(home_ref, place_ref, dq_ref, dk_ref, dv_ref):
@@ -211,6 +255,18 @@
     )
 
 
+def forward(block, axis, shift):
+    size = lax.axis_size(axis)
+    return lax.ppermute(block, axis, [(i, (i + shift) % size) for i in range(size)])
+
+
+def scatter_sum(blocks, axis):
+    total = blocks[0]
+    for n in range(1, lax.axis_size(axis)):
+        total = total + forward(blocks[n].astype(jnp.bfloat16), axis, n).astype(jnp.float32)
+    return total
+
+
 def after(value, earlier):
     return lax.optimization_barrier((value, earlier))[0]
 
@@ -224,39 +280,59 @@
     bf16 = jnp.bfloat16
     shape = jax.ShapeDtypeStruct
 
-    full_grad = lax.all_gather(output_grad, HEAD, axis=1, tiled=True)
+    smem, vmem = (pl.BlockSpec(memory_space=space) for space in (pltpu.SMEM, pltpu.VMEM))
+    here = jnp.stack([lax.axis_index(axis) for axis in (*SEQ, *HEAD)]).astype(jnp.int32)
+
     weight_z = copies_to_all(out_weight, Z).reshape(-1, width)
-    weight = lax.all_gather(weight_z, "x", axis=0, tiled=True)
-
     qkv = pl.pallas_call(
         pack_kernel,
         out_shape=shape((owners, heads * CAP, 3 * DH), bf16),
         compiler_params=PARAMS,
         name="pack_rows",
     )(cluster_id, query_rows, key_rows, value_rows)
-    qkv = lax.all_to_all(after(qkv, weight_z), SEQ, 0, 0, tiled=True)
-
+    pair = jnp.stack([output_grad, forward(output_grad, "core", 1)])
+    qkv = lax.all_to_all(after(qkv, (weight_z, pair)), SEQ, 0, 0, tiled=True)
+
+    pairs = [pair] + [forward(pair, "y", n) for n in range(1, lax.axis_size("y"))]
+    parts = [weight_z] + [forward(weight_z, "x", n) for n in range(1, lax.axis_size("x"))]
     cot, places = pl.pallas_call(
         cotangent_kernel,
         out_shape=(
             shape((owners * PAIR, DH), bf16),
             shape((tokens, 8), jnp.int32),
         ),
+        in_specs=[smem] + [vmem] * (2 + len(parts) + len(pairs)),
+        scratch_shapes=[pltpu.VMEM((len(parts), *weight_z.shape), bf16)],
         compiler_params=PARAMS,
         name="cotangent_rows",
-    )(cluster_id, full_grad, weight, saved_output)
-    share = jnp.einsum("tc,td->cd", full_grad, saved_output, preferred_element_type=jnp.float32)
-    share = after(share, weight)
-    cot = after(cot, (share, qkv)).reshape(owners * PAIR // 2, 2, DH)
+    )(here, cluster_id, saved_output, *parts, *pairs)
+    share = pl.pallas_call(
+        share_kernel,
+        out_shape=shape((4, 4, 4, out_weight.shape[0], width), jnp.float32),
+        in_specs=[smem] + [vmem] * (1 + len(pairs)),
+        compiler_params=PARAMS,
+        name="weight_share",
+    )(here, after(saved_output, places), *pairs)
+    share = scatter_sum(share, "x")
+    moved = [forward(share[n].astype(bf16), "z_lo", n) for n in range(1, 4)]
+    cot, own, qkv = lax.optimization_barrier((cot, share[0], qkv))
+    cot = cot.reshape(owners * PAIR // 2, 2, DH)
     cot = lax.all_to_all(cot, SEQ, 0, 0, tiled=True).reshape(owners * PAIR, DH)
-    share = lax.psum_scatter(share, "x", scatter_dimension=0, tiled=True)
+    own, share = pl.pallas_call(
+        add_kernel,
+        out_shape=(shape(own.shape[1:], jnp.float32), shape(own.shape, bf16)),
+        compiler_params=PARAMS,
+        cost_estimate=EARLY,
+        name="add_along_z_lo",
+    )(own, *moved)
+    moved = [forward(share[n], "z_hi", n) for n in range(1, 4)]
     weight_grad = pl.pallas_call(
-        copy_kernel,
-        out_shape=shape(out_weight.shape, jnp.float32),
-        compiler_params=PARAMS,
-        cost_estimate=EARLY,
-        name="weight_grad",
-    )(lax.psum_scatter(share, Z, scatter_dimension=0, tiled=True))
+        add_last_kernel,
+        out_shape=shape(own.shape, jnp.float32),
+        compiler_params=PARAMS,
+        cost_estimate=pl.CostEstimate(flops=50_000_000_000, bytes_accessed=0, transcendentals=0),
+        name="add_along_z_hi",
+    )(own, *moved)
 
     grads = pl.pallas_call(
         attend_kernel,

time: 269 us -> 258 us (0.959)
  starting transfers between devices: 38.6 us -> 102 us
  waiting for transfers between devices: 187 us -> 126 us
  between operations: 13.9 us -> 0.93 us
  matrix products: 3.64 us -> 0 us
    ppermute x0 -> x16, waiting for transfers between devices: none -> 82.9 us  [forward(): lax.ppermute(block, axis, [(i, (i + shift) % size) for i in range(size)])]
    ppermute x0 -> x16, starting transfers between devices: none -> 61.4 us  [forward(): lax.ppermute(block, axis, [(i, (i + shift) % size) for i in range(size)])]
    all_to_all x1, waiting for transfers between devices: 38.1 us -> 0.01 us  [local(): home = lax.all_to_all(grads, SEQ, 0, 0, tiled=True)]
    reduce_scatter x2 -> x0, waiting for transfers between devices: 36.8 us -> none  [the longest x1 36.8 us: local(): lax.psum_scatter(share, Z, scatter_dimension=0, tiled=True)]
    all_gather x2 -> x0, waiting for transfers between devices: 32.1 us -> none  [the longest x1 32.1 us: local(): weight = lax.all_gather(weight_z, 'x', axis=0, tiled=True)]
    all_to_all x1, waiting for transfers between devices: 33.8 us -> 9.67 us  [local(): qkv = lax.all_to_all(after(qkv, (weight_z, pair)), SEQ, 0, 0, tiled=True)]
    all_to_all x1, waiting for transfers between devices: 32.9 us -> 23.5 us  [local(): cot = lax.all_to_all(cot, SEQ, 0, 0, tiled=True).reshape(owners * PAIR, DH)]
    dot_general x1 -> x0, matrix products: 3.64 us -> none  [local(): jnp.einsum('tc,td->cd', full_grad, saved_output, preferred_element_type=j...]
  transfers between devices with their start and end apart: 8 -> 20, of which waited for: 6 -> 10; matrix products, arithmetic and copies ran while one was open for 2% -> 0% of each run, Pallas kernels for 6% -> 7%
where the time goes in v5:
time: 258 us; the launch traced here: 256 us
  waiting for transfers between devices  126 us (49%)
  starting transfers between devices  102 us (40%)
  Pallas kernels  19.6 us (8%)
  local copies, waits for them, and re-layouts  7.91 us (3%)
    ppermute x16, waiting for transfers between devices, forward(): lax.ppermute(block, axis, [(i, (i + shift) % size) for i in range(size)])  82.9 us
    ppermute x16, starting transfers between devices, forward(): lax.ppermute(block, axis, [(i, (i + shift) % size) for i in range(size)])  61.4 us
    all_to_all x1, waiting for transfers between devices, local(): cot = lax.all_to_all(cot, SEQ, 0, 0, tiled=True).reshape(owners * PAIR, DH)  23.5 us
    all_to_all x1, starting transfers between devices, copies_to_all(): lax.all_to_all(jnp.broadcast_to(block[None], (size, *block.shape)), axis,...  15.2 us
    all_to_all x1, waiting for transfers between devices, local(): qkv = lax.all_to_all(after(qkv, (weight_z, pair)), SEQ, 0, 0, tiled=True)  9.67 us
    all_to_all x1, waiting for transfers between devices, copies_to_all(): lax.all_to_all(jnp.broadcast_to(block[None], (size, *block.shape)), axis,...  9.63 us
    all_to_all x1, starting transfers between devices, local(): qkv = lax.all_to_all(after(qkv, (weight_z, pair)), SEQ, 0, 0, tiled=True)  9.52 us
    all_to_all x1, starting transfers between devices, local(): home = lax.all_to_all(grads, SEQ, 0, 0, tiled=True)  8.69 us
  transfers between devices with their start and end apart: 20, of which 10 were waited for; matrix products, arithmetic and copies ran while one was open for 0% of the time, Pallas kernels for 7%

profile of v5, /device:TPU:6, one launch (start us, length us, event | category | flops | bytes accessed | tf_op | source)
XLA Modules:
  0.0 256.2 jit_solution(3865595093719018746)
XLA Ops:
  2.1 15.2 %all-to-all-start = ((bf16[16,32,256]{2,1,0:T(8,128)(2,1)}), bf16[16,32,256]{2,1,0:T(8,128)(2,1)S(1)}, u32[]{:S(2)}, u32[]{:S(2)}) async-start(bf16[16,32,256]{2,1,0:T(8,128)(2,1)} %broadcast_in_dim.2), calls=%async_computation | async-start | bytes 524288 | tf_op jit(solution)/shard_map/all_to_all | solution.py:253
  22.8 3.2 %pack_rows.1 = bf16[64,32,384]{2,1,0:T(8,128)(2,1)} custom-call(s32[2,512]{1,0:T(2,128)S(1)} %copy-done.8, bf16[512,256]{1,0:T(8,128)(2,1)S(1)} %copy-done.3, bf16[512,256]{1,0:T(8,128)(2,1)S(1)} %copy-done.4, bf16[512,256]{1,0:T(8,128)(2,1)S(1)} %copy-done.5), custom_call_target="tpu_custom_call" | custom-call | tf_op jit(solution)/shard_map/pack_rows/pallas_call | solution.py:287
  26.1 9.6 %all-to-all-done = bf16[16,32,256]{2,1,0:T(8,128)(2,1)S(1)} async-done(((bf16[16,32,256]{2,1,0:T(8,128)(2,1)}), bf16[16,32,256]{2,1,0:T(8,128)(2,1)S(1)}, u32[]{:S(2)}, u32[]{:S(2)}) %all-to-all-start) | async-done | bytes 262176 | tf_op jit(solution)/shard_map/all_to_all | solution.py:253
  36.4 9.5 %all-to-all-start.1 = ((bf16[64,32,384]{2,1,0:T(8,128)(2,1)}), bf16[64,32,384]{2,1,0:T(8,128)(2,1)S(1)}, u32[]{:S(2)}, u32[]{:S(2)}) async-start(bf16[64,32,384]{2,1,0:T(8,128)(2,1)} %pack_rows.1), calls=%async_computation.1 | async-start | bytes 3145728 | tf_op jit(solution)/shard_map/all_to_all | solution.py:294
  45.9 4.9 %collective-permute-start.6 = (bf16[2,512,256]{2,1,0:T(8,128)(2,1)S(1)}, bf16[2,512,256]{2,1,0:T(8,128)(2,1)S(1)}, u32[]{:S(2)}, u32[]{:S(2)}) collective-permute-start(bf16[2,512,256]{2,1,0:T(8,128)(2,1)S(1)} %pad_maximum_fusion.refs_4_.refs_0_), channel_id=1, source_target_pairs={{0,6},{2,0},{4,2},{6,4},{1,7},{3,1},{5,3},{7,5},{8,14},{10,8},{12,... | collective-permute-start | bytes 1572872 | tf_op jit(solution)/shard_map/ppermute | solution.py:260
  61.8 10.8 %collective-permute-done.6.refs_7_.refs_3_ = bf16[2,512,256]{2,1,0:T(8,128)(2,1)S(1)} collective-permute-done((bf16[2,512,256]{2,1,0:T(8,128)(2,1)S(1)}, bf16[2,512,256]{2,1,0:T(8,128)(2,1)S(1)}, u32[]{:S(2)}, u32[]{:S(2)}) %collective-permute-start.6) | collective-permute-done | bytes 524320 | tf_op jit(solution)/shard_map/ppermute | solution.py:260
  75.2 3.2 %collective-permute-done.4.refs_5_.refs_1_ = bf16[2,512,256]{2,1,0:T(8,128)(2,1)} collective-permute-done((bf16[2,512,256]{2,1,0:T(8,128)(2,1)S(1)}, bf16[2,512,256]{2,1,0:T(8,128)(2,1)}, u32[]{:S(2)}, u32[]{:S(2)}) %collective-permute-start.4) | collective-permute-done | bytes 524320 | tf_op jit(solution)/shard_map/ppermute | solution.py:260
  78.4 3.4 %collective-permute-done.refs_1_ = bf16[512,256]{1,0:T(8,128)(2,1)} collective-permute-done((bf16[512,256]{1,0:T(8,128)(2,1)}, bf16[512,256]{1,0:T(8,128)(2,1)}, u32[]{:S(2)}, u32[]{:S(2)}) %collective-permute-start) | collective-permute-done | bytes 262176 | tf_op jit(solution)/shard_map/ppermute | solution.py:260
  82.7 5.9 %cotangent_rows.1 = (bf16[2176,128]{1,0:T(8,128)(2,1)}, s32[512,8]{1,0:T(8,128)S(1)}) custom-call(s32[5]{0:T(128)S(1)} %stack.32.here_ref, s32[2,512]{1,0:T(2,128)S(1)} %copy-done.9, bf16[512,256]{1,0:T(8,128)(2,1)S(1)} %copy-done, bf16[512,256]{1,0:T(8,128)(2,1)S(1)} %bitcast.43, bf16[512,256]{1,0:T(8,128)(2,1)} %collective-permute-done.refs_1_, ...), custom_call_target="tpu_custom_call" | custom-call | tf_op jit(solution)/shard_map/cotangent_rows/pallas_call | solution.py:298
  91.4 3.7 %collective-permute-start.7 = (bf16[4,4,32,256]{3,2,1,0:T(8,128)(2,1)S(1)}, bf16[4,4,32,256]{3,2,1,0:T(8,128)(2,1)S(1)}, u32[]{:S(2)}, u32[]{:S(2)}) collective-permute-start(bf16[4,4,32,256]{3,2,1,0:T(8,128)(2,1)S(1)} %get-tuple-element.30), channel_id=1, source_target_pairs={{0,128},{128,256},{256,384},{384,0},{1,129},{129,257},{257,385},{3... | collective-permute-start | bytes 786440 | tf_op jit(solution)/shard_map/ppermute | solution.py:260
  97.2 3.1 %collective-permute-start.8 = (bf16[4,4,32,256]{3,2,1,0:T(8,128)(2,1)S(1)}, bf16[4,4,32,256]{3,2,1,0:T(8,128)(2,1)S(1)}, u32[]{:S(2)}, u32[]{:S(2)}) collective-permute-start(bf16[4,4,32,256]{3,2,1,0:T(8,128)(2,1)S(1)} %get-tuple-element.32), channel_id=1, source_target_pairs={{0,256},{128,384},{256,0},{384,128},{1,257},{129,385},{257,1},{385... | collective-permute-start | bytes 786440 | tf_op jit(solution)/shard_map/ppermute | solution.py:260
  103.3 8.8 %collective-permute-done.9 = bf16[4,4,32,256]{3,2,1,0:T(8,128)(2,1)S(1)} collective-permute-done((bf16[4,4,32,256]{3,2,1,0:T(8,128)(2,1)S(1)}, bf16[4,4,32,256]{3,2,1,0:T(8,128)(2,1)S(1)}, u32[]{:S(2)}, u32[]{:S(2)}) %collective-permute-start.9) | collective-permute-done | bytes 262176 | tf_op jit(solution)/shard_map/ppermute | solution.py:260
  112.3 9.7 %all-to-all-done.1.qkv_ref = bf16[64,32,384]{2,1,0:T(8,128)(2,1)S(1)} async-done(((bf16[64,32,384]{2,1,0:T(8,128)(2,1)}), bf16[64,32,384]{2,1,0:T(8,128)(2,1)S(1)}, u32[]{:S(2)}, u32[]{:S(2)}) %all-to-all-start.1) | async-done | bytes 1572896 | tf_op jit(solution)/shard_map/all_to_all | solution.py:294
  122.0 7.0 %all-to-all-start.2 = ((bf16[1088,2,128]{2,1,0:T(2,128)(2,1)}), bf16[1088,2,128]{2,1,0:T(2,128)(2,1)S(1)}, u32[]{:S(2)}, u32[]{:S(2)}) async-start(bf16[1088,2,128]{2,1,0:T(2,128)(2,1)} %bitcast.13), calls=%async_computation.2 | async-start | bytes 1114112 | tf_op jit(solution)/shard_map/all_to_all | solution.py:320
  129.0 5.2 %collective-permute-start.12 = (bf16[4,32,256]{2,1,0:T(8,128)(2,1)S(1)}, bf16[4,32,256]{2,1,0:T(8,128)(2,1)S(1)}, u32[]{:S(2)}, u32[]{:S(2)}) collective-permute-start(bf16[4,32,256]{2,1,0:T(8,128)(2,1)S(1)} %get-tuple-element.33), channel_id=1, source_target_pairs={{0,24},{8,0},{16,8},{24,16},{1,25},{9,1},{17,9},{25,17},{2,26},{10... | collective-permute-start | bytes 196616 | tf_op jit(solution)/shard_map/ppermute | solution.py:260
  136.1 3.2 %collective-permute-start.10 = (bf16[4,32,256]{2,1,0:T(8,128)(2,1)S(1)}, bf16[4,32,256]{2,1,0:T(8,128)(2,1)S(1)}, u32[]{:S(2)}, u32[]{:S(2)}) collective-permute-start(bf16[4,32,256]{2,1,0:T(8,128)(2,1)S(1)} %get-tuple-element.35), channel_id=1, source_target_pairs={{0,8},{8,16},{16,24},{24,0},{1,9},{9,17},{17,25},{25,1},{2,10},{10... | collective-permute-start | bytes 196616 | tf_op jit(solution)/shard_map/ppermute | solution.py:260
  139.3 23.5 %all-to-all-done.2 = bf16[1088,2,128]{2,1,0:T(2,128)(2,1)S(1)} async-done(((bf16[1088,2,128]{2,1,0:T(2,128)(2,1)}), bf16[1088,2,128]{2,1,0:T(2,128)(2,1)S(1)}, u32[]{:S(2)}, u32[]{:S(2)}) %all-to-all-start.2) | async-done | bytes 557088 | tf_op jit(solution)/shard_map/all_to_all | solution.py:320
  162.9 5.4 %attend_cluster.1 = bf16[64,32,384]{2,1,0:T(8,128)(2,1)} custom-call(bf16[64,32,384]{2,1,0:T(8,128)(2,1)S(1)} %all-to-all-done.1.qkv_ref, bf16[2176,128]{1,0:T(8,128)(2,1)S(1)} %bitcast.39), custom_call_target="tpu_custom_call" | custom-call | tf_op jit(solution)/shard_map/attend_cluster/pallas_call | solution.py:337
  168.2 8.7 %all-to-all-start.3 = ((bf16[64,32,384]{2,1,0:T(8,128)(2,1)}), bf16[64,32,384]{2,1,0:T(8,128)(2,1)S(1)}, u32[]{:S(2)}, u32[]{:S(2)}) async-start(bf16[64,32,384]{2,1,0:T(8,128)(2,1)} %attend_cluster.1), calls=%async_computation.3 | async-start | bytes 3145728 | tf_op jit(solution)/shard_map/all_to_all | solution.py:347
  177.0 7.4 %collective-permute-start.15 = (bf16[32,256]{1,0:T(8,128)(2,1)S(1)}, bf16[32,256]{1,0:T(8,128)(2,1)S(1)}, u32[]{:S(2)}, u32[]{:S(2)}) collective-permute-start(bf16[32,256]{1,0:T(8,128)(2,1)S(1)} %get-tuple-element.36), channel_id=1, source_target_pairs={{0,96},{32,0},{64,32},{96,64},{1,97},{33,1},{65,33},{97,65},{2,98}... | collective-permute-start | bytes 49160 | tf_op jit(solution)/shard_map/ppermute | solution.py:260
  184.4 7.2 %collective-permute-start.14 = (bf16[32,256]{1,0:T(8,128)(2,1)S(1)}, bf16[32,256]{1,0:T(8,128)(2,1)S(1)}, u32[]{:S(2)}, u32[]{:S(2)}) collective-permute-start(bf16[32,256]{1,0:T(8,128)(2,1)S(1)} %get-tuple-element.37), channel_id=1, source_target_pairs={{0,64},{32,96},{64,0},{96,32},{1,65},{33,97},{65,1},{97,33},{2,66}... | collective-permute-start | bytes 49160 | tf_op jit(solution)/shard_map/ppermute | solution.py:260
  191.6 7.3 %collective-permute-start.13 = (bf16[32,256]{1,0:T(8,128)(2,1)S(1)}, bf16[32,256]{1,0:T(8,128)(2,1)S(1)}, u32[]{:S(2)}, u32[]{:S(2)}) collective-permute-start(bf16[32,256]{1,0:T(8,128)(2,1)S(1)} %get-tuple-element.38), channel_id=1, source_target_pairs={{0,32},{32,64},{64,96},{96,0},{1,33},{33,65},{65,97},{97,1},{2,34}... | collective-permute-start | bytes 49160 | tf_op jit(solution)/shard_map/ppermute | solution.py:260
  198.9 47.8 %collective-permute-done.15.refs_2_ = bf16[32,256]{1,0:T(8,128)(2,1)S(1)} collective-permute-done((bf16[32,256]{1,0:T(8,128)(2,1)S(1)}, bf16[32,256]{1,0:T(8,128)(2,1)S(1)}, u32[]{:S(2)}, u32[]{:S(2)}) %collective-permute-start.15) | collective-permute-done | bytes 16416 | tf_op jit(solution)/shard_map/ppermute | solution.py:260
  246.8 5.9 %collective-permute-done.14.refs_1_ = bf16[32,256]{1,0:T(8,128)(2,1)S(1)} collective-permute-done((bf16[32,256]{1,0:T(8,128)(2,1)S(1)}, bf16[32,256]{1,0:T(8,128)(2,1)S(1)}, u32[]{:S(2)}, u32[]{:S(2)}) %collective-permute-start.14) | collective-permute-done | bytes 16416 | tf_op jit(solution)/shard_map/ppermute | solution.py:260
  (54 shorter events, 35.7 us)
Async XLA Ops:
  0.6 25.4 %copy-start.10 = (bf16[512,256]{1,0:T(8,128)(2,1)S(1)}, bf16[512,256]{1,0:T(8,128)(2,1)}, u32[]{:S(2)}) copy-start(bf16[512,256]{1,0:T(8,128)(2,1)} %param.12) | copy-start | bytes 786436
  2.1 33.6 %all-to-all-start = ((bf16[16,32,256]{2,1,0:T(8,128)(2,1)}), bf16[16,32,256]{2,1,0:T(8,128)(2,1)S(1)}, u32[]{:S(2)}, u32[]{:S(2)}) async-start(bf16[16,32,256]{2,1,0:T(8,128)(2,1)} %broadcast_in_dim.2), calls=%async_computation | async-start | bytes 524288 | tf_op jit(solution)/shard_map/all_to_all | solution.py:253
  17.3 8.7 %collective-permute-start.3 = (bf16[512,256]{1,0:T(8,128)(2,1)}, bf16[512,256]{1,0:T(8,128)(2,1)S(1)}, u32[]{:S(2)}, u32[]{:S(2)}) collective-permute-start(bf16[512,256]{1,0:T(8,128)(2,1)} %param.12), channel_id=1, source_target_pairs={{0,1},{1,0},{2,3},{3,2},{4,5},{5,4},{6,7},{7,6},{8,9},{9,8},{10,11... | collective-permute-start | bytes 786440 | tf_op jit(solution)/shard_map/ppermute | solution.py:260
  36.4 45.4 %copy-start = (bf16[512,256]{1,0:T(8,128)(2,1)S(1)}, bf16[512,256]{1,0:T(8,128)(2,1)}, u32[]{:S(2)}) copy-start(bf16[512,256]{1,0:T(8,128)(2,1)} %saved_ref.2) | copy-start | bytes 786436
  36.4 45.4 %copy-start.9 = (s32[2,512]{1,0:T(2,128)S(1)}, s32[2,512]{1,0:T(2,128)}, u32[]{:S(2)}) copy-start(s32[2,512]{1,0:T(2,128)} %ids_ref.3) | copy-start | bytes 12292
  36.4 85.6 %all-to-all-start.1 = ((bf16[64,32,384]{2,1,0:T(8,128)(2,1)}), bf16[64,32,384]{2,1,0:T(8,128)(2,1)S(1)}, u32[]{:S(2)}, u32[]{:S(2)}) async-start(bf16[64,32,384]{2,1,0:T(8,128)(2,1)} %pack_rows.1), calls=%async_computation.1 | async-start | bytes 3145728 | tf_op jit(solution)/shard_map/all_to_all | solution.py:294
  45.9 26.7 %collective-permute-start.6 = (bf16[2,512,256]{2,1,0:T(8,128)(2,1)S(1)}, bf16[2,512,256]{2,1,0:T(8,128)(2,1)S(1)}, u32[]{:S(2)}, u32[]{:S(2)}) collective-permute-start(bf16[2,512,256]{2,1,0:T(8,128)(2,1)S(1)} %pad_maximum_fusion.refs_4_.refs_0_), channel_id=1, source_target_pairs={{0,6},{2,0},{4,2},{6,4},{1,7},{3,1},{5,3},{7,5},{8,14},{10,8},{12,... | collective-permute-start | bytes 1572872 | tf_op jit(solution)/shard_map/ppermute | solution.py:260
  50.9 24.3 %collective-permute-start.5 = (bf16[2,512,256]{2,1,0:T(8,128)(2,1)S(1)}, bf16[2,512,256]{2,1,0:T(8,128)(2,1)S(1)}, u32[]{:S(2)}, u32[]{:S(2)}) collective-permute-start(bf16[2,512,256]{2,1,0:T(8,128)(2,1)S(1)} %pad_maximum_fusion.refs_4_.refs_0_), channel_id=1, source_target_pairs={{0,4},{2,6},{4,0},{6,2},{1,5},{3,7},{5,1},{7,3},{8,12},{10,14},{12... | collective-permute-start | bytes 1572872 | tf_op jit(solution)/shard_map/ppermute | solution.py:260
  53.4 25.0 %collective-permute-start.4 = (bf16[2,512,256]{2,1,0:T(8,128)(2,1)S(1)}, bf16[2,512,256]{2,1,0:T(8,128)(2,1)}, u32[]{:S(2)}, u32[]{:S(2)}) collective-permute-start(bf16[2,512,256]{2,1,0:T(8,128)(2,1)S(1)} %pad_maximum_fusion.refs_4_.refs_0_), channel_id=1, source_target_pairs={{0,2},{2,4},{4,6},{6,0},{1,3},{3,5},{5,7},{7,1},{8,10},{10,12},{12... | collective-permute-start | bytes 1572872 | tf_op jit(solution)/shard_map/ppermute | solution.py:260
  56.3 22.1 %collective-permute-start.2 = (bf16[512,256]{1,0:T(8,128)(2,1)}, bf16[512,256]{1,0:T(8,128)(2,1)}, u32[]{:S(2)}, u32[]{:S(2)}) collective-permute-start(bf16[512,256]{1,0:T(8,128)(2,1)} %bitcast.40), channel_id=1, source_target_pairs={{0,384},{128,0},{256,128},{384,256},{1,385},{129,1},{257,129},{385... | collective-permute-start | bytes 786440 | tf_op jit(solution)/shard_map/ppermute | solution.py:260
  59.0 19.4 %collective-permute-start.1 = (bf16[512,256]{1,0:T(8,128)(2,1)}, bf16[512,256]{1,0:T(8,128)(2,1)}, u32[]{:S(2)}, u32[]{:S(2)}) collective-permute-start(bf16[512,256]{1,0:T(8,128)(2,1)} %bitcast.41), channel_id=1, source_target_pairs={{0,256},{128,384},{256,0},{384,128},{1,257},{129,385},{257,1},{385... | collective-permute-start | bytes 786440 | tf_op jit(solution)/shard_map/ppermute | solution.py:260
  72.6 9.1 %collective-permute-start = (bf16[512,256]{1,0:T(8,128)(2,1)}, bf16[512,256]{1,0:T(8,128)(2,1)}, u32[]{:S(2)}, u32[]{:S(2)}) collective-permute-start(bf16[512,256]{1,0:T(8,128)(2,1)} %bitcast.42), channel_id=1, source_target_pairs={{0,128},{128,256},{256,384},{384,0},{1,129},{129,257},{257,385},{3... | collective-permute-start | bytes 786440 | tf_op jit(solution)/shard_map/ppermute | solution.py:260
  91.4 12.0 %collective-permute-start.7 = (bf16[4,4,32,256]{3,2,1,0:T(8,128)(2,1)S(1)}, bf16[4,4,32,256]{3,2,1,0:T(8,128)(2,1)S(1)}, u32[]{:S(2)}, u32[]{:S(2)}) collective-permute-start(bf16[4,4,32,256]{3,2,1,0:T(8,128)(2,1)S(1)} %get-tuple-element.30), channel_id=1, source_target_pairs={{0,128},{128,256},{256,384},{384,0},{1,129},{129,257},{257,385},{3... | collective-permute-start | bytes 786440 | tf_op jit(solution)/shard_map/ppermute | solution.py:260
  95.1 17.1 %collective-permute-start.9 = (bf16[4,4,32,256]{3,2,1,0:T(8,128)(2,1)S(1)}, bf16[4,4,32,256]{3,2,1,0:T(8,128)(2,1)S(1)}, u32[]{:S(2)}, u32[]{:S(2)}) collective-permute-start(bf16[4,4,32,256]{3,2,1,0:T(8,128)(2,1)S(1)} %get-tuple-element.31), channel_id=1, source_target_pairs={{0,384},{128,0},{256,128},{384,256},{1,385},{129,1},{257,129},{385... | collective-permute-start | bytes 786440 | tf_op jit(solution)/shard_map/ppermute | solution.py:260
  97.2 14.9 %collective-permute-start.8 = (bf16[4,4,32,256]{3,2,1,0:T(8,128)(2,1)S(1)}, bf16[4,4,32,256]{3,2,1,0:T(8,128)(2,1)S(1)}, u32[]{:S(2)}, u32[]{:S(2)}) collective-permute-start(bf16[4,4,32,256]{3,2,1,0:T(8,128)(2,1)S(1)} %get-tuple-element.32), channel_id=1, source_target_pairs={{0,256},{128,384},{256,0},{384,128},{1,257},{129,385},{257,1},{385... | collective-permute-start | bytes 786440 | tf_op jit(solution)/shard_map/ppermute | solution.py:260
  122.0 40.9 %all-to-all-start.2 = ((bf16[1088,2,128]{2,1,0:T(2,128)(2,1)}), bf16[1088,2,128]{2,1,0:T(2,128)(2,1)S(1)}, u32[]{:S(2)}, u32[]{:S(2)}) async-start(bf16[1088,2,128]{2,1,0:T(2,128)(2,1)} %bitcast.13), calls=%async_computation.2 | async-start | bytes 1114112 | tf_op jit(solution)/shard_map/all_to_all | solution.py:320
  129.0 47.9 %collective-permute-start.12 = (bf16[4,32,256]{2,1,0:T(8,128)(2,1)S(1)}, bf16[4,32,256]{2,1,0:T(8,128)(2,1)S(1)}, u32[]{:S(2)}, u32[]{:S(2)}) collective-permute-start(bf16[4,32,256]{2,1,0:T(8,128)(2,1)S(1)} %get-tuple-element.33), channel_id=1, source_target_pairs={{0,24},{8,0},{16,8},{24,16},{1,25},{9,1},{17,9},{25,17},{2,26},{10... | collective-permute-start | bytes 196616 | tf_op jit(solution)/shard_map/ppermute | solution.py:260
  134.2 42.8 %collective-permute-start.11 = (bf16[4,32,256]{2,1,0:T(8,128)(2,1)S(1)}, bf16[4,32,256]{2,1,0:T(8,128)(2,1)S(1)}, u32[]{:S(2)}, u32[]{:S(2)}) collective-permute-start(bf16[4,32,256]{2,1,0:T(8,128)(2,1)S(1)} %get-tuple-element.34), channel_id=1, source_target_pairs={{0,16},{8,24},{16,0},{24,8},{1,17},{9,25},{17,1},{25,9},{2,18},{10... | collective-permute-start | bytes 196616 | tf_op jit(solution)/shard_map/ppermute | solution.py:260
  136.1 40.8 %collective-permute-start.10 = (bf16[4,32,256]{2,1,0:T(8,128)(2,1)S(1)}, bf16[4,32,256]{2,1,0:T(8,128)(2,1)S(1)}, u32[]{:S(2)}, u32[]{:S(2)}) collective-permute-start(bf16[4,32,256]{2,1,0:T(8,128)(2,1)S(1)} %get-tuple-element.35), channel_id=1, source_target_pairs={{0,8},{8,16},{16,24},{24,0},{1,9},{9,17},{17,25},{25,1},{2,10},{10... | collective-permute-start | bytes 196616 | tf_op jit(solution)/shard_map/ppermute | solution.py:260
  168.2 85.0 %all-to-all-start.3 = ((bf16[64,32,384]{2,1,0:T(8,128)(2,1)}), bf16[64,32,384]{2,1,0:T(8,128)(2,1)S(1)}, u32[]{:S(2)}, u32[]{:S(2)}) async-start(bf16[64,32,384]{2,1,0:T(8,128)(2,1)} %attend_cluster.1), calls=%async_computation.3 | async-start | bytes 3145728 | tf_op jit(solution)/shard_map/all_to_all | solution.py:347
  177.0 69.7 %collective-permute-start.15 = (bf16[32,256]{1,0:T(8,128)(2,1)S(1)}, bf16[32,256]{1,0:T(8,128)(2,1)S(1)}, u32[]{:S(2)}, u32[]{:S(2)}) collective-permute-start(bf16[32,256]{1,0:T(8,128)(2,1)S(1)} %get-tuple-element.36), channel_id=1, source_target_pairs={{0,96},{32,0},{64,32},{96,64},{1,97},{33,1},{65,33},{97,65},{2,98}... | collective-permute-start | bytes 49160 | tf_op jit(solution)/shard_map/ppermute | solution.py:260
  184.4 68.2 %collective-permute-start.14 = (bf16[32,256]{1,0:T(8,128)(2,1)S(1)}, bf16[32,256]{1,0:T(8,128)(2,1)S(1)}, u32[]{:S(2)}, u32[]{:S(2)}) collective-permute-start(bf16[32,256]{1,0:T(8,128)(2,1)S(1)} %get-tuple-element.37), channel_id=1, source_target_pairs={{0,64},{32,96},{64,0},{96,32},{1,65},{33,97},{65,1},{97,33},{2,66}... | collective-permute-start | bytes 49160 | tf_op jit(solution)/shard_map/ppermute | solution.py:260
  191.6 61.0 %collective-permute-start.13 = (bf16[32,256]{1,0:T(8,128)(2,1)S(1)}, bf16[32,256]{1,0:T(8,128)(2,1)S(1)}, u32[]{:S(2)}, u32[]{:S(2)}) collective-permute-start(bf16[32,256]{1,0:T(8,128)(2,1)S(1)} %get-tuple-element.38), channel_id=1, source_target_pairs={{0,32},{32,64},{64,96},{96,0},{1,33},{33,65},{65,97},{97,1},{2,34}... | collective-permute-start | bytes 49160 | tf_op jit(solution)/shard_map/ppermute | solution.py:260
  252.6 1.0 copy-start.7
  (7 other events, 5.9 us)

commit v6 on v5

--- a/solution.py
+++ b/solution.py
@@ -20,7 +20,7 @@
 Z = ("z_hi", "z_lo")
 SEQ = ("x", *Z)
 HEAD = ("y", "core")
-EARLY = pl.CostEstimate(flops=40_000_000_000, bytes_accessed=0, transcendentals=0)
+EARLY = pl.CostEstimate(flops=90_000_000_000, bytes_accessed=0, transcendentals=0)
 PARAMS = pltpu.CompilerParams(vmem_limit_bytes=24 * 1024 * 1024)
 
 
@@ -241,11 +241,10 @@
     slot_iota = lax.broadcasted_iota(jnp.int32, (tokens, slots), 1)
     for h in range(heads):
         select = jnp.where(slot_iota == place_ref[:, h : h + 1], 1.0, 0.0).astype(jnp.bfloat16)
+        rows = home_ref[:, h * CAP : (h + 1) * CAP, :].reshape(slots, 3 * DH)
+        rows = jnp.dot(select, rows, preferred_element_type=jnp.float32).astype(jnp.bfloat16)
         for n, ref in enumerate((dq_ref, dk_ref, dv_ref)):
-            rows = home_ref[:, h * CAP : (h + 1) * CAP, n * DH : (n + 1) * DH].reshape(slots, DH)
-            ref[:, h * DH : (h + 1) * DH] = jnp.dot(
-                select, rows, preferred_element_type=jnp.float32
-            ).astype(jnp.bfloat16)
+            ref[:, h * DH : (h + 1) * DH] = rows[:, n * DH : (n + 1) * DH]
 
 
 def copies_to_all(block, axis):
@@ -326,14 +325,6 @@
         name="add_along_z_lo",
     )(own, *moved)
     moved = [forward(share[n], "z_hi", n) for n in range(1, 4)]
-    weight_grad = pl.pallas_call(
-        add_last_kernel,
-        out_shape=shape(own.shape, jnp.float32),
-        compiler_params=PARAMS,
-        cost_estimate=pl.CostEstimate(flops=50_000_000_000, bytes_accessed=0, transcendentals=0),
-        name="add_along_z_hi",
-    )(own, *moved)
-
     grads = pl.pallas_call(
         attend_kernel,
         out_shape=shape((owners, heads * CAP, 3 * DH), bf16),
@@ -351,6 +342,13 @@
         compiler_params=PARAMS,
         name="unpack_rows",
     )(home, places)
+    own, moved, dq = lax.optimization_barrier((own, moved, dq))
+    weight_grad = pl.pallas_call(
+        add_last_kernel,
+        out_shape=shape(own.shape, jnp.float32),
+        compiler_params=PARAMS,
+        name="add_along_z_hi",
+    )(own, *moved)
     return dq, dk, dv, weight_grad
 
 

time: 258 us -> 255 us (0.988)
    ppermute x16, waiting for transfers between devices: 82.9 us -> 30.9 us  [forward(): lax.ppermute(block, axis, [(i, (i + shift) % size) for i in range(size)])]
    all_to_all x1, waiting for transfers between devices: 0.01 us -> 49.8 us  [local(): home = lax.all_to_all(grads, SEQ, 0, 0, tiled=True)]
where the time goes in v6:
time: 255 us; the launch traced here: 253 us
  waiting for transfers between devices  124 us (49%)
  starting transfers between devices  102 us (40%)
  Pallas kernels  19.1 us (7%)
  local copies, waits for them, and re-layouts  7.58 us (3%)
    ppermute x16, starting transfers between devices, forward(): lax.ppermute(block, axis, [(i, (i + shift) % size) for i in range(size)])  61.4 us
    all_to_all x1, waiting for transfers between devices, local(): home = lax.all_to_all(grads, SEQ, 0, 0, tiled=True)  49.8 us
    ppermute x16, waiting for transfers between devices, forward(): lax.ppermute(block, axis, [(i, (i + shift) % size) for i in range(size)])  30.9 us
    all_to_all x1, waiting for transfers between devices, local(): cot = lax.all_to_all(cot, SEQ, 0, 0, tiled=True).reshape(owners * PAIR, DH)  23.5 us
    all_to_all x1, starting transfers between devices, copies_to_all(): lax.all_to_all(jnp.broadcast_to(block[None], (size, *block.shape)), axis,...  15.2 us
    all_to_all x1, waiting for transfers between devices, local(): qkv = lax.all_to_all(after(qkv, (weight_z, pair)), SEQ, 0, 0, tiled=True)  9.67 us
    all_to_all x1, waiting for transfers between devices, copies_to_all(): lax.all_to_all(jnp.broadcast_to(block[None], (size, *block.shape)), axis,...  9.63 us
    all_to_all x1, starting transfers between devices, local(): qkv = lax.all_to_all(after(qkv, (weight_z, pair)), SEQ, 0, 0, tiled=True)  9.52 us
  transfers between devices with their start and end apart: 20, of which 10 were waited for; matrix products, arithmetic and copies ran while one was open for 0% of the time, Pallas kernels for 7%

profile of v6, /device:TPU:6, one launch (start us, length us, event | category | flops | bytes accessed | tf_op | source)
XLA Modules:
  0.0 253.3 jit_solution(6771604844786941522)
XLA Ops:
  2.1 15.2 %all-to-all-start = ((bf16[16,32,256]{2,1,0:T(8,128)(2,1)}), bf16[16,32,256]{2,1,0:T(8,128)(2,1)S(1)}, u32[]{:S(2)}, u32[]{:S(2)}) async-start(bf16[16,32,256]{2,1,0:T(8,128)(2,1)} %broadcast_in_dim.2), calls=%async_computation | async-start | bytes 524288 | tf_op jit(solution)/shard_map/all_to_all | solution.py:252
  22.8 3.2 %pack_rows.1 = bf16[64,32,384]{2,1,0:T(8,128)(2,1)} custom-call(s32[2,512]{1,0:T(2,128)S(1)} %copy-done.8, bf16[512,256]{1,0:T(8,128)(2,1)S(1)} %copy-done.3, bf16[512,256]{1,0:T(8,128)(2,1)S(1)} %copy-done.4, bf16[512,256]{1,0:T(8,128)(2,1)S(1)} %copy-done.5), custom_call_target="tpu_custom_call" | custom-call | tf_op jit(solution)/shard_map/pack_rows/pallas_call | solution.py:286
  26.1 9.6 %all-to-all-done = bf16[16,32,256]{2,1,0:T(8,128)(2,1)S(1)} async-done(((bf16[16,32,256]{2,1,0:T(8,128)(2,1)}), bf16[16,32,256]{2,1,0:T(8,128)(2,1)S(1)}, u32[]{:S(2)}, u32[]{:S(2)}) %all-to-all-start) | async-done | bytes 262176 | tf_op jit(solution)/shard_map/all_to_all | solution.py:252
  36.4 9.5 %all-to-all-start.1 = ((bf16[64,32,384]{2,1,0:T(8,128)(2,1)}), bf16[64,32,384]{2,1,0:T(8,128)(2,1)S(1)}, u32[]{:S(2)}, u32[]{:S(2)}) async-start(bf16[64,32,384]{2,1,0:T(8,128)(2,1)} %pack_rows.1), calls=%async_computation.1 | async-start | bytes 3145728 | tf_op jit(solution)/shard_map/all_to_all | solution.py:293
  45.9 4.9 %collective-permute-start.6 = (bf16[2,512,256]{2,1,0:T(8,128)(2,1)S(1)}, bf16[2,512,256]{2,1,0:T(8,128)(2,1)S(1)}, u32[]{:S(2)}, u32[]{:S(2)}) collective-permute-start(bf16[2,512,256]{2,1,0:T(8,128)(2,1)S(1)} %pad_maximum_fusion.refs_4_.refs_0_), channel_id=1, source_target_pairs={{0,6},{2,0},{4,2},{6,4},{1,7},{3,1},{5,3},{7,5},{8,14},{10,8},{12,... | collective-permute-start | bytes 1572872 | tf_op jit(solution)/shard_map/ppermute | solution.py:259
  61.8 10.8 %collective-permute-done.6.refs_7_.refs_3_ = bf16[2,512,256]{2,1,0:T(8,128)(2,1)S(1)} collective-permute-done((bf16[2,512,256]{2,1,0:T(8,128)(2,1)S(1)}, bf16[2,512,256]{2,1,0:T(8,128)(2,1)S(1)}, u32[]{:S(2)}, u32[]{:S(2)}) %collective-permute-start.6) | collective-permute-done | bytes 524320 | tf_op jit(solution)/shard_map/ppermute | solution.py:259
  75.2 3.2 %collective-permute-done.4.refs_5_.refs_1_ = bf16[2,512,256]{2,1,0:T(8,128)(2,1)} collective-permute-done((bf16[2,512,256]{2,1,0:T(8,128)(2,1)S(1)}, bf16[2,512,256]{2,1,0:T(8,128)(2,1)}, u32[]{:S(2)}, u32[]{:S(2)}) %collective-permute-start.4) | collective-permute-done | bytes 524320 | tf_op jit(solution)/shard_map/ppermute | solution.py:259
  78.4 3.4 %collective-permute-done.refs_1_ = bf16[512,256]{1,0:T(8,128)(2,1)} collective-permute-done((bf16[512,256]{1,0:T(8,128)(2,1)}, bf16[512,256]{1,0:T(8,128)(2,1)}, u32[]{:S(2)}, u32[]{:S(2)}) %collective-permute-start) | collective-permute-done | bytes 262176 | tf_op jit(solution)/shard_map/ppermute | solution.py:259
  82.7 5.9 %cotangent_rows.1 = (bf16[2176,128]{1,0:T(8,128)(2,1)}, s32[512,8]{1,0:T(8,128)S(1)}) custom-call(s32[5]{0:T(128)S(1)} %stack.32.here_ref, s32[2,512]{1,0:T(2,128)S(1)} %copy-done.9, bf16[512,256]{1,0:T(8,128)(2,1)S(1)} %copy-done, bf16[512,256]{1,0:T(8,128)(2,1)S(1)} %bitcast.43, bf16[512,256]{1,0:T(8,128)(2,1)} %collective-permute-done.refs_1_, ...), custom_call_target="tpu_custom_call" | custom-call | tf_op jit(solution)/shard_map/cotangent_rows/pallas_call | solution.py:297
  91.4 3.7 %collective-permute-start.7 = (bf16[4,4,32,256]{3,2,1,0:T(8,128)(2,1)S(1)}, bf16[4,4,32,256]{3,2,1,0:T(8,128)(2,1)S(1)}, u32[]{:S(2)}, u32[]{:S(2)}) collective-permute-start(bf16[4,4,32,256]{3,2,1,0:T(8,128)(2,1)S(1)} %get-tuple-element.40), channel_id=1, source_target_pairs={{0,128},{128,256},{256,384},{384,0},{1,129},{129,257},{257,385},{3... | collective-permute-start | bytes 786440 | tf_op jit(solution)/shard_map/ppermute | solution.py:259
  97.2 3.1 %collective-permute-start.8 = (bf16[4,4,32,256]{3,2,1,0:T(8,128)(2,1)S(1)}, bf16[4,4,32,256]{3,2,1,0:T(8,128)(2,1)S(1)}, u32[]{:S(2)}, u32[]{:S(2)}) collective-permute-start(bf16[4,4,32,256]{3,2,1,0:T(8,128)(2,1)S(1)} %get-tuple-element.42), channel_id=1, source_target_pairs={{0,256},{128,384},{256,0},{384,128},{1,257},{129,385},{257,1},{385... | collective-permute-start | bytes 786440 | tf_op jit(solution)/shard_map/ppermute | solution.py:259
  100.4 3.0 %collective-permute-done.7 = bf16[4,4,32,256]{3,2,1,0:T(8,128)(2,1)S(1)} collective-permute-done((bf16[4,4,32,256]{3,2,1,0:T(8,128)(2,1)S(1)}, bf16[4,4,32,256]{3,2,1,0:T(8,128)(2,1)S(1)}, u32[]{:S(2)}, u32[]{:S(2)}) %collective-permute-start.7) | collective-permute-done | bytes 262176 | tf_op jit(solution)/shard_map/ppermute | solution.py:259
  103.3 8.8 %collective-permute-done.9 = bf16[4,4,32,256]{3,2,1,0:T(8,128)(2,1)S(1)} collective-permute-done((bf16[4,4,32,256]{3,2,1,0:T(8,128)(2,1)S(1)}, bf16[4,4,32,256]{3,2,1,0:T(8,128)(2,1)S(1)}, u32[]{:S(2)}, u32[]{:S(2)}) %collective-permute-start.9) | collective-permute-done | bytes 262176 | tf_op jit(solution)/shard_map/ppermute | solution.py:259
  112.3 9.7 %all-to-all-done.1.qkv_ref = bf16[64,32,384]{2,1,0:T(8,128)(2,1)S(1)} async-done(((bf16[64,32,384]{2,1,0:T(8,128)(2,1)}), bf16[64,32,384]{2,1,0:T(8,128)(2,1)S(1)}, u32[]{:S(2)}, u32[]{:S(2)}) %all-to-all-start.1) | async-done | bytes 1572896 | tf_op jit(solution)/shard_map/all_to_all | solution.py:293
  122.0 7.0 %all-to-all-start.2 = ((bf16[1088,2,128]{2,1,0:T(2,128)(2,1)}), bf16[1088,2,128]{2,1,0:T(2,128)(2,1)S(1)}, u32[]{:S(2)}, u32[]{:S(2)}) async-start(bf16[1088,2,128]{2,1,0:T(2,128)(2,1)} %bitcast.19), calls=%async_computation.2 | async-start | bytes 1114112 | tf_op jit(solution)/shard_map/all_to_all | solution.py:319
  129.0 5.2 %collective-permute-start.12 = (bf16[4,32,256]{2,1,0:T(8,128)(2,1)S(1)}, bf16[4,32,256]{2,1,0:T(8,128)(2,1)S(1)}, u32[]{:S(2)}, u32[]{:S(2)}) collective-permute-start(bf16[4,32,256]{2,1,0:T(8,128)(2,1)S(1)} %get-tuple-element.43), channel_id=1, source_target_pairs={{0,24},{8,0},{16,8},{24,16},{1,25},{9,1},{17,9},{25,17},{2,26},{10... | collective-permute-start | bytes 196616 | tf_op jit(solution)/shard_map/ppermute | solution.py:259
  136.1 3.2 %collective-permute-start.10 = (bf16[4,32,256]{2,1,0:T(8,128)(2,1)S(1)}, bf16[4,32,256]{2,1,0:T(8,128)(2,1)S(1)}, u32[]{:S(2)}, u32[]{:S(2)}) collective-permute-start(bf16[4,32,256]{2,1,0:T(8,128)(2,1)S(1)} %get-tuple-element.45), channel_id=1, source_target_pairs={{0,8},{8,16},{16,24},{24,0},{1,9},{9,17},{17,25},{25,1},{2,10},{10... | collective-permute-start | bytes 196616 | tf_op jit(solution)/shard_map/ppermute | solution.py:259
  139.3 23.5 %all-to-all-done.2 = bf16[1088,2,128]{2,1,0:T(2,128)(2,1)S(1)} async-done(((bf16[1088,2,128]{2,1,0:T(2,128)(2,1)}), bf16[1088,2,128]{2,1,0:T(2,128)(2,1)S(1)}, u32[]{:S(2)}, u32[]{:S(2)}) %all-to-all-start.2) | async-done | bytes 557088 | tf_op jit(solution)/shard_map/all_to_all | solution.py:319
  162.9 5.4 %attend_cluster.1 = bf16[64,32,384]{2,1,0:T(8,128)(2,1)} custom-call(bf16[64,32,384]{2,1,0:T(8,128)(2,1)S(1)} %all-to-all-done.1.qkv_ref, bf16[2176,128]{1,0:T(8,128)(2,1)S(1)} %bitcast.39), custom_call_target="tpu_custom_call" | custom-call | tf_op jit(solution)/shard_map/attend_cluster/pallas_call | solution.py:328
  168.2 8.7 %all-to-all-start.3 = ((bf16[64,32,384]{2,1,0:T(8,128)(2,1)}), bf16[64,32,384]{2,1,0:T(8,128)(2,1)S(1)}, u32[]{:S(2)}, u32[]{:S(2)}) async-start(bf16[64,32,384]{2,1,0:T(8,128)(2,1)} %attend_cluster.1), calls=%async_computation.3 | async-start | bytes 3145728 | tf_op jit(solution)/shard_map/all_to_all | solution.py:338
  177.0 7.4 %collective-permute-start.15 = (bf16[32,256]{1,0:T(8,128)(2,1)S(1)}, bf16[32,256]{1,0:T(8,128)(2,1)S(1)}, u32[]{:S(2)}, u32[]{:S(2)}) collective-permute-start(bf16[32,256]{1,0:T(8,128)(2,1)S(1)} %get-tuple-element.46), channel_id=1, source_target_pairs={{0,96},{32,0},{64,32},{96,64},{1,97},{33,1},{65,33},{97,65},{2,98}... | collective-permute-start | bytes 49160 | tf_op jit(solution)/shard_map/ppermute | solution.py:259
  184.4 7.2 %collective-permute-start.14 = (bf16[32,256]{1,0:T(8,128)(2,1)S(1)}, bf16[32,256]{1,0:T(8,128)(2,1)S(1)}, u32[]{:S(2)}, u32[]{:S(2)}) collective-permute-start(bf16[32,256]{1,0:T(8,128)(2,1)S(1)} %get-tuple-element.47), channel_id=1, source_target_pairs={{0,64},{32,96},{64,0},{96,32},{1,65},{33,97},{65,1},{97,33},{2,66}... | collective-permute-start | bytes 49160 | tf_op jit(solution)/shard_map/ppermute | solution.py:259
  191.6 7.3 %collective-permute-start.13 = (bf16[32,256]{1,0:T(8,128)(2,1)S(1)}, bf16[32,256]{1,0:T(8,128)(2,1)S(1)}, u32[]{:S(2)}, u32[]{:S(2)}) collective-permute-start(bf16[32,256]{1,0:T(8,128)(2,1)S(1)} %get-tuple-element.48), channel_id=1, source_target_pairs={{0,32},{32,64},{64,96},{96,0},{1,33},{33,65},{65,97},{97,1},{2,34}... | collective-permute-start | bytes 49160 | tf_op jit(solution)/shard_map/ppermute | solution.py:259
  199.0 49.8 %all-to-all-done.3.home_ref = bf16[64,32,384]{2,1,0:T(8,128)(2,1)S(1)} async-done(((bf16[64,32,384]{2,1,0:T(8,128)(2,1)}), bf16[64,32,384]{2,1,0:T(8,128)(2,1)S(1)}, u32[]{:S(2)}, u32[]{:S(2)}) %all-to-all-start.3) | async-done | bytes 1572896 | tf_op jit(solution)/shard_map/all_to_all | solution.py:338
  (54 shorter events, 33.7 us)
Async XLA Ops:
  0.6 25.4 %copy-start.10 = (bf16[512,256]{1,0:T(8,128)(2,1)S(1)}, bf16[512,256]{1,0:T(8,128)(2,1)}, u32[]{:S(2)}) copy-start(bf16[512,256]{1,0:T(8,128)(2,1)} %param.12) | copy-start | bytes 786436
  2.1 33.6 %all-to-all-start = ((bf16[16,32,256]{2,1,0:T(8,128)(2,1)}), bf16[16,32,256]{2,1,0:T(8,128)(2,1)S(1)}, u32[]{:S(2)}, u32[]{:S(2)}) async-start(bf16[16,32,256]{2,1,0:T(8,128)(2,1)} %broadcast_in_dim.2), calls=%async_computation | async-start | bytes 524288 | tf_op jit(solution)/shard_map/all_to_all | solution.py:252
  17.3 8.7 %collective-permute-start.3 = (bf16[512,256]{1,0:T(8,128)(2,1)}, bf16[512,256]{1,0:T(8,128)(2,1)S(1)}, u32[]{:S(2)}, u32[]{:S(2)}) collective-permute-start(bf16[512,256]{1,0:T(8,128)(2,1)} %param.12), channel_id=1, source_target_pairs={{0,1},{1,0},{2,3},{3,2},{4,5},{5,4},{6,7},{7,6},{8,9},{9,8},{10,11... | collective-permute-start | bytes 786440 | tf_op jit(solution)/shard_map/ppermute | solution.py:259
  36.4 45.4 %copy-start = (bf16[512,256]{1,0:T(8,128)(2,1)S(1)}, bf16[512,256]{1,0:T(8,128)(2,1)}, u32[]{:S(2)}) copy-start(bf16[512,256]{1,0:T(8,128)(2,1)} %saved_ref.2) | copy-start | bytes 786436
  36.4 45.4 %copy-start.9 = (s32[2,512]{1,0:T(2,128)S(1)}, s32[2,512]{1,0:T(2,128)}, u32[]{:S(2)}) copy-start(s32[2,512]{1,0:T(2,128)} %ids_ref.3) | copy-start | bytes 12292
  36.4 85.6 %all-to-all-start.1 = ((bf16[64,32,384]{2,1,0:T(8,128)(2,1)}), bf16[64,32,384]{2,1,0:T(8,128)(2,1)S(1)}, u32[]{:S(2)}, u32[]{:S(2)}) async-start(bf16[64,32,384]{2,1,0:T(8,128)(2,1)} %pack_rows.1), calls=%async_computation.1 | async-start | bytes 3145728 | tf_op jit(solution)/shard_map/all_to_all | solution.py:293
  45.9 26.7 %collective-permute-start.6 = (bf16[2,512,256]{2,1,0:T(8,128)(2,1)S(1)}, bf16[2,512,256]{2,1,0:T(8,128)(2,1)S(1)}, u32[]{:S(2)}, u32[]{:S(2)}) collective-permute-start(bf16[2,512,256]{2,1,0:T(8,128)(2,1)S(1)} %pad_maximum_fusion.refs_4_.refs_0_), channel_id=1, source_target_pairs={{0,6},{2,0},{4,2},{6,4},{1,7},{3,1},{5,3},{7,5},{8,14},{10,8},{12,... | collective-permute-start | bytes 1572872 | tf_op jit(solution)/shard_map/ppermute | solution.py:259
  50.9 24.3 %collective-permute-start.5 = (bf16[2,512,256]{2,1,0:T(8,128)(2,1)S(1)}, bf16[2,512,256]{2,1,0:T(8,128)(2,1)S(1)}, u32[]{:S(2)}, u32[]{:S(2)}) collective-permute-start(bf16[2,512,256]{2,1,0:T(8,128)(2,1)S(1)} %pad_maximum_fusion.refs_4_.refs_0_), channel_id=1, source_target_pairs={{0,4},{2,6},{4,0},{6,2},{1,5},{3,7},{5,1},{7,3},{8,12},{10,14},{12... | collective-permute-start | bytes 1572872 | tf_op jit(solution)/shard_map/ppermute | solution.py:259
  53.4 25.0 %collective-permute-start.4 = (bf16[2,512,256]{2,1,0:T(8,128)(2,1)S(1)}, bf16[2,512,256]{2,1,0:T(8,128)(2,1)}, u32[]{:S(2)}, u32[]{:S(2)}) collective-permute-start(bf16[2,512,256]{2,1,0:T(8,128)(2,1)S(1)} %pad_maximum_fusion.refs_4_.refs_0_), channel_id=1, source_target_pairs={{0,2},{2,4},{4,6},{6,0},{1,3},{3,5},{5,7},{7,1},{8,10},{10,12},{12... | collective-permute-start | bytes 1572872 | tf_op jit(solution)/shard_map/ppermute | solution.py:259
  56.3 22.1 %collective-permute-start.2 = (bf16[512,256]{1,0:T(8,128)(2,1)}, bf16[512,256]{1,0:T(8,128)(2,1)}, u32[]{:S(2)}, u32[]{:S(2)}) collective-permute-start(bf16[512,256]{1,0:T(8,128)(2,1)} %bitcast.40), channel_id=1, source_target_pairs={{0,384},{128,0},{256,128},{384,256},{1,385},{129,1},{257,129},{385... | collective-permute-start | bytes 786440 | tf_op jit(solution)/shard_map/ppermute | solution.py:259
  59.0 19.4 %collective-permute-start.1 = (bf16[512,256]{1,0:T(8,128)(2,1)}, bf16[512,256]{1,0:T(8,128)(2,1)}, u32[]{:S(2)}, u32[]{:S(2)}) collective-permute-start(bf16[512,256]{1,0:T(8,128)(2,1)} %bitcast.41), channel_id=1, source_target_pairs={{0,256},{128,384},{256,0},{384,128},{1,257},{129,385},{257,1},{385... | collective-permute-start | bytes 786440 | tf_op jit(solution)/shard_map/ppermute | solution.py:259
  72.6 9.1 %collective-permute-start = (bf16[512,256]{1,0:T(8,128)(2,1)}, bf16[512,256]{1,0:T(8,128)(2,1)}, u32[]{:S(2)}, u32[]{:S(2)}) collective-permute-start(bf16[512,256]{1,0:T(8,128)(2,1)} %bitcast.42), channel_id=1, source_target_pairs={{0,128},{128,256},{256,384},{384,0},{1,129},{129,257},{257,385},{3... | collective-permute-start | bytes 786440 | tf_op jit(solution)/shard_map/ppermute | solution.py:259
  91.4 12.0 %collective-permute-start.7 = (bf16[4,4,32,256]{3,2,1,0:T(8,128)(2,1)S(1)}, bf16[4,4,32,256]{3,2,1,0:T(8,128)(2,1)S(1)}, u32[]{:S(2)}, u32[]{:S(2)}) collective-permute-start(bf16[4,4,32,256]{3,2,1,0:T(8,128)(2,1)S(1)} %get-tuple-element.40), channel_id=1, source_target_pairs={{0,128},{128,256},{256,384},{384,0},{1,129},{129,257},{257,385},{3... | collective-permute-start | bytes 786440 | tf_op jit(solution)/shard_map/ppermute | solution.py:259
  95.1 17.1 %collective-permute-start.9 = (bf16[4,4,32,256]{3,2,1,0:T(8,128)(2,1)S(1)}, bf16[4,4,32,256]{3,2,1,0:T(8,128)(2,1)S(1)}, u32[]{:S(2)}, u32[]{:S(2)}) collective-permute-start(bf16[4,4,32,256]{3,2,1,0:T(8,128)(2,1)S(1)} %get-tuple-element.41), channel_id=1, source_target_pairs={{0,384},{128,0},{256,128},{384,256},{1,385},{129,1},{257,129},{385... | collective-permute-start | bytes 786440 | tf_op jit(solution)/shard_map/ppermute | solution.py:259
  97.2 14.9 %collective-permute-start.8 = (bf16[4,4,32,256]{3,2,1,0:T(8,128)(2,1)S(1)}, bf16[4,4,32,256]{3,2,1,0:T(8,128)(2,1)S(1)}, u32[]{:S(2)}, u32[]{:S(2)}) collective-permute-start(bf16[4,4,32,256]{3,2,1,0:T(8,128)(2,1)S(1)} %get-tuple-element.42), channel_id=1, source_target_pairs={{0,256},{128,384},{256,0},{384,128},{1,257},{129,385},{257,1},{385... | collective-permute-start | bytes 786440 | tf_op jit(solution)/shard_map/ppermute | solution.py:259
  122.0 40.9 %all-to-all-start.2 = ((bf16[1088,2,128]{2,1,0:T(2,128)(2,1)}), bf16[1088,2,128]{2,1,0:T(2,128)(2,1)S(1)}, u32[]{:S(2)}, u32[]{:S(2)}) async-start(bf16[1088,2,128]{2,1,0:T(2,128)(2,1)} %bitcast.19), calls=%async_computation.2 | async-start | bytes 1114112 | tf_op jit(solution)/shard_map/all_to_all | solution.py:319
  129.0 48.0 %collective-permute-start.12 = (bf16[4,32,256]{2,1,0:T(8,128)(2,1)S(1)}, bf16[4,32,256]{2,1,0:T(8,128)(2,1)S(1)}, u32[]{:S(2)}, u32[]{:S(2)}) collective-permute-start(bf16[4,32,256]{2,1,0:T(8,128)(2,1)S(1)} %get-tuple-element.43), channel_id=1, source_target_pairs={{0,24},{8,0},{16,8},{24,16},{1,25},{9,1},{17,9},{25,17},{2,26},{10... | collective-permute-start | bytes 196616 | tf_op jit(solution)/shard_map/ppermute | solution.py:259
  134.2 42.8 %collective-permute-start.11 = (bf16[4,32,256]{2,1,0:T(8,128)(2,1)S(1)}, bf16[4,32,256]{2,1,0:T(8,128)(2,1)S(1)}, u32[]{:S(2)}, u32[]{:S(2)}) collective-permute-start(bf16[4,32,256]{2,1,0:T(8,128)(2,1)S(1)} %get-tuple-element.44), channel_id=1, source_target_pairs={{0,16},{8,24},{16,0},{24,8},{1,17},{9,25},{17,1},{25,9},{2,18},{10... | collective-permute-start | bytes 196616 | tf_op jit(solution)/shard_map/ppermute | solution.py:259
  136.1 40.9 %collective-permute-start.10 = (bf16[4,32,256]{2,1,0:T(8,128)(2,1)S(1)}, bf16[4,32,256]{2,1,0:T(8,128)(2,1)S(1)}, u32[]{:S(2)}, u32[]{:S(2)}) collective-permute-start(bf16[4,32,256]{2,1,0:T(8,128)(2,1)S(1)} %get-tuple-element.45), channel_id=1, source_target_pairs={{0,8},{8,16},{16,24},{24,0},{1,9},{9,17},{17,25},{25,1},{2,10},{10... | collective-permute-start | bytes 196616 | tf_op jit(solution)/shard_map/ppermute | solution.py:259
  168.2 80.5 %all-to-all-start.3 = ((bf16[64,32,384]{2,1,0:T(8,128)(2,1)}), bf16[64,32,384]{2,1,0:T(8,128)(2,1)S(1)}, u32[]{:S(2)}, u32[]{:S(2)}) async-start(bf16[64,32,384]{2,1,0:T(8,128)(2,1)} %attend_cluster.1), calls=%async_computation.3 | async-start | bytes 3145728 | tf_op jit(solution)/shard_map/all_to_all | solution.py:338
  176.9 71.8 %copy-start.7 = (s32[512,8]{1,0:T(8,128)S(1)}, s32[512,8]{1,0:T(8,128)}, u32[]{:S(2)}) copy-start(s32[512,8]{1,0:T(8,128)} %copy-done.6) | copy-start | bytes 49156
  177.0 73.9 %collective-permute-start.15 = (bf16[32,256]{1,0:T(8,128)(2,1)S(1)}, bf16[32,256]{1,0:T(8,128)(2,1)S(1)}, u32[]{:S(2)}, u32[]{:S(2)}) collective-permute-start(bf16[32,256]{1,0:T(8,128)(2,1)S(1)} %get-tuple-element.46), channel_id=1, source_target_pairs={{0,96},{32,0},{64,32},{96,64},{1,97},{33,1},{65,33},{97,65},{2,98}... | collective-permute-start | bytes 49160 | tf_op jit(solution)/shard_map/ppermute | solution.py:259
  184.4 68.2 %collective-permute-start.14 = (bf16[32,256]{1,0:T(8,128)(2,1)S(1)}, bf16[32,256]{1,0:T(8,128)(2,1)S(1)}, u32[]{:S(2)}, u32[]{:S(2)}) collective-permute-start(bf16[32,256]{1,0:T(8,128)(2,1)S(1)} %get-tuple-element.47), channel_id=1, source_target_pairs={{0,64},{32,96},{64,0},{96,32},{1,65},{33,97},{65,1},{97,33},{2,66}... | collective-permute-start | bytes 49160 | tf_op jit(solution)/shard_map/ppermute | solution.py:259
  191.6 61.0 %collective-permute-start.13 = (bf16[32,256]{1,0:T(8,128)(2,1)S(1)}, bf16[32,256]{1,0:T(8,128)(2,1)S(1)}, u32[]{:S(2)}, u32[]{:S(2)}) collective-permute-start(bf16[32,256]{1,0:T(8,128)(2,1)S(1)} %get-tuple-element.48), channel_id=1, source_target_pairs={{0,32},{32,64},{64,96},{96,0},{1,33},{33,65},{65,97},{97,1},{2,34}... | collective-permute-start | bytes 49160 | tf_op jit(solution)/shard_map/ppermute | solution.py:259
  (7 other events, 5.9 us)

commit v7 on v6

--- a/solution.py
+++ b/solution.py
@@ -228,11 +228,6 @@
     sent_ref[...] = total.astype(jnp.bfloat16)
 
 
-def add_last_kernel(own_ref, *refs):
-    *others, sum_ref = refs
-    sum_ref[...] = own_ref[...] + sum(ref[...].astype(jnp.float32) for ref in others)
-
-
 def unpack_kernel(home_ref, place_ref, dq_ref, dk_ref, dv_ref):
     owners = home_ref.shape[0]
     heads = home_ref.shape[1] // CAP
@@ -290,7 +285,7 @@
         name="pack_rows",
     )(cluster_id, query_rows, key_rows, value_rows)
     pair = jnp.stack([output_grad, forward(output_grad, "core", 1)])
-    qkv = lax.all_to_all(after(qkv, (weight_z, pair)), SEQ, 0, 0, tiled=True)
+    qkv = lax.all_to_all(after(qkv, (weight_z[:16, :DH], pair)), SEQ, 0, 0, tiled=True)
 
     pairs = [pair] + [forward(pair, "y", n) for n in range(1, lax.axis_size("y"))]
     parts = [weight_z] + [forward(weight_z, "x", n) for n in range(1, lax.axis_size("x"))]
@@ -343,12 +338,7 @@
         name="unpack_rows",
     )(home, places)
     own, moved, dq = lax.optimization_barrier((own, moved, dq))
-    weight_grad = pl.pallas_call(
-        add_last_kernel,
-        out_shape=shape(own.shape, jnp.float32),
-        compiler_params=PARAMS,
-        name="add_along_z_hi",
-    )(own, *moved)
+    weight_grad = own + sum(block.astype(jnp.float32) for block in moved)
     return dq, dk, dv, weight_grad
 
 

time: 255 us -> 255 us (level)
  no operation moved by 1% of the time
where the time goes in v7:
time: 255 us; the launch traced here: 253 us
  waiting for transfers between devices  123 us (48%)
  starting transfers between devices  102 us (40%)
  Pallas kernels  18.5 us (7%)
  local copies, waits for them, and re-layouts  7.59 us (3%)
    ppermute x16, starting transfers between devices, forward(): lax.ppermute(block, axis, [(i, (i + shift) % size) for i in range(size)])  61.4 us
    all_to_all x1, waiting for transfers between devices, local(): home = lax.all_to_all(grads, SEQ, 0, 0, tiled=True)  49.8 us
    ppermute x16, waiting for transfers between devices, forward(): lax.ppermute(block, axis, [(i, (i + shift) % size) for i in range(size)])  30.9 us
    all_to_all x1, waiting for transfers between devices, local(): cot = lax.all_to_all(cot, SEQ, 0, 0, tiled=True).reshape(owners * PAIR, DH)  23.5 us
    all_to_all x1, starting transfers between devices, copies_to_all(): lax.all_to_all(jnp.broadcast_to(block[None], (size, *block.shape)), axis,...  15.2 us
    all_to_all x1, waiting for transfers between devices, local(): lax.all_to_all(after(qkv, (weight_z[:16, :DH], pair)), SEQ, 0, 0, tiled=T...  9.67 us
    all_to_all x1, waiting for transfers between devices, copies_to_all(): lax.all_to_all(jnp.broadcast_to(block[None], (size, *block.shape)), axis,...  9.6 us
    all_to_all x1, starting transfers between devices, local(): lax.all_to_all(after(qkv, (weight_z[:16, :DH], pair)), SEQ, 0, 0, tiled=T...  9.39 us
  transfers between devices with their start and end apart: 20, of which 10 were waited for; matrix products, arithmetic and copies ran while one was open for 0% of the time, Pallas kernels for 7%

profile of v7, /device:TPU:6, one launch (start us, length us, event | category | flops | bytes accessed | tf_op | source)
XLA Modules:
  0.0 253.1 jit_solution(15704201579077837301)
XLA Ops:
  2.1 15.2 %all-to-all-start = ((bf16[16,32,256]{2,1,0:T(8,128)(2,1)}), bf16[16,32,256]{2,1,0:T(8,128)(2,1)S(1)}, u32[]{:S(2)}, u32[]{:S(2)}) async-start(bf16[16,32,256]{2,1,0:T(8,128)(2,1)} %broadcast_in_dim.2), calls=%async_computation | async-start | bytes 524288 | tf_op jit(solution)/shard_map/all_to_all | solution.py:247
  22.8 3.2 %pack_rows.1 = bf16[64,32,384]{2,1,0:T(8,128)(2,1)} custom-call(s32[2,512]{1,0:T(2,128)S(1)} %copy-done.8, bf16[512,256]{1,0:T(8,128)(2,1)S(1)} %copy-done.3, bf16[512,256]{1,0:T(8,128)(2,1)S(1)} %copy-done.4, bf16[512,256]{1,0:T(8,128)(2,1)S(1)} %copy-done.5), custom_call_target="tpu_custom_call" | custom-call | tf_op jit(solution)/shard_map/pack_rows/pallas_call | solution.py:281
  26.1 9.6 %all-to-all-done = bf16[16,32,256]{2,1,0:T(8,128)(2,1)S(1)} async-done(((bf16[16,32,256]{2,1,0:T(8,128)(2,1)}), bf16[16,32,256]{2,1,0:T(8,128)(2,1)S(1)}, u32[]{:S(2)}, u32[]{:S(2)}) %all-to-all-start) | async-done | bytes 262176 | tf_op jit(solution)/shard_map/all_to_all | solution.py:247
  36.4 9.4 %all-to-all-start.1 = ((bf16[64,32,384]{2,1,0:T(8,128)(2,1)}), bf16[64,32,384]{2,1,0:T(8,128)(2,1)S(1)}, u32[]{:S(2)}, u32[]{:S(2)}) async-start(bf16[64,32,384]{2,1,0:T(8,128)(2,1)} %pack_rows.1), calls=%async_computation.1 | async-start | bytes 3145728 | tf_op jit(solution)/shard_map/all_to_all | solution.py:288
  45.8 4.9 %collective-permute-start.6 = (bf16[2,512,256]{2,1,0:T(8,128)(2,1)S(1)}, bf16[2,512,256]{2,1,0:T(8,128)(2,1)S(1)}, u32[]{:S(2)}, u32[]{:S(2)}) collective-permute-start(bf16[2,512,256]{2,1,0:T(8,128)(2,1)S(1)} %pad_maximum_fusion.refs_4_.refs_0_), channel_id=1, source_target_pairs={{0,6},{2,0},{4,2},{6,4},{1,7},{3,1},{5,3},{7,5},{8,14},{10,8},{12,... | collective-permute-start | bytes 1572872 | tf_op jit(solution)/shard_map/ppermute | solution.py:254
  61.7 10.8 %collective-permute-done.6.refs_7_.refs_3_ = bf16[2,512,256]{2,1,0:T(8,128)(2,1)S(1)} collective-permute-done((bf16[2,512,256]{2,1,0:T(8,128)(2,1)S(1)}, bf16[2,512,256]{2,1,0:T(8,128)(2,1)S(1)}, u32[]{:S(2)}, u32[]{:S(2)}) %collective-permute-start.6) | collective-permute-done | bytes 524320 | tf_op jit(solution)/shard_map/ppermute | solution.py:254
  75.0 3.2 %collective-permute-done.4.refs_5_.refs_1_ = bf16[2,512,256]{2,1,0:T(8,128)(2,1)} collective-permute-done((bf16[2,512,256]{2,1,0:T(8,128)(2,1)S(1)}, bf16[2,512,256]{2,1,0:T(8,128)(2,1)}, u32[]{:S(2)}, u32[]{:S(2)}) %collective-permute-start.4) | collective-permute-done | bytes 524320 | tf_op jit(solution)/shard_map/ppermute | solution.py:254
  78.2 3.4 %collective-permute-done.refs_1_ = bf16[512,256]{1,0:T(8,128)(2,1)} collective-permute-done((bf16[512,256]{1,0:T(8,128)(2,1)}, bf16[512,256]{1,0:T(8,128)(2,1)}, u32[]{:S(2)}, u32[]{:S(2)}) %collective-permute-start) | collective-permute-done | bytes 262176 | tf_op jit(solution)/shard_map/ppermute | solution.py:254
  82.6 5.9 %cotangent_rows.1 = (bf16[2176,128]{1,0:T(8,128)(2,1)}, s32[512,8]{1,0:T(8,128)S(1)}) custom-call(s32[5]{0:T(128)S(1)} %stack.32.here_ref, s32[2,512]{1,0:T(2,128)S(1)} %copy-done.9, bf16[512,256]{1,0:T(8,128)(2,1)S(1)} %copy-done, bf16[512,256]{1,0:T(8,128)(2,1)S(1)} %bitcast.43, bf16[512,256]{1,0:T(8,128)(2,1)} %collective-permute-done.refs_1_, ...), custom_call_target="tpu_custom_call" | custom-call | tf_op jit(solution)/shard_map/cotangent_rows/pallas_call | solution.py:292
  91.2 3.7 %collective-permute-start.7 = (bf16[4,4,32,256]{3,2,1,0:T(8,128)(2,1)S(1)}, bf16[4,4,32,256]{3,2,1,0:T(8,128)(2,1)S(1)}, u32[]{:S(2)}, u32[]{:S(2)}) collective-permute-start(bf16[4,4,32,256]{3,2,1,0:T(8,128)(2,1)S(1)} %get-tuple-element.40), channel_id=1, source_target_pairs={{0,128},{128,256},{256,384},{384,0},{1,129},{129,257},{257,385},{3... | collective-permute-start | bytes 786440 | tf_op jit(solution)/shard_map/ppermute | solution.py:254
  97.1 3.1 %collective-permute-start.8 = (bf16[4,4,32,256]{3,2,1,0:T(8,128)(2,1)S(1)}, bf16[4,4,32,256]{3,2,1,0:T(8,128)(2,1)S(1)}, u32[]{:S(2)}, u32[]{:S(2)}) collective-permute-start(bf16[4,4,32,256]{3,2,1,0:T(8,128)(2,1)S(1)} %get-tuple-element.42), channel_id=1, source_target_pairs={{0,256},{128,384},{256,0},{384,128},{1,257},{129,385},{257,1},{385... | collective-permute-start | bytes 786440 | tf_op jit(solution)/shard_map/ppermute | solution.py:254
  100.2 3.0 %collective-permute-done.7 = bf16[4,4,32,256]{3,2,1,0:T(8,128)(2,1)S(1)} collective-permute-done((bf16[4,4,32,256]{3,2,1,0:T(8,128)(2,1)S(1)}, bf16[4,4,32,256]{3,2,1,0:T(8,128)(2,1)S(1)}, u32[]{:S(2)}, u32[]{:S(2)}) %collective-permute-start.7) | collective-permute-done | bytes 262176 | tf_op jit(solution)/shard_map/ppermute | solution.py:254
  103.2 8.8 %collective-permute-done.9 = bf16[4,4,32,256]{3,2,1,0:T(8,128)(2,1)S(1)} collective-permute-done((bf16[4,4,32,256]{3,2,1,0:T(8,128)(2,1)S(1)}, bf16[4,4,32,256]{3,2,1,0:T(8,128)(2,1)S(1)}, u32[]{:S(2)}, u32[]{:S(2)}) %collective-permute-start.9) | collective-permute-done | bytes 262176 | tf_op jit(solution)/shard_map/ppermute | solution.py:254
  112.2 9.7 %all-to-all-done.1.qkv_ref = bf16[64,32,384]{2,1,0:T(8,128)(2,1)S(1)} async-done(((bf16[64,32,384]{2,1,0:T(8,128)(2,1)}), bf16[64,32,384]{2,1,0:T(8,128)(2,1)S(1)}, u32[]{:S(2)}, u32[]{:S(2)}) %all-to-all-start.1) | async-done | bytes 1572896 | tf_op jit(solution)/shard_map/all_to_all | solution.py:288
  121.9 7.0 %all-to-all-start.2 = ((bf16[1088,2,128]{2,1,0:T(2,128)(2,1)}), bf16[1088,2,128]{2,1,0:T(2,128)(2,1)S(1)}, u32[]{:S(2)}, u32[]{:S(2)}) async-start(bf16[1088,2,128]{2,1,0:T(2,128)(2,1)} %bitcast.19), calls=%async_computation.2 | async-start | bytes 1114112 | tf_op jit(solution)/shard_map/all_to_all | solution.py:314
  128.9 5.2 %collective-permute-start.12 = (bf16[4,32,256]{2,1,0:T(8,128)(2,1)S(1)}, bf16[4,32,256]{2,1,0:T(8,128)(2,1)S(1)}, u32[]{:S(2)}, u32[]{:S(2)}) collective-permute-start(bf16[4,32,256]{2,1,0:T(8,128)(2,1)S(1)} %get-tuple-element.43), channel_id=1, source_target_pairs={{0,24},{8,0},{16,8},{24,16},{1,25},{9,1},{17,9},{25,17},{2,26},{10... | collective-permute-start | bytes 196616 | tf_op jit(solution)/shard_map/ppermute | solution.py:254
  136.0 3.2 %collective-permute-start.10 = (bf16[4,32,256]{2,1,0:T(8,128)(2,1)S(1)}, bf16[4,32,256]{2,1,0:T(8,128)(2,1)S(1)}, u32[]{:S(2)}, u32[]{:S(2)}) collective-permute-start(bf16[4,32,256]{2,1,0:T(8,128)(2,1)S(1)} %get-tuple-element.45), channel_id=1, source_target_pairs={{0,8},{8,16},{16,24},{24,0},{1,9},{9,17},{17,25},{25,1},{2,10},{10... | collective-permute-start | bytes 196616 | tf_op jit(solution)/shard_map/ppermute | solution.py:254
  139.2 23.5 %all-to-all-done.2 = bf16[1088,2,128]{2,1,0:T(2,128)(2,1)S(1)} async-done(((bf16[1088,2,128]{2,1,0:T(2,128)(2,1)}), bf16[1088,2,128]{2,1,0:T(2,128)(2,1)S(1)}, u32[]{:S(2)}, u32[]{:S(2)}) %all-to-all-start.2) | async-done | bytes 557088 | tf_op jit(solution)/shard_map/all_to_all | solution.py:314
  162.7 5.4 %attend_cluster.1 = bf16[64,32,384]{2,1,0:T(8,128)(2,1)} custom-call(bf16[64,32,384]{2,1,0:T(8,128)(2,1)S(1)} %all-to-all-done.1.qkv_ref, bf16[2176,128]{1,0:T(8,128)(2,1)S(1)} %bitcast.39), custom_call_target="tpu_custom_call" | custom-call | tf_op jit(solution)/shard_map/attend_cluster/pallas_call | solution.py:323
  168.1 8.7 %all-to-all-start.3 = ((bf16[64,32,384]{2,1,0:T(8,128)(2,1)}), bf16[64,32,384]{2,1,0:T(8,128)(2,1)S(1)}, u32[]{:S(2)}, u32[]{:S(2)}) async-start(bf16[64,32,384]{2,1,0:T(8,128)(2,1)} %attend_cluster.1), calls=%async_computation.3 | async-start | bytes 3145728 | tf_op jit(solution)/shard_map/all_to_all | solution.py:333
  176.9 7.4 %collective-permute-start.15 = (bf16[32,256]{1,0:T(8,128)(2,1)S(1)}, bf16[32,256]{1,0:T(8,128)(2,1)S(1)}, u32[]{:S(2)}, u32[]{:S(2)}) collective-permute-start(bf16[32,256]{1,0:T(8,128)(2,1)S(1)} %get-tuple-element.46), channel_id=1, source_target_pairs={{0,96},{32,0},{64,32},{96,64},{1,97},{33,1},{65,33},{97,65},{2,98}... | collective-permute-start | bytes 49160 | tf_op jit(solution)/shard_map/ppermute | solution.py:254
  184.3 7.2 %collective-permute-start.14 = (bf16[32,256]{1,0:T(8,128)(2,1)S(1)}, bf16[32,256]{1,0:T(8,128)(2,1)S(1)}, u32[]{:S(2)}, u32[]{:S(2)}) collective-permute-start(bf16[32,256]{1,0:T(8,128)(2,1)S(1)} %get-tuple-element.47), channel_id=1, source_target_pairs={{0,64},{32,96},{64,0},{96,32},{1,65},{33,97},{65,1},{97,33},{2,66}... | collective-permute-start | bytes 49160 | tf_op jit(solution)/shard_map/ppermute | solution.py:254
  191.5 7.3 %collective-permute-start.13 = (bf16[32,256]{1,0:T(8,128)(2,1)S(1)}, bf16[32,256]{1,0:T(8,128)(2,1)S(1)}, u32[]{:S(2)}, u32[]{:S(2)}) collective-permute-start(bf16[32,256]{1,0:T(8,128)(2,1)S(1)} %get-tuple-element.48), channel_id=1, source_target_pairs={{0,32},{32,64},{64,96},{96,0},{1,33},{33,65},{65,97},{97,1},{2,34}... | collective-permute-start | bytes 49160 | tf_op jit(solution)/shard_map/ppermute | solution.py:254
  198.8 49.8 %all-to-all-done.3.home_ref = bf16[64,32,384]{2,1,0:T(8,128)(2,1)S(1)} async-done(((bf16[64,32,384]{2,1,0:T(8,128)(2,1)}), bf16[64,32,384]{2,1,0:T(8,128)(2,1)S(1)}, u32[]{:S(2)}, u32[]{:S(2)}) %all-to-all-start.3) | async-done | bytes 1572896 | tf_op jit(solution)/shard_map/all_to_all | solution.py:333
  (54 shorter events, 33.7 us)
Async XLA Ops:
  0.6 25.4 %copy-start.10 = (bf16[512,256]{1,0:T(8,128)(2,1)S(1)}, bf16[512,256]{1,0:T(8,128)(2,1)}, u32[]{:S(2)}) copy-start(bf16[512,256]{1,0:T(8,128)(2,1)} %param.12) | copy-start | bytes 786436
  2.1 33.6 %all-to-all-start = ((bf16[16,32,256]{2,1,0:T(8,128)(2,1)}), bf16[16,32,256]{2,1,0:T(8,128)(2,1)S(1)}, u32[]{:S(2)}, u32[]{:S(2)}) async-start(bf16[16,32,256]{2,1,0:T(8,128)(2,1)} %broadcast_in_dim.2), calls=%async_computation | async-start | bytes 524288 | tf_op jit(solution)/shard_map/all_to_all | solution.py:247
  17.3 8.7 %collective-permute-start.3 = (bf16[512,256]{1,0:T(8,128)(2,1)}, bf16[512,256]{1,0:T(8,128)(2,1)S(1)}, u32[]{:S(2)}, u32[]{:S(2)}) collective-permute-start(bf16[512,256]{1,0:T(8,128)(2,1)} %param.12), channel_id=1, source_target_pairs={{0,1},{1,0},{2,3},{3,2},{4,5},{5,4},{6,7},{7,6},{8,9},{9,8},{10,11... | collective-permute-start | bytes 786440 | tf_op jit(solution)/shard_map/ppermute | solution.py:254
  26.1 55.6 %copy-start = (bf16[512,256]{1,0:T(8,128)(2,1)S(1)}, bf16[512,256]{1,0:T(8,128)(2,1)}, u32[]{:S(2)}) copy-start(bf16[512,256]{1,0:T(8,128)(2,1)} %saved_ref.2) | copy-start | bytes 786436
  26.1 55.5 %copy-start.9 = (s32[2,512]{1,0:T(2,128)S(1)}, s32[2,512]{1,0:T(2,128)}, u32[]{:S(2)}) copy-start(s32[2,512]{1,0:T(2,128)} %ids_ref.3) | copy-start | bytes 12292
  36.4 85.5 %all-to-all-start.1 = ((bf16[64,32,384]{2,1,0:T(8,128)(2,1)}), bf16[64,32,384]{2,1,0:T(8,128)(2,1)S(1)}, u32[]{:S(2)}, u32[]{:S(2)}) async-start(bf16[64,32,384]{2,1,0:T(8,128)(2,1)} %pack_rows.1), calls=%async_computation.1 | async-start | bytes 3145728 | tf_op jit(solution)/shard_map/all_to_all | solution.py:288
  45.8 26.7 %collective-permute-start.6 = (bf16[2,512,256]{2,1,0:T(8,128)(2,1)S(1)}, bf16[2,512,256]{2,1,0:T(8,128)(2,1)S(1)}, u32[]{:S(2)}, u32[]{:S(2)}) collective-permute-start(bf16[2,512,256]{2,1,0:T(8,128)(2,1)S(1)} %pad_maximum_fusion.refs_4_.refs_0_), channel_id=1, source_target_pairs={{0,6},{2,0},{4,2},{6,4},{1,7},{3,1},{5,3},{7,5},{8,14},{10,8},{12,... | collective-permute-start | bytes 1572872 | tf_op jit(solution)/shard_map/ppermute | solution.py:254
  50.7 24.3 %collective-permute-start.5 = (bf16[2,512,256]{2,1,0:T(8,128)(2,1)S(1)}, bf16[2,512,256]{2,1,0:T(8,128)(2,1)S(1)}, u32[]{:S(2)}, u32[]{:S(2)}) collective-permute-start(bf16[2,512,256]{2,1,0:T(8,128)(2,1)S(1)} %pad_maximum_fusion.refs_4_.refs_0_), channel_id=1, source_target_pairs={{0,4},{2,6},{4,0},{6,2},{1,5},{3,7},{5,1},{7,3},{8,12},{10,14},{12... | collective-permute-start | bytes 1572872 | tf_op jit(solution)/shard_map/ppermute | solution.py:254
  53.3 25.0 %collective-permute-start.4 = (bf16[2,512,256]{2,1,0:T(8,128)(2,1)S(1)}, bf16[2,512,256]{2,1,0:T(8,128)(2,1)}, u32[]{:S(2)}, u32[]{:S(2)}) collective-permute-start(bf16[2,512,256]{2,1,0:T(8,128)(2,1)S(1)} %pad_maximum_fusion.refs_4_.refs_0_), channel_id=1, source_target_pairs={{0,2},{2,4},{4,6},{6,0},{1,3},{3,5},{5,7},{7,1},{8,10},{10,12},{12... | collective-permute-start | bytes 1572872 | tf_op jit(solution)/shard_map/ppermute | solution.py:254
  56.2 22.1 %collective-permute-start.2 = (bf16[512,256]{1,0:T(8,128)(2,1)}, bf16[512,256]{1,0:T(8,128)(2,1)}, u32[]{:S(2)}, u32[]{:S(2)}) collective-permute-start(bf16[512,256]{1,0:T(8,128)(2,1)} %bitcast.40), channel_id=1, source_target_pairs={{0,384},{128,0},{256,128},{384,256},{1,385},{129,1},{257,129},{385... | collective-permute-start | bytes 786440 | tf_op jit(solution)/shard_map/ppermute | solution.py:254
  58.8 19.4 %collective-permute-start.1 = (bf16[512,256]{1,0:T(8,128)(2,1)}, bf16[512,256]{1,0:T(8,128)(2,1)}, u32[]{:S(2)}, u32[]{:S(2)}) collective-permute-start(bf16[512,256]{1,0:T(8,128)(2,1)} %bitcast.41), channel_id=1, source_target_pairs={{0,256},{128,384},{256,0},{384,128},{1,257},{129,385},{257,1},{385... | collective-permute-start | bytes 786440 | tf_op jit(solution)/shard_map/ppermute | solution.py:254
  72.5 9.1 %collective-permute-start = (bf16[512,256]{1,0:T(8,128)(2,1)}, bf16[512,256]{1,0:T(8,128)(2,1)}, u32[]{:S(2)}, u32[]{:S(2)}) collective-permute-start(bf16[512,256]{1,0:T(8,128)(2,1)} %bitcast.42), channel_id=1, source_target_pairs={{0,128},{128,256},{256,384},{384,0},{1,129},{129,257},{257,385},{3... | collective-permute-start | bytes 786440 | tf_op jit(solution)/shard_map/ppermute | solution.py:254
  91.2 12.0 %collective-permute-start.7 = (bf16[4,4,32,256]{3,2,1,0:T(8,128)(2,1)S(1)}, bf16[4,4,32,256]{3,2,1,0:T(8,128)(2,1)S(1)}, u32[]{:S(2)}, u32[]{:S(2)}) collective-permute-start(bf16[4,4,32,256]{3,2,1,0:T(8,128)(2,1)S(1)} %get-tuple-element.40), channel_id=1, source_target_pairs={{0,128},{128,256},{256,384},{384,0},{1,129},{129,257},{257,385},{3... | collective-permute-start | bytes 786440 | tf_op jit(solution)/shard_map/ppermute | solution.py:254
  94.9 17.1 %collective-permute-start.9 = (bf16[4,4,32,256]{3,2,1,0:T(8,128)(2,1)S(1)}, bf16[4,4,32,256]{3,2,1,0:T(8,128)(2,1)S(1)}, u32[]{:S(2)}, u32[]{:S(2)}) collective-permute-start(bf16[4,4,32,256]{3,2,1,0:T(8,128)(2,1)S(1)} %get-tuple-element.41), channel_id=1, source_target_pairs={{0,384},{128,0},{256,128},{384,256},{1,385},{129,1},{257,129},{385... | collective-permute-start | bytes 786440 | tf_op jit(solution)/shard_map/ppermute | solution.py:254
  97.1 14.9 %collective-permute-start.8 = (bf16[4,4,32,256]{3,2,1,0:T(8,128)(2,1)S(1)}, bf16[4,4,32,256]{3,2,1,0:T(8,128)(2,1)S(1)}, u32[]{:S(2)}, u32[]{:S(2)}) collective-permute-start(bf16[4,4,32,256]{3,2,1,0:T(8,128)(2,1)S(1)} %get-tuple-element.42), channel_id=1, source_target_pairs={{0,256},{128,384},{256,0},{384,128},{1,257},{129,385},{257,1},{385... | collective-permute-start | bytes 786440 | tf_op jit(solution)/shard_map/ppermute | solution.py:254
  121.9 40.9 %all-to-all-start.2 = ((bf16[1088,2,128]{2,1,0:T(2,128)(2,1)}), bf16[1088,2,128]{2,1,0:T(2,128)(2,1)S(1)}, u32[]{:S(2)}, u32[]{:S(2)}) async-start(bf16[1088,2,128]{2,1,0:T(2,128)(2,1)} %bitcast.19), calls=%async_computation.2 | async-start | bytes 1114112 | tf_op jit(solution)/shard_map/all_to_all | solution.py:314
  128.9 48.0 %collective-permute-start.12 = (bf16[4,32,256]{2,1,0:T(8,128)(2,1)S(1)}, bf16[4,32,256]{2,1,0:T(8,128)(2,1)S(1)}, u32[]{:S(2)}, u32[]{:S(2)}) collective-permute-start(bf16[4,32,256]{2,1,0:T(8,128)(2,1)S(1)} %get-tuple-element.43), channel_id=1, source_target_pairs={{0,24},{8,0},{16,8},{24,16},{1,25},{9,1},{17,9},{25,17},{2,26},{10... | collective-permute-start | bytes 196616 | tf_op jit(solution)/shard_map/ppermute | solution.py:254
  134.1 42.8 %collective-permute-start.11 = (bf16[4,32,256]{2,1,0:T(8,128)(2,1)S(1)}, bf16[4,32,256]{2,1,0:T(8,128)(2,1)S(1)}, u32[]{:S(2)}, u32[]{:S(2)}) collective-permute-start(bf16[4,32,256]{2,1,0:T(8,128)(2,1)S(1)} %get-tuple-element.44), channel_id=1, source_target_pairs={{0,16},{8,24},{16,0},{24,8},{1,17},{9,25},{17,1},{25,9},{2,18},{10... | collective-permute-start | bytes 196616 | tf_op jit(solution)/shard_map/ppermute | solution.py:254
  136.0 40.9 %collective-permute-start.10 = (bf16[4,32,256]{2,1,0:T(8,128)(2,1)S(1)}, bf16[4,32,256]{2,1,0:T(8,128)(2,1)S(1)}, u32[]{:S(2)}, u32[]{:S(2)}) collective-permute-start(bf16[4,32,256]{2,1,0:T(8,128)(2,1)S(1)} %get-tuple-element.45), channel_id=1, source_target_pairs={{0,8},{8,16},{16,24},{24,0},{1,9},{9,17},{17,25},{25,1},{2,10},{10... | collective-permute-start | bytes 196616 | tf_op jit(solution)/shard_map/ppermute | solution.py:254
  168.1 80.5 %all-to-all-start.3 = ((bf16[64,32,384]{2,1,0:T(8,128)(2,1)}), bf16[64,32,384]{2,1,0:T(8,128)(2,1)S(1)}, u32[]{:S(2)}, u32[]{:S(2)}) async-start(bf16[64,32,384]{2,1,0:T(8,128)(2,1)} %attend_cluster.1), calls=%async_computation.3 | async-start | bytes 3145728 | tf_op jit(solution)/shard_map/all_to_all | solution.py:333
  176.8 71.8 %copy-start.7 = (s32[512,8]{1,0:T(8,128)S(1)}, s32[512,8]{1,0:T(8,128)}, u32[]{:S(2)}) copy-start(s32[512,8]{1,0:T(8,128)} %copy-done.6) | copy-start | bytes 49156
  176.9 73.9 %collective-permute-start.15 = (bf16[32,256]{1,0:T(8,128)(2,1)S(1)}, bf16[32,256]{1,0:T(8,128)(2,1)S(1)}, u32[]{:S(2)}, u32[]{:S(2)}) collective-permute-start(bf16[32,256]{1,0:T(8,128)(2,1)S(1)} %get-tuple-element.46), channel_id=1, source_target_pairs={{0,96},{32,0},{64,32},{96,64},{1,97},{33,1},{65,33},{97,65},{2,98}... | collective-permute-start | bytes 49160 | tf_op jit(solution)/shard_map/ppermute | solution.py:254
  184.3 68.2 %collective-permute-start.14 = (bf16[32,256]{1,0:T(8,128)(2,1)S(1)}, bf16[32,256]{1,0:T(8,128)(2,1)S(1)}, u32[]{:S(2)}, u32[]{:S(2)}) collective-permute-start(bf16[32,256]{1,0:T(8,128)(2,1)S(1)} %get-tuple-element.47), channel_id=1, source_target_pairs={{0,64},{32,96},{64,0},{96,32},{1,65},{33,97},{65,1},{97,33},{2,66}... | collective-permute-start | bytes 49160 | tf_op jit(solution)/shard_map/ppermute | solution.py:254
  191.5 61.0 %collective-permute-start.13 = (bf16[32,256]{1,0:T(8,128)(2,1)S(1)}, bf16[32,256]{1,0:T(8,128)(2,1)S(1)}, u32[]{:S(2)}, u32[]{:S(2)}) collective-permute-start(bf16[32,256]{1,0:T(8,128)(2,1)S(1)} %get-tuple-element.48), channel_id=1, source_target_pairs={{0,32},{32,64},{64,96},{96,0},{1,33},{33,65},{65,97},{97,1},{2,34}... | collective-permute-start | bytes 49160 | tf_op jit(solution)/shard_map/ppermute | solution.py:254
  (7 other events, 5.9 us)

commit v8 on v7

--- a/solution.py
+++ b/solution.py
@@ -49,13 +49,13 @@
     for h, (_, rank) in enumerate(pair_places(ids, owners)):
         place = ids[h : h + 1, :] * CAP + rank.astype(jnp.int32)
         select = jnp.where(slot_iota == place, 1.0, 0.0).astype(jnp.bfloat16)
-        for n, ref in enumerate((q_ref, k_ref, v_ref)):
-            rows = jnp.dot(
-                select, ref[:, h * DH : (h + 1) * DH], preferred_element_type=jnp.float32
-            ).astype(jnp.bfloat16)
-            out_ref[:, h * CAP : (h + 1) * CAP, n * DH : (n + 1) * DH] = rows.reshape(
-                owners, CAP, DH
-            )
+        columns = [ref[:, h * DH : (h + 1) * DH] for ref in (q_ref, k_ref, v_ref)]
+        rows = jnp.dot(
+            select, jnp.concatenate(columns, axis=1), preferred_element_type=jnp.float32
+        )
+        out_ref[:, h * CAP : (h + 1) * CAP, :] = rows.astype(jnp.bfloat16).reshape(
+            owners, CAP, 3 * DH
+        )
 
 
 def block_of(here_ref, back, other):

time: 255 us -> 255 us (level)
  no operation moved by 1% of the time
where the time goes in v8:
time: 255 us; the launch traced here: 253 us
  waiting for transfers between devices  124 us (49%)
  starting transfers between devices  102 us (40%)
  Pallas kernels  18 us (7%)
  local copies, waits for them, and re-layouts  7.59 us (3%)
    ppermute x16, starting transfers between devices, forward(): lax.ppermute(block, axis, [(i, (i + shift) % size) for i in range(size)])  61.4 us
    all_to_all x1, waiting for transfers between devices, local(): home = lax.all_to_all(grads, SEQ, 0, 0, tiled=True)  49.8 us
    ppermute x16, waiting for transfers between devices, forward(): lax.ppermute(block, axis, [(i, (i + shift) % size) for i in range(size)])  30.9 us
    all_to_all x1, waiting for transfers between devices, local(): cot = lax.all_to_all(cot, SEQ, 0, 0, tiled=True).reshape(owners * PAIR, DH)  23.5 us
    all_to_all x1, starting transfers between devices, copies_to_all(): lax.all_to_all(jnp.broadcast_to(block[None], (size, *block.shape)), axis,...  15.2 us
    all_to_all x1, waiting for transfers between devices, copies_to_all(): lax.all_to_all(jnp.broadcast_to(block[None], (size, *block.shape)), axis,...  10.1 us
    all_to_all x1, waiting for transfers between devices, local(): lax.all_to_all(after(qkv, (weight_z[:16, :DH], pair)), SEQ, 0, 0, tiled=T...  9.67 us
    all_to_all x1, starting transfers between devices, local(): lax.all_to_all(after(qkv, (weight_z[:16, :DH], pair)), SEQ, 0, 0, tiled=T...  9.39 us
  transfers between devices with their start and end apart: 20, of which 10 were waited for; matrix products, arithmetic and copies ran while one was open for 0% of the time, Pallas kernels for 7%

profile of v8, /device:TPU:6, one launch (start us, length us, event | category | flops | bytes accessed | tf_op | source)
XLA Modules:
  0.0 253.1 jit_solution(16300911604267894056)
XLA Ops:
  2.1 15.2 %all-to-all-start = ((bf16[16,32,256]{2,1,0:T(8,128)(2,1)}), bf16[16,32,256]{2,1,0:T(8,128)(2,1)S(1)}, u32[]{:S(2)}, u32[]{:S(2)}) async-start(bf16[16,32,256]{2,1,0:T(8,128)(2,1)} %broadcast_in_dim.2), calls=%async_computation | async-start | bytes 524288 | tf_op jit(solution)/shard_map/all_to_all | solution.py:247
  25.5 10.1 %all-to-all-done = bf16[16,32,256]{2,1,0:T(8,128)(2,1)S(1)} async-done(((bf16[16,32,256]{2,1,0:T(8,128)(2,1)}), bf16[16,32,256]{2,1,0:T(8,128)(2,1)S(1)}, u32[]{:S(2)}, u32[]{:S(2)}) %all-to-all-start) | async-done | bytes 262176 | tf_op jit(solution)/shard_map/all_to_all | solution.py:247
  36.4 9.4 %all-to-all-start.1 = ((bf16[64,32,384]{2,1,0:T(8,128)(2,1)}), bf16[64,32,384]{2,1,0:T(8,128)(2,1)S(1)}, u32[]{:S(2)}, u32[]{:S(2)}) async-start(bf16[64,32,384]{2,1,0:T(8,128)(2,1)} %pack_rows.1), calls=%async_computation.1 | async-start | bytes 3145728 | tf_op jit(solution)/shard_map/all_to_all | solution.py:288
  45.8 4.9 %collective-permute-start.6 = (bf16[2,512,256]{2,1,0:T(8,128)(2,1)S(1)}, bf16[2,512,256]{2,1,0:T(8,128)(2,1)S(1)}, u32[]{:S(2)}, u32[]{:S(2)}) collective-permute-start(bf16[2,512,256]{2,1,0:T(8,128)(2,1)S(1)} %pad_maximum_fusion.refs_4_.refs_0_), channel_id=1, source_target_pairs={{0,6},{2,0},{4,2},{6,4},{1,7},{3,1},{5,3},{7,5},{8,14},{10,8},{12,... | collective-permute-start | bytes 1572872 | tf_op jit(solution)/shard_map/ppermute | solution.py:254
  53.3 2.9 %collective-permute-start.4 = (bf16[2,512,256]{2,1,0:T(8,128)(2,1)S(1)}, bf16[2,512,256]{2,1,0:T(8,128)(2,1)}, u32[]{:S(2)}, u32[]{:S(2)}) collective-permute-start(bf16[2,512,256]{2,1,0:T(8,128)(2,1)S(1)} %pad_maximum_fusion.refs_4_.refs_0_), channel_id=1, source_target_pairs={{0,2},{2,4},{4,6},{6,0},{1,3},{3,5},{5,7},{7,1},{8,10},{10,12},{12... | collective-permute-start | bytes 1572872 | tf_op jit(solution)/shard_map/ppermute | solution.py:254
  61.7 10.8 %collective-permute-done.6.refs_7_.refs_3_ = bf16[2,512,256]{2,1,0:T(8,128)(2,1)S(1)} collective-permute-done((bf16[2,512,256]{2,1,0:T(8,128)(2,1)S(1)}, bf16[2,512,256]{2,1,0:T(8,128)(2,1)S(1)}, u32[]{:S(2)}, u32[]{:S(2)}) %collective-permute-start.6) | collective-permute-done | bytes 524320 | tf_op jit(solution)/shard_map/ppermute | solution.py:254
  75.0 3.2 %collective-permute-done.4.refs_5_.refs_1_ = bf16[2,512,256]{2,1,0:T(8,128)(2,1)} collective-permute-done((bf16[2,512,256]{2,1,0:T(8,128)(2,1)S(1)}, bf16[2,512,256]{2,1,0:T(8,128)(2,1)}, u32[]{:S(2)}, u32[]{:S(2)}) %collective-permute-start.4) | collective-permute-done | bytes 524320 | tf_op jit(solution)/shard_map/ppermute | solution.py:254
  78.2 3.4 %collective-permute-done.refs_1_ = bf16[512,256]{1,0:T(8,128)(2,1)} collective-permute-done((bf16[512,256]{1,0:T(8,128)(2,1)}, bf16[512,256]{1,0:T(8,128)(2,1)}, u32[]{:S(2)}, u32[]{:S(2)}) %collective-permute-start) | collective-permute-done | bytes 262176 | tf_op jit(solution)/shard_map/ppermute | solution.py:254
  82.6 5.9 %cotangent_rows.1 = (bf16[2176,128]{1,0:T(8,128)(2,1)}, s32[512,8]{1,0:T(8,128)S(1)}) custom-call(s32[5]{0:T(128)S(1)} %stack.32.here_ref, s32[2,512]{1,0:T(2,128)S(1)} %copy-done.9, bf16[512,256]{1,0:T(8,128)(2,1)S(1)} %copy-done, bf16[512,256]{1,0:T(8,128)(2,1)S(1)} %bitcast.43, bf16[512,256]{1,0:T(8,128)(2,1)} %collective-permute-done.refs_1_, ...), custom_call_target="tpu_custom_call" | custom-call | tf_op jit(solution)/shard_map/cotangent_rows/pallas_call | solution.py:292
  91.2 3.7 %collective-permute-start.7 = (bf16[4,4,32,256]{3,2,1,0:T(8,128)(2,1)S(1)}, bf16[4,4,32,256]{3,2,1,0:T(8,128)(2,1)S(1)}, u32[]{:S(2)}, u32[]{:S(2)}) collective-permute-start(bf16[4,4,32,256]{3,2,1,0:T(8,128)(2,1)S(1)} %get-tuple-element.40), channel_id=1, source_target_pairs={{0,128},{128,256},{256,384},{384,0},{1,129},{129,257},{257,385},{3... | collective-permute-start | bytes 786440 | tf_op jit(solution)/shard_map/ppermute | solution.py:254
  97.1 3.1 %collective-permute-start.8 = (bf16[4,4,32,256]{3,2,1,0:T(8,128)(2,1)S(1)}, bf16[4,4,32,256]{3,2,1,0:T(8,128)(2,1)S(1)}, u32[]{:S(2)}, u32[]{:S(2)}) collective-permute-start(bf16[4,4,32,256]{3,2,1,0:T(8,128)(2,1)S(1)} %get-tuple-element.42), channel_id=1, source_target_pairs={{0,256},{128,384},{256,0},{384,128},{1,257},{129,385},{257,1},{385... | collective-permute-start | bytes 786440 | tf_op jit(solution)/shard_map/ppermute | solution.py:254
  100.2 3.0 %collective-permute-done.7 = bf16[4,4,32,256]{3,2,1,0:T(8,128)(2,1)S(1)} collective-permute-done((bf16[4,4,32,256]{3,2,1,0:T(8,128)(2,1)S(1)}, bf16[4,4,32,256]{3,2,1,0:T(8,128)(2,1)S(1)}, u32[]{:S(2)}, u32[]{:S(2)}) %collective-permute-start.7) | collective-permute-done | bytes 262176 | tf_op jit(solution)/shard_map/ppermute | solution.py:254
  103.2 8.8 %collective-permute-done.9 = bf16[4,4,32,256]{3,2,1,0:T(8,128)(2,1)S(1)} collective-permute-done((bf16[4,4,32,256]{3,2,1,0:T(8,128)(2,1)S(1)}, bf16[4,4,32,256]{3,2,1,0:T(8,128)(2,1)S(1)}, u32[]{:S(2)}, u32[]{:S(2)}) %collective-permute-start.9) | collective-permute-done | bytes 262176 | tf_op jit(solution)/shard_map/ppermute | solution.py:254
  112.2 9.7 %all-to-all-done.1.qkv_ref = bf16[64,32,384]{2,1,0:T(8,128)(2,1)S(1)} async-done(((bf16[64,32,384]{2,1,0:T(8,128)(2,1)}), bf16[64,32,384]{2,1,0:T(8,128)(2,1)S(1)}, u32[]{:S(2)}, u32[]{:S(2)}) %all-to-all-start.1) | async-done | bytes 1572896 | tf_op jit(solution)/shard_map/all_to_all | solution.py:288
  121.9 7.0 %all-to-all-start.2 = ((bf16[1088,2,128]{2,1,0:T(2,128)(2,1)}), bf16[1088,2,128]{2,1,0:T(2,128)(2,1)S(1)}, u32[]{:S(2)}, u32[]{:S(2)}) async-start(bf16[1088,2,128]{2,1,0:T(2,128)(2,1)} %bitcast.19), calls=%async_computation.2 | async-start | bytes 1114112 | tf_op jit(solution)/shard_map/all_to_all | solution.py:314
  128.9 5.2 %collective-permute-start.12 = (bf16[4,32,256]{2,1,0:T(8,128)(2,1)S(1)}, bf16[4,32,256]{2,1,0:T(8,128)(2,1)S(1)}, u32[]{:S(2)}, u32[]{:S(2)}) collective-permute-start(bf16[4,32,256]{2,1,0:T(8,128)(2,1)S(1)} %get-tuple-element.43), channel_id=1, source_target_pairs={{0,24},{8,0},{16,8},{24,16},{1,25},{9,1},{17,9},{25,17},{2,26},{10... | collective-permute-start | bytes 196616 | tf_op jit(solution)/shard_map/ppermute | solution.py:254
  136.0 3.2 %collective-permute-start.10 = (bf16[4,32,256]{2,1,0:T(8,128)(2,1)S(1)}, bf16[4,32,256]{2,1,0:T(8,128)(2,1)S(1)}, u32[]{:S(2)}, u32[]{:S(2)}) collective-permute-start(bf16[4,32,256]{2,1,0:T(8,128)(2,1)S(1)} %get-tuple-element.45), channel_id=1, source_target_pairs={{0,8},{8,16},{16,24},{24,0},{1,9},{9,17},{17,25},{25,1},{2,10},{10... | collective-permute-start | bytes 196616 | tf_op jit(solution)/shard_map/ppermute | solution.py:254
  139.2 23.5 %all-to-all-done.2 = bf16[1088,2,128]{2,1,0:T(2,128)(2,1)S(1)} async-done(((bf16[1088,2,128]{2,1,0:T(2,128)(2,1)}), bf16[1088,2,128]{2,1,0:T(2,128)(2,1)S(1)}, u32[]{:S(2)}, u32[]{:S(2)}) %all-to-all-start.2) | async-done | bytes 557088 | tf_op jit(solution)/shard_map/all_to_all | solution.py:314
  162.7 5.4 %attend_cluster.1 = bf16[64,32,384]{2,1,0:T(8,128)(2,1)} custom-call(bf16[64,32,384]{2,1,0:T(8,128)(2,1)S(1)} %all-to-all-done.1.qkv_ref, bf16[2176,128]{1,0:T(8,128)(2,1)S(1)} %bitcast.39), custom_call_target="tpu_custom_call" | custom-call | tf_op jit(solution)/shard_map/attend_cluster/pallas_call | solution.py:323
  168.1 8.7 %all-to-all-start.3 = ((bf16[64,32,384]{2,1,0:T(8,128)(2,1)}), bf16[64,32,384]{2,1,0:T(8,128)(2,1)S(1)}, u32[]{:S(2)}, u32[]{:S(2)}) async-start(bf16[64,32,384]{2,1,0:T(8,128)(2,1)} %attend_cluster.1), calls=%async_computation.3 | async-start | bytes 3145728 | tf_op jit(solution)/shard_map/all_to_all | solution.py:333
  176.9 7.4 %collective-permute-start.15 = (bf16[32,256]{1,0:T(8,128)(2,1)S(1)}, bf16[32,256]{1,0:T(8,128)(2,1)S(1)}, u32[]{:S(2)}, u32[]{:S(2)}) collective-permute-start(bf16[32,256]{1,0:T(8,128)(2,1)S(1)} %get-tuple-element.46), channel_id=1, source_target_pairs={{0,96},{32,0},{64,32},{96,64},{1,97},{33,1},{65,33},{97,65},{2,98}... | collective-permute-start | bytes 49160 | tf_op jit(solution)/shard_map/ppermute | solution.py:254
  184.3 7.2 %collective-permute-start.14 = (bf16[32,256]{1,0:T(8,128)(2,1)S(1)}, bf16[32,256]{1,0:T(8,128)(2,1)S(1)}, u32[]{:S(2)}, u32[]{:S(2)}) collective-permute-start(bf16[32,256]{1,0:T(8,128)(2,1)S(1)} %get-tuple-element.47), channel_id=1, source_target_pairs={{0,64},{32,96},{64,0},{96,32},{1,65},{33,97},{65,1},{97,33},{2,66}... | collective-permute-start | bytes 49160 | tf_op jit(solution)/shard_map/ppermute | solution.py:254
  191.5 7.3 %collective-permute-start.13 = (bf16[32,256]{1,0:T(8,128)(2,1)S(1)}, bf16[32,256]{1,0:T(8,128)(2,1)S(1)}, u32[]{:S(2)}, u32[]{:S(2)}) collective-permute-start(bf16[32,256]{1,0:T(8,128)(2,1)S(1)} %get-tuple-element.48), channel_id=1, source_target_pairs={{0,32},{32,64},{64,96},{96,0},{1,33},{33,65},{65,97},{97,1},{2,34}... | collective-permute-start | bytes 49160 | tf_op jit(solution)/shard_map/ppermute | solution.py:254
  198.8 49.8 %all-to-all-done.3.home_ref = bf16[64,32,384]{2,1,0:T(8,128)(2,1)S(1)} async-done(((bf16[64,32,384]{2,1,0:T(8,128)(2,1)}), bf16[64,32,384]{2,1,0:T(8,128)(2,1)S(1)}, u32[]{:S(2)}, u32[]{:S(2)}) %all-to-all-start.3) | async-done | bytes 1572896 | tf_op jit(solution)/shard_map/all_to_all | solution.py:333
  (54 shorter events, 33.5 us)
Async XLA Ops:
  0.6 24.8 %copy-start.10 = (bf16[512,256]{1,0:T(8,128)(2,1)S(1)}, bf16[512,256]{1,0:T(8,128)(2,1)}, u32[]{:S(2)}) copy-start(bf16[512,256]{1,0:T(8,128)(2,1)} %param.12) | copy-start | bytes 786436
  2.1 33.6 %all-to-all-start = ((bf16[16,32,256]{2,1,0:T(8,128)(2,1)}), bf16[16,32,256]{2,1,0:T(8,128)(2,1)S(1)}, u32[]{:S(2)}, u32[]{:S(2)}) async-start(bf16[16,32,256]{2,1,0:T(8,128)(2,1)} %broadcast_in_dim.2), calls=%async_computation | async-start | bytes 524288 | tf_op jit(solution)/shard_map/all_to_all | solution.py:247
  17.3 8.1 %collective-permute-start.3 = (bf16[512,256]{1,0:T(8,128)(2,1)}, bf16[512,256]{1,0:T(8,128)(2,1)S(1)}, u32[]{:S(2)}, u32[]{:S(2)}) collective-permute-start(bf16[512,256]{1,0:T(8,128)(2,1)} %param.12), channel_id=1, source_target_pairs={{0,1},{1,0},{2,3},{3,2},{4,5},{5,4},{6,7},{7,6},{8,9},{9,8},{10,11... | collective-permute-start | bytes 786440 | tf_op jit(solution)/shard_map/ppermute | solution.py:254
  25.5 56.1 %copy-start = (bf16[512,256]{1,0:T(8,128)(2,1)S(1)}, bf16[512,256]{1,0:T(8,128)(2,1)}, u32[]{:S(2)}) copy-start(bf16[512,256]{1,0:T(8,128)(2,1)} %saved_ref.2) | copy-start | bytes 786436
  25.5 56.1 %copy-start.9 = (s32[2,512]{1,0:T(2,128)S(1)}, s32[2,512]{1,0:T(2,128)}, u32[]{:S(2)}) copy-start(s32[2,512]{1,0:T(2,128)} %ids_ref.3) | copy-start | bytes 12292
  36.4 85.5 %all-to-all-start.1 = ((bf16[64,32,384]{2,1,0:T(8,128)(2,1)}), bf16[64,32,384]{2,1,0:T(8,128)(2,1)S(1)}, u32[]{:S(2)}, u32[]{:S(2)}) async-start(bf16[64,32,384]{2,1,0:T(8,128)(2,1)} %pack_rows.1), calls=%async_computation.1 | async-start | bytes 3145728 | tf_op jit(solution)/shard_map/all_to_all | solution.py:288
  45.8 26.7 %collective-permute-start.6 = (bf16[2,512,256]{2,1,0:T(8,128)(2,1)S(1)}, bf16[2,512,256]{2,1,0:T(8,128)(2,1)S(1)}, u32[]{:S(2)}, u32[]{:S(2)}) collective-permute-start(bf16[2,512,256]{2,1,0:T(8,128)(2,1)S(1)} %pad_maximum_fusion.refs_4_.refs_0_), channel_id=1, source_target_pairs={{0,6},{2,0},{4,2},{6,4},{1,7},{3,1},{5,3},{7,5},{8,14},{10,8},{12,... | collective-permute-start | bytes 1572872 | tf_op jit(solution)/shard_map/ppermute | solution.py:254
  50.7 24.3 %collective-permute-start.5 = (bf16[2,512,256]{2,1,0:T(8,128)(2,1)S(1)}, bf16[2,512,256]{2,1,0:T(8,128)(2,1)S(1)}, u32[]{:S(2)}, u32[]{:S(2)}) collective-permute-start(bf16[2,512,256]{2,1,0:T(8,128)(2,1)S(1)} %pad_maximum_fusion.refs_4_.refs_0_), channel_id=1, source_target_pairs={{0,4},{2,6},{4,0},{6,2},{1,5},{3,7},{5,1},{7,3},{8,12},{10,14},{12... | collective-permute-start | bytes 1572872 | tf_op jit(solution)/shard_map/ppermute | solution.py:254
  53.3 25.0 %collective-permute-start.4 = (bf16[2,512,256]{2,1,0:T(8,128)(2,1)S(1)}, bf16[2,512,256]{2,1,0:T(8,128)(2,1)}, u32[]{:S(2)}, u32[]{:S(2)}) collective-permute-start(bf16[2,512,256]{2,1,0:T(8,128)(2,1)S(1)} %pad_maximum_fusion.refs_4_.refs_0_), channel_id=1, source_target_pairs={{0,2},{2,4},{4,6},{6,0},{1,3},{3,5},{5,7},{7,1},{8,10},{10,12},{12... | collective-permute-start | bytes 1572872 | tf_op jit(solution)/shard_map/ppermute | solution.py:254
  56.2 22.1 %collective-permute-start.2 = (bf16[512,256]{1,0:T(8,128)(2,1)}, bf16[512,256]{1,0:T(8,128)(2,1)}, u32[]{:S(2)}, u32[]{:S(2)}) collective-permute-start(bf16[512,256]{1,0:T(8,128)(2,1)} %bitcast.40), channel_id=1, source_target_pairs={{0,384},{128,0},{256,128},{384,256},{1,385},{129,1},{257,129},{385... | collective-permute-start | bytes 786440 | tf_op jit(solution)/shard_map/ppermute | solution.py:254
  58.8 19.4 %collective-permute-start.1 = (bf16[512,256]{1,0:T(8,128)(2,1)}, bf16[512,256]{1,0:T(8,128)(2,1)}, u32[]{:S(2)}, u32[]{:S(2)}) collective-permute-start(bf16[512,256]{1,0:T(8,128)(2,1)} %bitcast.41), channel_id=1, source_target_pairs={{0,256},{128,384},{256,0},{384,128},{1,257},{129,385},{257,1},{385... | collective-permute-start | bytes 786440 | tf_op jit(solution)/shard_map/ppermute | solution.py:254
  72.5 9.1 %collective-permute-start = (bf16[512,256]{1,0:T(8,128)(2,1)}, bf16[512,256]{1,0:T(8,128)(2,1)}, u32[]{:S(2)}, u32[]{:S(2)}) collective-permute-start(bf16[512,256]{1,0:T(8,128)(2,1)} %bitcast.42), channel_id=1, source_target_pairs={{0,128},{128,256},{256,384},{384,0},{1,129},{129,257},{257,385},{3... | collective-permute-start | bytes 786440 | tf_op jit(solution)/shard_map/ppermute | solution.py:254
  91.2 12.0 %collective-permute-start.7 = (bf16[4,4,32,256]{3,2,1,0:T(8,128)(2,1)S(1)}, bf16[4,4,32,256]{3,2,1,0:T(8,128)(2,1)S(1)}, u32[]{:S(2)}, u32[]{:S(2)}) collective-permute-start(bf16[4,4,32,256]{3,2,1,0:T(8,128)(2,1)S(1)} %get-tuple-element.40), channel_id=1, source_target_pairs={{0,128},{128,256},{256,384},{384,0},{1,129},{129,257},{257,385},{3... | collective-permute-start | bytes 786440 | tf_op jit(solution)/shard_map/ppermute | solution.py:254
  94.9 17.1 %collective-permute-start.9 = (bf16[4,4,32,256]{3,2,1,0:T(8,128)(2,1)S(1)}, bf16[4,4,32,256]{3,2,1,0:T(8,128)(2,1)S(1)}, u32[]{:S(2)}, u32[]{:S(2)}) collective-permute-start(bf16[4,4,32,256]{3,2,1,0:T(8,128)(2,1)S(1)} %get-tuple-element.41), channel_id=1, source_target_pairs={{0,384},{128,0},{256,128},{384,256},{1,385},{129,1},{257,129},{385... | collective-permute-start | bytes 786440 | tf_op jit(solution)/shard_map/ppermute | solution.py:254
  97.1 14.9 %collective-permute-start.8 = (bf16[4,4,32,256]{3,2,1,0:T(8,128)(2,1)S(1)}, bf16[4,4,32,256]{3,2,1,0:T(8,128)(2,1)S(1)}, u32[]{:S(2)}, u32[]{:S(2)}) collective-permute-start(bf16[4,4,32,256]{3,2,1,0:T(8,128)(2,1)S(1)} %get-tuple-element.42), channel_id=1, source_target_pairs={{0,256},{128,384},{256,0},{384,128},{1,257},{129,385},{257,1},{385... | collective-permute-start | bytes 786440 | tf_op jit(solution)/shard_map/ppermute | solution.py:254
  121.9 40.9 %all-to-all-start.2 = ((bf16[1088,2,128]{2,1,0:T(2,128)(2,1)}), bf16[1088,2,128]{2,1,0:T(2,128)(2,1)S(1)}, u32[]{:S(2)}, u32[]{:S(2)}) async-start(bf16[1088,2,128]{2,1,0:T(2,128)(2,1)} %bitcast.19), calls=%async_computation.2 | async-start | bytes 1114112 | tf_op jit(solution)/shard_map/all_to_all | solution.py:314
  128.9 48.0 %collective-permute-start.12 = (bf16[4,32,256]{2,1,0:T(8,128)(2,1)S(1)}, bf16[4,32,256]{2,1,0:T(8,128)(2,1)S(1)}, u32[]{:S(2)}, u32[]{:S(2)}) collective-permute-start(bf16[4,32,256]{2,1,0:T(8,128)(2,1)S(1)} %get-tuple-element.43), channel_id=1, source_target_pairs={{0,24},{8,0},{16,8},{24,16},{1,25},{9,1},{17,9},{25,17},{2,26},{10... | collective-permute-start | bytes 196616 | tf_op jit(solution)/shard_map/ppermute | solution.py:254
  134.1 42.8 %collective-permute-start.11 = (bf16[4,32,256]{2,1,0:T(8,128)(2,1)S(1)}, bf16[4,32,256]{2,1,0:T(8,128)(2,1)S(1)}, u32[]{:S(2)}, u32[]{:S(2)}) collective-permute-start(bf16[4,32,256]{2,1,0:T(8,128)(2,1)S(1)} %get-tuple-element.44), channel_id=1, source_target_pairs={{0,16},{8,24},{16,0},{24,8},{1,17},{9,25},{17,1},{25,9},{2,18},{10... | collective-permute-start | bytes 196616 | tf_op jit(solution)/shard_map/ppermute | solution.py:254
  136.0 40.9 %collective-permute-start.10 = (bf16[4,32,256]{2,1,0:T(8,128)(2,1)S(1)}, bf16[4,32,256]{2,1,0:T(8,128)(2,1)S(1)}, u32[]{:S(2)}, u32[]{:S(2)}) collective-permute-start(bf16[4,32,256]{2,1,0:T(8,128)(2,1)S(1)} %get-tuple-element.45), channel_id=1, source_target_pairs={{0,8},{8,16},{16,24},{24,0},{1,9},{9,17},{17,25},{25,1},{2,10},{10... | collective-permute-start | bytes 196616 | tf_op jit(solution)/shard_map/ppermute | solution.py:254
  168.1 80.5 %all-to-all-start.3 = ((bf16[64,32,384]{2,1,0:T(8,128)(2,1)}), bf16[64,32,384]{2,1,0:T(8,128)(2,1)S(1)}, u32[]{:S(2)}, u32[]{:S(2)}) async-start(bf16[64,32,384]{2,1,0:T(8,128)(2,1)} %attend_cluster.1), calls=%async_computation.3 | async-start | bytes 3145728 | tf_op jit(solution)/shard_map/all_to_all | solution.py:333
  176.8 71.8 %copy-start.7 = (s32[512,8]{1,0:T(8,128)S(1)}, s32[512,8]{1,0:T(8,128)}, u32[]{:S(2)}) copy-start(s32[512,8]{1,0:T(8,128)} %copy-done.6) | copy-start | bytes 49156
  176.9 73.9 %collective-permute-start.15 = (bf16[32,256]{1,0:T(8,128)(2,1)S(1)}, bf16[32,256]{1,0:T(8,128)(2,1)S(1)}, u32[]{:S(2)}, u32[]{:S(2)}) collective-permute-start(bf16[32,256]{1,0:T(8,128)(2,1)S(1)} %get-tuple-element.46), channel_id=1, source_target_pairs={{0,96},{32,0},{64,32},{96,64},{1,97},{33,1},{65,33},{97,65},{2,98}... | collective-permute-start | bytes 49160 | tf_op jit(solution)/shard_map/ppermute | solution.py:254
  184.3 68.2 %collective-permute-start.14 = (bf16[32,256]{1,0:T(8,128)(2,1)S(1)}, bf16[32,256]{1,0:T(8,128)(2,1)S(1)}, u32[]{:S(2)}, u32[]{:S(2)}) collective-permute-start(bf16[32,256]{1,0:T(8,128)(2,1)S(1)} %get-tuple-element.47), channel_id=1, source_target_pairs={{0,64},{32,96},{64,0},{96,32},{1,65},{33,97},{65,1},{97,33},{2,66}... | collective-permute-start | bytes 49160 | tf_op jit(solution)/shard_map/ppermute | solution.py:254
  191.5 61.0 %collective-permute-start.13 = (bf16[32,256]{1,0:T(8,128)(2,1)S(1)}, bf16[32,256]{1,0:T(8,128)(2,1)S(1)}, u32[]{:S(2)}, u32[]{:S(2)}) collective-permute-start(bf16[32,256]{1,0:T(8,128)(2,1)S(1)} %get-tuple-element.48), channel_id=1, source_target_pairs={{0,32},{32,64},{64,96},{96,0},{1,33},{33,65},{65,97},{97,1},{2,34}... | collective-permute-start | bytes 49160 | tf_op jit(solution)/shard_map/ppermute | solution.py:254
  (7 other events, 5.9 us)
